TPU v7x, 32 devices: a whole 2x2x4 slice. The times are simulated.
32 devices in a mesh: seq: 4 (over z), head: 4 (over y, x), rep: 2 (over core).
Axes of the slice: x: 2, y: 2, z: 4, core: 2. Of those that a mesh axis runs over, the one named last changes fastest.
Arguments:
- queries: bfloat16 [64, 64, 128], P(('seq', 'head', 'rep'))
- prefix_keys: bfloat16 [16384, 4, 128], P(('seq', 'rep'), 'head')
- prefix_values: bfloat16 [16384, 4, 128], P(('seq', 'rep'), 'head'), may hold values from -6 to 6
- suffix_keys: bfloat16 [64, 2048, 4, 128], P(('seq', 'head', 'rep')), may hold values from -8.375 to 8.375
- suffix_values: bfloat16 [64, 2048, 4, 128], P(('seq', 'head', 'rep')), may hold values from -6 to 6
- suffix_lengths: int32 [64], P(('seq', 'head', 'rep')), may hold values from 256 to 2048, as said below
- slot_map: int32 [64], P(('seq', 'head', 'rep')), may hold values from 0 to 63, as said below
Outputs:
- attention: float32 [64, 64, 128], P(('seq', 'head', 'rep'))
- log_total: float32 [64, 64], P(('seq', 'head', 'rep'))
Inputs may be any that keep to these rules, and one draw needn't show every extreme that they name: `suffix_lengths`: every request has at least 256 live suffix positions, and some request has exactly 2048. slot_map is a permutation of the slots that keeps each aligned block of 2 requests in the block of 2 slots with the same indices.
All inputs are finite; a program needn't handle non-finite values.
Results may differ from a plain program's by a relative error of at most 0.00099.
Values may be sent and summed in bfloat16 or wider, within the bound.
No kernel may reach another device: no remote copies, remote signals or barrier semaphores. Data moves between devices by JAX's collectives and lax.ppermute only.
A program may use at most 64 MiB of HBM per device.

v0:
```python
import functools
import math

import jax
import jax.numpy as jnp
from jax import lax
from jax.experimental import pallas as pl
from jax.experimental.pallas import tpu as pltpu
from jax.sharding import PartitionSpec as P

ROW_TILE = 128
STEP_ROWS = 512
SUF_COPIES = 4
IN_FLIGHT = 4
LANES = 128
LOG_ROWS = 8
VALUE_BITS = 15
LOG_BITS = 30
LEAST = 1e-25
PEAK_LEAST = 1e-33
NT = (((1,), (1,)), ((), ()))
PREFIX_VMEM = 14 * 1024 * 1024
SUFFIX_VMEM = 20 * 1024 * 1024
SMALL_VMEM = 8 * 1024 * 1024
IN_VMEM = pl.BlockSpec(memory_space=pltpu.VMEM)
IN_HBM = pl.BlockSpec(memory_space=pltpu.HBM)


def in_hbm(array):
    return pltpu.with_memory_space_constraint(array, pltpu.HBM)


def layout_kernel(q_hbm, sent_hbm, buf, in_sems, out_sems):
    groups, rows, width = buf.shape
    count = q_hbm.shape[0]
    group = rows // count
    repeats = sent_hbm.shape[0] // groups
    reads = [
        pltpu.make_async_copy(
            q_hbm.at[r, pl.ds(g * group, group)], buf.at[g, pl.ds(r * group, group)], in_sems.at[g, r]
        )
        for g in range(groups)
        for r in range(count)
    ]
    for read in reads:
        read.start()
    for read in reads:
        read.wait()
    writes = [
        pltpu.make_async_copy(buf, sent_hbm.at[pl.ds(s * groups, groups)], out_sems.at[s])
        for s in range(repeats)
    ]
    for write in writes:
        write.start()
    for write in writes:
        write.wait()


def layout_queries(queries, groups, repeats):
    count, heads, width = queries.shape
    rows = count * heads // groups
    return pl.pallas_call(
        layout_kernel,
        in_specs=[IN_HBM],
        out_specs=IN_HBM,
        out_shape=pltpu.HBM((repeats * groups, rows, width), queries.dtype),
        scratch_shapes=[
            pltpu.VMEM((groups, rows, width), queries.dtype),
            pltpu.SemaphoreType.DMA((groups, count)),
            pltpu.SemaphoreType.DMA((repeats,)),
        ],
        compiler_params=pltpu.CompilerParams(vmem_limit_bytes=SMALL_VMEM),
        name="layout_queries",
    )(in_hbm(queries))


def suffix_kernel(*refs, place, carried, kv_count, score_scale):
    slot_hbm, length_hbm, q_hbm, k_hbm, v_hbm = refs[:5]
    refs = refs[5:]
    count, heads, width = q_hbm.shape
    carried_refs, refs = refs[:carried], refs[carried:]
    last = place == count - 1
    earlier, refs = (refs[: 2 * place], refs[2 * place :]) if last else ((), refs)
    mixed_ref, log_ref = refs[:2]
    brought_refs, refs = refs[2 : 2 + carried], refs[2 + carried :]
    slot_ref, length_ref, q_ref, k_buf, v_buf, score_ref, sems, small_sems = refs
    rows = k_hbm.shape[1]
    copy_rows = rows // SUF_COPIES
    copies = []
    for which, (source, target) in enumerate(((k_hbm, k_buf), (v_hbm, v_buf))):
        for c in range(SUF_COPIES):
            part = pl.ds(c * copy_rows, copy_rows)
            copies.append(
                pltpu.make_async_copy(source.at[place, part], target.at[part], sems.at[which, c])
            )
    small = [
        pltpu.make_async_copy(source, target, small_sems.at[i])
        for i, (source, target) in enumerate(
            [(slot_hbm, slot_ref), (length_hbm, length_ref), (q_hbm, q_ref)]
            + list(zip(carried_refs, brought_refs))
        )
    ]
    carries = small[3:]
    for copy in small[:3] + copies[:IN_FLIGHT]:
        copy.start()

    def arrive(i):
        copies[i].wait()
        if i + IN_FLIGHT < len(copies):
            copies[i + IN_FLIGHT].start()
        elif i + IN_FLIGHT - len(copies) < carried:
            carries[i + IN_FLIGHT - len(copies)].start()

    for copy in small[:3]:
        copy.wait()

    def request_of(slot):
        found = jnp.int32(0)
        for r in range(1, count):
            found = jnp.where(lax.rem(slot_ref[r], count) == slot, r, found)
        return found

    request = request_of(place)
    limit = length_ref[request] * kv_count
    query = q_ref[request]
    lane = lax.broadcasted_iota(jnp.int32, (heads, LANES), 1)
    group = lax.broadcasted_iota(jnp.int32, (heads, LANES), 0) // (heads // kv_count)
    lane = jnp.where((lane % kv_count) == group, lane, rows)
    peak = jnp.full((heads, LANES), -1e30, jnp.float32)
    for c in range(SUF_COPIES):
        arrive(c)
        part = lax.dot_general(
            query, k_buf[c * copy_rows : (c + 1) * copy_rows], NT, preferred_element_type=jnp.float32
        )
        for begin in range(0, copy_rows, LANES):
            at = c * copy_rows + begin
            tile = jnp.where(lane < limit - at, part[:, begin : begin + LANES], -1e30)
            score_ref[:, at : at + LANES] = tile
            peak = jnp.maximum(peak, tile)
    row_max = jnp.max(peak, axis=1, keepdims=True)
    sums = jnp.zeros((heads, LANES), jnp.float32)
    acc = jnp.zeros((heads, width), jnp.float32)
    for c in range(SUF_COPIES):
        arrive(SUF_COPIES + c)
        part = slice(c * copy_rows, (c + 1) * copy_rows)
        terms = jnp.exp((score_ref[:, part] - row_max) * score_scale)
        for begin in range(0, copy_rows, LANES):
            sums = sums + terms[:, begin : begin + LANES]
        acc = acc + jnp.dot(
            terms.astype(jnp.bfloat16), v_buf[part], preferred_element_type=jnp.float32
        )
    total = jnp.sum(sums, axis=1, keepdims=True)
    mixed = acc / total
    log = jnp.broadcast_to(row_max * score_scale + jnp.log(total), (heads, width))
    for carry in carries:
        carry.wait()
    if not last:
        mixed_ref[...] = mixed
        log_ref[...] = log
        return
    mixed_ref[request] = mixed
    log_ref[request] = log
    for slot in range(place):
        mixed_ref[request_of(slot)] = earlier[2 * slot][...]
        log_ref[request_of(slot)] = earlier[2 * slot + 1][...]


def suffix_partials(place, queries, keys, values, lengths, slots, carried, earlier, score_scale):
    count, heads, width = queries.shape
    kv_count = keys.shape[2]
    rows = keys.shape[1] * kv_count
    result = (count, heads, width) if place == count - 1 else (heads, width)
    operands = (
        slots,
        lengths,
        queries,
        keys.reshape(count, rows, width),
        values.reshape(count, rows, width),
        *carried,
    )
    return pl.pallas_call(
        functools.partial(
            suffix_kernel,
            place=place,
            carried=len(carried),
            kv_count=kv_count,
            score_scale=score_scale,
        ),
        in_specs=[IN_HBM] * len(operands) + [IN_VMEM] * len(earlier),
        out_specs=[IN_VMEM] * (2 + len(carried)),
        out_shape=[pltpu.VMEM(result, jnp.float32)] * 2
        + [pltpu.VMEM(array.shape, array.dtype) for array in carried],
        scratch_shapes=[
            pltpu.SMEM((count,), jnp.int32),
            pltpu.SMEM((count,), jnp.int32),
            pltpu.VMEM((count, heads, width), queries.dtype),
            pltpu.VMEM((rows, width), keys.dtype),
            pltpu.VMEM((rows, width), values.dtype),
            pltpu.VMEM((heads, rows), jnp.float32),
            pltpu.SemaphoreType.DMA((2, SUF_COPIES)),
            pltpu.SemaphoreType.DMA((3 + len(carried),)),
        ],
        compiler_params=pltpu.CompilerParams(vmem_limit_bytes=SUFFIX_VMEM),
        cost_estimate=pl.CostEstimate(
            flops=4 * heads * rows * width,
            bytes_accessed=4 * rows * width,
            transcendentals=heads * rows,
        ),
        name=f"suffix_attention_{place}",
    )(*map(in_hbm, operands), *earlier)


def exponent(size, least):
    return jnp.floor(jnp.log2(jnp.maximum(size, least))) + 1.0


def prefix_kernel(
    q_ref, k0_ref, v0_ref, k1_ref, v1_ref, out_ref, score_ref, *, per_dest, score_scale
):
    width = q_ref.shape[1]
    tiles = q_ref.shape[0] // ROW_TILE
    dests = ROW_TILE // per_dest
    keys, values = (k0_ref, k1_ref), (v0_ref, v1_ref)
    units = [(tile, block) for tile in range(tiles) for block in range(2)]
    lane = lax.broadcasted_iota(jnp.int32, (per_dest, width), 1)
    row = lax.broadcasted_iota(jnp.int32, (per_dest, width), 0)
    diagonal = lane == row

    def score(unit, slot):
        tile, block = unit
        score_ref[slot] = lax.dot_general(
            q_ref[tile * ROW_TILE : (tile + 1) * ROW_TILE],
            keys[block][...],
            NT,
            preferred_element_type=jnp.float32,
        )

    score(units[0], 0)
    held = None
    for step, (tile, block) in enumerate(units):
        if step + 1 < len(units):
            score(units[step + 1], (step + 1) % 2)
        scores = score_ref[step % 2]
        row_max = jnp.max(scores, axis=1, keepdims=True)
        terms = jnp.exp((scores - row_max) * score_scale)
        total = jnp.sum(terms, axis=1, keepdims=True)
        acc = jnp.dot(
            terms.astype(jnp.bfloat16), values[block][...], preferred_element_type=jnp.float32
        )
        if block == 0:
            held = (row_max, total, acc)
            continue
        max0, total0, acc0 = held
        top = jnp.maximum(max0, row_max)
        weight0 = jnp.exp((max0 - top) * score_scale)
        weight1 = jnp.exp((row_max - top) * score_scale)
        joined = weight0 * total0 + weight1 * total
        mixed = (weight0 * acc0 + weight1 * acc) / joined
        logs = jnp.broadcast_to(top * score_scale + jnp.log(joined), (ROW_TILE, width))
        peak = jnp.max(jnp.abs(mixed), axis=1, keepdims=True)
        coded = jnp.round(mixed * jnp.exp2(VALUE_BITS - exponent(peak, PEAK_LEAST)))
        most = 2.0**VALUE_BITS - 1
        coded = jnp.clip(coded, -most, most).astype(jnp.int32)
        peaks = jnp.broadcast_to(peak, (ROW_TILE, width))
        half = per_dest // 2
        for k in range(dests):
            rows = slice(k * per_dest, (k + 1) * per_dest)
            dest = tile * dests + k
            high, low = coded[k * per_dest : k * per_dest + half], coded[k * per_dest + half : rows.stop]
            out_ref[dest, :half] = (high << 16) | (low & 0xFFFF)
            log_line = jnp.sum(jnp.where(diagonal, logs[rows], 0.0), axis=0, keepdims=True)
            peak_line = jnp.sum(jnp.where(diagonal, peaks[rows], 0.0), axis=0, keepdims=True)
            log_power = exponent(jnp.abs(log_line), LEAST)
            lines = jnp.concatenate(
                [
                    jnp.round(log_line * jnp.exp2(LOG_BITS - log_power)),
                    log_power,
                    exponent(peak_line, PEAK_LEAST),
                    jnp.zeros((LOG_ROWS - 3, width), jnp.float32),
                ],
                axis=0,
            )
            out_ref[dest, half:] = lines.astype(jnp.int32)


def prefix_partials(rows_q, keys, values, far_keys, far_values, per_dest, score_scale):
    rows, width = rows_q.shape
    length = keys.shape[0]
    step_rows = min(STEP_ROWS, rows)
    blocked = {}
    if step_rows == rows:
        blocked["in_specs"] = [IN_VMEM] * 5
        blocked["out_specs"] = IN_VMEM
    else:
        blocked["grid"] = (rows // step_rows,)
        blocked["in_specs"] = [pl.BlockSpec((step_rows, width), lambda i: (i, 0))]
        blocked["in_specs"] += [pl.BlockSpec((length, width), lambda i: (0, 0))] * 4
        blocked["out_specs"] = pl.BlockSpec(
            (step_rows // per_dest, per_dest // 2 + LOG_ROWS, width), lambda i: (i, 0, 0)
        )
    return pl.pallas_call(
        functools.partial(prefix_kernel, per_dest=per_dest, score_scale=score_scale),
        **blocked,
        out_shape=jax.ShapeDtypeStruct(
            (rows // per_dest, per_dest // 2 + LOG_ROWS, width), jnp.int32
        ),
        scratch_shapes=[pltpu.VMEM((2, ROW_TILE, length), jnp.float32)],
        compiler_params=pltpu.CompilerParams(vmem_limit_bytes=PREFIX_VMEM),
        cost_estimate=pl.CostEstimate(
            flops=8 * rows * length * width,
            bytes_accessed=8 * length * width + 6 * rows * width,
            transcendentals=2 * rows * length,
        ),
        name="prefix_attention",
    )(rows_q, keys, values, far_keys, far_values)


def join_kernel(got_ref, suf_ref, suf_log_ref, out_ref, log_ref, *, kv_count):
    count, heads, width = out_ref.shape
    group = heads // kv_count
    per_dest = count * group
    half = per_dest // 2
    parts = got_ref.shape[0] // kv_count
    lane = lax.broadcasted_iota(jnp.int32, (per_dest, width), 1)
    row = lax.broadcasted_iota(jnp.int32, (per_dest, width), 0)
    diagonal = lane == row

    def column(line):
        return jnp.sum(jnp.where(diagonal, line, 0.0), axis=1, keepdims=True)

    lines = [jnp.zeros((1, width), jnp.float32) for _ in range(count)]
    for g in range(kv_count):
        heads_of = slice(g * group, (g + 1) * group)
        suf_mixed = jnp.concatenate([suf_ref[r, heads_of] for r in range(count)], axis=0)
        suf_log = jnp.concatenate([suf_log_ref[r, heads_of] for r in range(count)], axis=0)
        logs, scales = [], []
        top = suf_log
        for s in range(parts):
            tail = got_ref[s * kv_count + g, half:].astype(jnp.float32)
            log_line = tail[0:1] * jnp.exp2(tail[1:2] - LOG_BITS)
            logs.append(jnp.broadcast_to(column(log_line), (per_dest, width)))
            scales.append(column(jnp.exp2(tail[2:3] - VALUE_BITS)))
            top = jnp.maximum(top, logs[-1])
        weight = jnp.exp(suf_log - top)
        acc = weight * suf_mixed
        total = weight
        for s in range(parts):
            words = got_ref[s * kv_count + g, :half]
            coded = jnp.concatenate([words >> 16, (words << 16) >> 16], axis=0)
            weight = jnp.exp(logs[s] - top)
            acc = acc + (weight * scales[s]) * coded.astype(jnp.float32)
            total = total + weight
        acc = acc / total
        logged = top + jnp.log(total)
        for r in range(count):
            rows = slice(r * group, (r + 1) * group)
            out_ref[r, heads_of] = acc[rows]
            place = lane[:group] == row[:group] + g * group
            lines[r] = lines[r] + jnp.sum(jnp.where(place, logged[rows], 0.0), axis=0, keepdims=True)
    for r in range(count):
        log_ref[r : r + 1] = lines[r][:, :heads]


def join_partials(got, suf_mixed, suf_log, kv_count):
    count, heads, width = suf_mixed.shape
    return pl.pallas_call(
        functools.partial(join_kernel, kv_count=kv_count),
        in_specs=[IN_VMEM] * 3,
        out_specs=[IN_VMEM] * 2,
        out_shape=[
            jax.ShapeDtypeStruct((count, heads, width), jnp.float32),
            jax.ShapeDtypeStruct((count, heads), jnp.float32),
        ],
        compiler_params=pltpu.CompilerParams(vmem_limit_bytes=SMALL_VMEM),
        name="join_partials",
    )(got, suf_mixed, suf_log)


def per_device(
    queries, prefix_keys, prefix_values, suffix_keys, suffix_values, suffix_lengths, slot_map
):
    count, heads, width = queries.shape
    kv_count = suffix_keys.shape[2]
    per_dest = count * heads // kv_count
    score_scale = 1.0 / math.sqrt(width)
    sent = layout_queries(queries, kv_count, lax.axis_size("seq"))
    got_q = lax.all_to_all(sent, ("seq", "head"), split_axis=0, concat_axis=0, tiled=True)
    keys = prefix_keys[:, 0, :]
    values = prefix_values[:, 0, :]
    far_keys = lax.ppermute(keys, "rep", [(0, 1), (1, 0)])
    far_values = lax.ppermute(values, "rep", [(0, 1), (1, 0)])
    earlier = []
    for place in range(count):
        first, last = place == 0, place == count - 1
        mixed, log, *brought = suffix_partials(
            place,
            queries,
            suffix_keys,
            suffix_values,
            suffix_lengths,
            slot_map,
            (keys, values) if first else (),
            earlier if last else (),
            score_scale,
        )
        earlier += [mixed, log]
        if first:
            near_keys, near_values = brought
    partials = prefix_partials(
        got_q.reshape(-1, width), near_keys, near_values, far_keys, far_values, per_dest, score_scale
    )
    got = lax.all_to_all(partials, ("seq", "head"), split_axis=0, concat_axis=0, tiled=True)
    return join_partials(got, mixed, log, kv_count)


def solution(mesh):
    by_request = P(("seq", "head", "rep"))
    by_block = P(("seq", "rep"), "head", None)
    placed = (by_request, by_block, by_block, by_request, by_request, by_request, by_request)
    return jax.shard_map(
        per_device,
        mesh=mesh,
        in_specs=placed,
        out_specs=(by_request, by_request),
        check_vma=False,
    )
```

profile of v0, /device:TPU:0, one launch (start us, length us, event | category | flops | bytes accessed | tf_op | source)
XLA Modules:
  0.0 35.2 jit_solution(2360301756978720367)
XLA Ops:
  0.6 0.5 %collective-permute-start = (bf16[2048,128]{1,0:T(8,128)(2,1)}, bf16[2048,128]{1,0:T(8,128)(2,1)S(1)}, u32[]{:S(2)}, u32[]{:S(2)}) collective-permute-start(bf16[2048,128]{1,0:T(8,128)(2,1)} %bitcast.10), channel_id=1, source_target_pairs={{0,1},{1,0},{2,3},{3,2},{4,5},{5,4},{6,7},{7,6},{8,9},{9,8},{10,11... | collective-permute-start | bytes 1572872 | tf_op jit(solution)/shard_map/ppermute | solution.py:390
  1.1 0.1 collective-permute-start.1
  1.2 1.6 %layout_queries.1 = bf16[16,32,128]{2,1,0:T(8,128)(2,1)} custom-call(bf16[2,64,128]{2,1,0:T(8,128)(2,1)} %refs_2_.3), custom_call_target="tpu_custom_call" | custom-call | tf_op jit(solution)/shard_map/layout_queries/pallas_call | solution.py:62
  2.8 8.3 %all-to-all-start = ((bf16[16,32,128]{2,1,0:T(8,128)(2,1)}), bf16[16,32,128]{2,1,0:T(8,128)(2,1)S(1)}, u32[]{:S(2)}, u32[]{:S(2)}) async-start(bf16[16,32,128]{2,1,0:T(8,128)(2,1)} %layout_queries.1), calls=%async_computation | async-start | bytes 262144 | tf_op jit(solution)/shard_map/all_to_all | solution.py:387
  11.1 4.0 %suffix_attention_0.1 = (f32[64,128]{1,0:T(8,128)S(1)}, f32[64,128]{1,0:T(8,128)S(1)}, bf16[2048,128]{1,0:T(8,128)(2,1)S(1)}, bf16[2048,128]{1,0:T(8,128)(2,1)S(1)}) custom-call(s32[2]{0:T(128)} %refs_0_.3, s32[2]{0:T(128)} %refs_1_.3, bf16[2,64,128]{2,1,0:T(8,128)(2,1)} %refs_2_.3, bf16[2,8192,128]{2,1,0:T(8,128)(2,1)} %bitcast.6, ...), custom_call_target="tpu_custom_call" | custom-call | flops 268435456 | bytes 4194304 | tf_op jit(solution)/shard_map/suffix_attention_0/pallas_call | solution.py:181
  15.1 3.8 %all-to-all-done = bf16[16,32,128]{2,1,0:T(8,128)(2,1)S(1)} async-done(((bf16[16,32,128]{2,1,0:T(8,128)(2,1)}), bf16[16,32,128]{2,1,0:T(8,128)(2,1)S(1)}, u32[]{:S(2)}, u32[]{:S(2)}) %all-to-all-start) | async-done | bytes 131104 | tf_op jit(solution)/shard_map/all_to_all | solution.py:387
  18.9 0.0 collective-permute-done.k1_ref
  18.9 0.0 collective-permute-done.1.v1_ref
  18.9 3.9 %prefix_attention.1 = s32[16,24,128]{2,1,0:T(8,128)} custom-call(bf16[512,128]{1,0:T(8,128)(2,1)S(1)} %bitcast.5, bf16[2048,128]{1,0:T(8,128)(2,1)S(1)} %get-tuple-element.8.k0_ref, bf16[2048,128]{1,0:T(8,128)(2,1)S(1)} %get-tuple-element.9.v0_ref, bf16[2048,128]{1,0:T(8,128)(2,1)S(1)} %collective-permute-done.k1_ref, ...), custom_call_target="tpu_custom_call" | custom-call | flops 1073741824 | bytes 2490368 | tf_op jit(solution)/shard_map/prefix_attention/pallas_call | solution.py:301
  22.8 3.5 %all-to-all-start.1 = ((s32[16,24,128]{2,1,0:T(8,128)}), s32[16,24,128]{2,1,0:T(8,128)S(1)}, u32[]{:S(2)}, u32[]{:S(2)}) async-start(s32[16,24,128]{2,1,0:T(8,128)} %prefix_attention.1), calls=%async_computation.1 | async-start | bytes 393216 | tf_op jit(solution)/shard_map/all_to_all | solution.py:412
  26.3 3.7 %suffix_attention_1.1 = (f32[2,64,128]{2,1,0:T(8,128)S(1)}, f32[2,64,128]{2,1,0:T(8,128)S(1)}) custom-call(s32[2]{0:T(128)} %refs_0_.3, s32[2]{0:T(128)} %refs_1_.3, bf16[2,64,128]{2,1,0:T(8,128)(2,1)} %refs_2_.3, bf16[2,8192,128]{2,1,0:T(8,128)(2,1)} %bitcast.7, bf16[2,8192,128]{2,1,0:T(8,128)(2,1)} %bitcast.9, f32[64,128]{1,0:T(8,128)S(1)} %get-tuple-element.10.refs_5_, ...), custom_call_target="tpu_custom_call" | custom-call | flops 268435456 | bytes 4194304 | tf_op jit(solution)/shard_map/suffix_attention_1/pallas_call | solution.py:181
  30.0 4.4 %all-to-all-done.1.got_ref = s32[16,24,128]{2,1,0:T(8,128)S(1)} async-done(((s32[16,24,128]{2,1,0:T(8,128)}), s32[16,24,128]{2,1,0:T(8,128)S(1)}, u32[]{:S(2)}, u32[]{:S(2)}) %all-to-all-start.1) | async-done | bytes 196640 | tf_op jit(solution)/shard_map/all_to_all | solution.py:412
  34.4 0.9 %join_partials.1 = (f32[2,64,128]{2,1,0:T(8,128)}, f32[2,64]{1,0:T(2,128)}) custom-call(s32[16,24,128]{2,1,0:T(8,128)S(1)} %all-to-all-done.1.got_ref, f32[2,64,128]{2,1,0:T(8,128)S(1)} %get-tuple-element.12.suf_ref, f32[2,64,128]{2,1,0:T(8,128)S(1)} %get-tuple-element.13.suf_log_ref), custom_call_target="tpu_custom_call" | custom-call | tf_op jit(solution)/shard_map/join_partials/pallas_call | solution.py:366
Async XLA Ops:
  0.6 18.3 %collective-permute-start = (bf16[2048,128]{1,0:T(8,128)(2,1)}, bf16[2048,128]{1,0:T(8,128)(2,1)S(1)}, u32[]{:S(2)}, u32[]{:S(2)}) collective-permute-start(bf16[2048,128]{1,0:T(8,128)(2,1)} %bitcast.10), channel_id=1, source_target_pairs={{0,1},{1,0},{2,3},{3,2},{4,5},{5,4},{6,7},{7,6},{8,9},{9,8},{10,11... | collective-permute-start | bytes 1572872 | tf_op jit(solution)/shard_map/ppermute | solution.py:390
  1.1 17.8 %collective-permute-start.1 = (bf16[2048,128]{1,0:T(8,128)(2,1)}, bf16[2048,128]{1,0:T(8,128)(2,1)S(1)}, u32[]{:S(2)}, u32[]{:S(2)}) collective-permute-start(bf16[2048,128]{1,0:T(8,128)(2,1)} %bitcast.12), channel_id=1, source_target_pairs={{0,1},{1,0},{2,3},{3,2},{4,5},{5,4},{6,7},{7,6},{8,9},{9,8},{10,11... | collective-permute-start | bytes 1572872 | tf_op jit(solution)/shard_map/ppermute | solution.py:391
  2.8 16.1 %all-to-all-start = ((bf16[16,32,128]{2,1,0:T(8,128)(2,1)}), bf16[16,32,128]{2,1,0:T(8,128)(2,1)S(1)}, u32[]{:S(2)}, u32[]{:S(2)}) async-start(bf16[16,32,128]{2,1,0:T(8,128)(2,1)} %layout_queries.1), calls=%async_computation | async-start | bytes 262144 | tf_op jit(solution)/shard_map/all_to_all | solution.py:387
  22.8 11.6 %all-to-all-start.1 = ((s32[16,24,128]{2,1,0:T(8,128)}), s32[16,24,128]{2,1,0:T(8,128)S(1)}, u32[]{:S(2)}, u32[]{:S(2)}) async-start(s32[16,24,128]{2,1,0:T(8,128)} %prefix_attention.1), calls=%async_computation.1 | async-start | bytes 393216 | tf_op jit(solution)/shard_map/all_to_all | solution.py:412
where the time goes:
time: 35.7 us; the launch traced here: 35.2 us
  Pallas kernels  14 us (39%)
  starting transfers between devices  12.4 us (35%)
  waiting for transfers between devices  8.16 us (23%)
  between operations  0.67 us (2%)
    all_to_all x1, starting transfers between devices, per_device(): lax.all_to_all(sent, ('seq', 'head'), split_axis=0, concat_axis=0, tiled=...  8.3 us
    pallas_call x2, Pallas kernels, suffix_partials(): pl.pallas_call(functools.partial(suffix_kernel, place=place, carried=len(...  7.68 us
    all_to_all x1, waiting for transfers between devices, per_device(): lax.all_to_all(partials, ('seq', 'head'), split_axis=0, concat_axis=0, ti...  4.35 us
    pallas_call x1, Pallas kernels, prefix_partials(): pl.pallas_call(functools.partial(prefix_kernel, per_dest=per_dest, score_...  3.89 us
    all_to_all x1, waiting for transfers between devices, per_device(): lax.all_to_all(sent, ('seq', 'head'), split_axis=0, concat_axis=0, tiled=...  3.8 us
    all_to_all x1, starting transfers between devices, per_device(): lax.all_to_all(partials, ('seq', 'head'), split_axis=0, concat_axis=0, ti...  3.52 us
    pallas_call x1, Pallas kernels, layout_queries(): pl.pallas_call(layout_kernel, in_specs=[IN_HBM], out_specs=IN_HBM, out_sh...  1.56 us
    pallas_call x1, Pallas kernels, join_partials(): pl.pallas_call(functools.partial(join_kernel, kv_count=kv_count), in_spec...  0.86 us
  transfers between devices with their start and end apart: 4, of which 2 were waited for; matrix products, arithmetic and copies ran while one was open for 0% of the time, Pallas kernels for 26%

commit v1 on v0

--- a/solution.py
+++ b/solution.py
@@ -8,7 +8,7 @@
 from jax.experimental.pallas import tpu as pltpu
 from jax.sharding import PartitionSpec as P
 
-ROW_TILE = 128
+ROW_TILE = 256
 STEP_ROWS = 512
 SUF_COPIES = 4
 IN_FLIGHT = 4
@@ -16,10 +16,11 @@
 LOG_ROWS = 8
 VALUE_BITS = 15
 LOG_BITS = 30
+LOG2E = math.log2(math.e)
 LEAST = 1e-25
 PEAK_LEAST = 1e-33
 NT = (((1,), (1,)), ((), ()))
-PREFIX_VMEM = 14 * 1024 * 1024
+PREFIX_VMEM = 24 * 1024 * 1024
 SUFFIX_VMEM = 20 * 1024 * 1024
 SMALL_VMEM = 8 * 1024 * 1024
 IN_VMEM = pl.BlockSpec(memory_space=pltpu.VMEM)
@@ -30,48 +31,36 @@
     return pltpu.with_memory_space_constraint(array, pltpu.HBM)
 
 
-def layout_kernel(q_hbm, sent_hbm, buf, in_sems, out_sems):
-    groups, rows, width = buf.shape
-    count = q_hbm.shape[0]
-    group = rows // count
+def layout_kernel(q_hbm, sent_hbm, sems):
+    count, groups, group, _ = q_hbm.shape
     repeats = sent_hbm.shape[0] // groups
-    reads = [
+    copies = [
         pltpu.make_async_copy(
-            q_hbm.at[r, pl.ds(g * group, group)], buf.at[g, pl.ds(r * group, group)], in_sems.at[g, r]
-        )
-        for g in range(groups)
+            q_hbm.at[r],
+            sent_hbm.at[pl.ds(s * groups, groups), pl.ds(r * group, group)],
+            sems.at[s, r],
+        )
+        for s in range(repeats)
         for r in range(count)
     ]
-    for read in reads:
-        read.start()
-    for read in reads:
-        read.wait()
-    writes = [
-        pltpu.make_async_copy(buf, sent_hbm.at[pl.ds(s * groups, groups)], out_sems.at[s])
-        for s in range(repeats)
-    ]
-    for write in writes:
-        write.start()
-    for write in writes:
-        write.wait()
+    for copy in copies:
+        copy.start()
+    for copy in copies:
+        copy.wait()
 
 
 def layout_queries(queries, groups, repeats):
     count, heads, width = queries.shape
-    rows = count * heads // groups
+    group = heads // groups
     return pl.pallas_call(
         layout_kernel,
         in_specs=[IN_HBM],
         out_specs=IN_HBM,
-        out_shape=pltpu.HBM((repeats * groups, rows, width), queries.dtype),
-        scratch_shapes=[
-            pltpu.VMEM((groups, rows, width), queries.dtype),
-            pltpu.SemaphoreType.DMA((groups, count)),
-            pltpu.SemaphoreType.DMA((repeats,)),
-        ],
+        out_shape=pltpu.HBM((repeats * groups, count * group, width), queries.dtype),
+        scratch_shapes=[pltpu.SemaphoreType.DMA((repeats, count))],
         compiler_params=pltpu.CompilerParams(vmem_limit_bytes=SMALL_VMEM),
         name="layout_queries",
-    )(in_hbm(queries))
+    )(in_hbm(queries.reshape(count, groups, group, width)))
 
 
 def suffix_kernel(*refs, place, carried, kv_count, score_scale):
@@ -143,7 +132,7 @@
     for c in range(SUF_COPIES):
         arrive(SUF_COPIES + c)
         part = slice(c * copy_rows, (c + 1) * copy_rows)
-        terms = jnp.exp((score_ref[:, part] - row_max) * score_scale)
+        terms = jnp.exp2((score_ref[:, part] - row_max) * (score_scale * LOG2E))
         for begin in range(0, copy_rows, LANES):
             sums = sums + terms[:, begin : begin + LANES]
         acc = acc + jnp.dot(
@@ -215,13 +204,15 @@
 
 
 def prefix_kernel(
-    q_ref, k0_ref, v0_ref, k1_ref, v1_ref, out_ref, score_ref, *, per_dest, score_scale
+    q_ref, k0_ref, v0_ref, k1_ref, v1_ref, out_hbm, out_ref, score_ref, sems, *, per_dest, score_scale
 ):
     width = q_ref.shape[1]
     tiles = q_ref.shape[0] // ROW_TILE
     dests = ROW_TILE // per_dest
     keys, values = (k0_ref, k1_ref), (v0_ref, v1_ref)
     units = [(tile, block) for tile in range(tiles) for block in range(2)]
+    first_dest = 0 if out_hbm.shape == out_ref.shape else pl.program_id(0) * (tiles * dests)
+    copies = []
     lane = lax.broadcasted_iota(jnp.int32, (per_dest, width), 1)
     row = lax.broadcasted_iota(jnp.int32, (per_dest, width), 0)
     diagonal = lane == row
@@ -242,7 +233,7 @@
             score(units[step + 1], (step + 1) % 2)
         scores = score_ref[step % 2]
         row_max = jnp.max(scores, axis=1, keepdims=True)
-        terms = jnp.exp((scores - row_max) * score_scale)
+        terms = jnp.exp2((scores - row_max) * (score_scale * LOG2E))
         total = jnp.sum(terms, axis=1, keepdims=True)
         acc = jnp.dot(
             terms.astype(jnp.bfloat16), values[block][...], preferred_element_type=jnp.float32
@@ -281,30 +272,40 @@
                 axis=0,
             )
             out_ref[dest, half:] = lines.astype(jnp.int32)
+        ready = pl.ds(tile * dests, dests)
+        copies.append(
+            pltpu.make_async_copy(
+                out_ref.at[ready],
+                out_hbm.at[pl.ds(first_dest + tile * dests, dests)],
+                sems.at[tile],
+            )
+        )
+        copies[-1].start()
+    for copy in copies:
+        copy.wait()
 
 
 def prefix_partials(rows_q, keys, values, far_keys, far_values, per_dest, score_scale):
     rows, width = rows_q.shape
     length = keys.shape[0]
     step_rows = min(STEP_ROWS, rows)
-    blocked = {}
-    if step_rows == rows:
-        blocked["in_specs"] = [IN_VMEM] * 5
-        blocked["out_specs"] = IN_VMEM
-    else:
+    dests = step_rows // per_dest
+    out_rows = per_dest // 2 + LOG_ROWS
+    blocked = {"in_specs": [IN_VMEM] * 5}
+    if step_rows < rows:
         blocked["grid"] = (rows // step_rows,)
         blocked["in_specs"] = [pl.BlockSpec((step_rows, width), lambda i: (i, 0))]
         blocked["in_specs"] += [pl.BlockSpec((length, width), lambda i: (0, 0))] * 4
-        blocked["out_specs"] = pl.BlockSpec(
-            (step_rows // per_dest, per_dest // 2 + LOG_ROWS, width), lambda i: (i, 0, 0)
-        )
     return pl.pallas_call(
         functools.partial(prefix_kernel, per_dest=per_dest, score_scale=score_scale),
         **blocked,
-        out_shape=jax.ShapeDtypeStruct(
-            (rows // per_dest, per_dest // 2 + LOG_ROWS, width), jnp.int32
-        ),
-        scratch_shapes=[pltpu.VMEM((2, ROW_TILE, length), jnp.float32)],
+        out_specs=IN_HBM,
+        out_shape=pltpu.HBM((rows // per_dest, out_rows, width), jnp.int32),
+        scratch_shapes=[
+            pltpu.VMEM((dests, out_rows, width), jnp.int32),
+            pltpu.VMEM((2, ROW_TILE, length), jnp.float32),
+            pltpu.SemaphoreType.DMA((step_rows // ROW_TILE,)),
+        ],
         compiler_params=pltpu.CompilerParams(vmem_limit_bytes=PREFIX_VMEM),
         cost_estimate=pl.CostEstimate(
             flops=8 * rows * length * width,

time: 35.7 us -> 39.1 us (1.095)
  Pallas kernels: 14 us -> 17.4 us
    pallas_call x1, Pallas kernels: 1.56 us -> 5.14 us  [layout_queries(): pl.pallas_call(layout_kernel, in_specs=[IN_HBM], out_specs=IN_HBM, out_sh...]
  transfers between devices with their start and end apart: 4 -> 4, of which waited for: 2 -> 2; matrix products, arithmetic and copies ran while one was open for 0% -> 0% of each run, Pallas kernels for 26% -> 33%
where the time goes in v1:
time: 39.1 us; the launch traced here: 38.7 us
  Pallas kernels  17.4 us (45%)
  starting transfers between devices  12.4 us (32%)
  waiting for transfers between devices  8.19 us (21%)
  between operations  0.68 us (2%)
    all_to_all x1, starting transfers between devices, per_device(): lax.all_to_all(sent, ('seq', 'head'), split_axis=0, concat_axis=0, tiled=...  8.3 us
    pallas_call x2, Pallas kernels, suffix_partials(): pl.pallas_call(functools.partial(suffix_kernel, place=place, carried=len(...  7.65 us
    pallas_call x1, Pallas kernels, layout_queries(): pl.pallas_call(layout_kernel, in_specs=[IN_HBM], out_specs=IN_HBM, out_sh...  5.14 us
    all_to_all x1, waiting for transfers between devices, per_device(): lax.all_to_all(partials, ('seq', 'head'), split_axis=0, concat_axis=0, ti...  4.36 us
    all_to_all x1, waiting for transfers between devices, per_device(): lax.all_to_all(sent, ('seq', 'head'), split_axis=0, concat_axis=0, tiled=...  3.82 us
    pallas_call x1, Pallas kernels, prefix_partials(): pl.pallas_call(functools.partial(prefix_kernel, per_dest=per_dest, score_...  3.76 us
    all_to_all x1, starting transfers between devices, per_device(): lax.all_to_all(partials, ('seq', 'head'), split_axis=0, concat_axis=0, ti...  3.53 us
    pallas_call x1, Pallas kernels, join_partials(): pl.pallas_call(functools.partial(join_kernel, kv_count=kv_count), in_spec...  0.86 us
  transfers between devices with their start and end apart: 4, of which 2 were waited for; matrix products, arithmetic and copies ran while one was open for 0% of the time, Pallas kernels for 33%

profile of v1, /device:TPU:0, one launch (start us, length us, event | category | flops | bytes accessed | tf_op | source)
XLA Modules:
  0.0 38.7 jit_solution(189919405558153223)
XLA Ops:
  0.6 0.5 %collective-permute-start = (bf16[2048,128]{1,0:T(8,128)(2,1)}, bf16[2048,128]{1,0:T(8,128)(2,1)S(1)}, u32[]{:S(2)}, u32[]{:S(2)}) collective-permute-start(bf16[2048,128]{1,0:T(8,128)(2,1)} %bitcast.11), channel_id=1, source_target_pairs={{0,1},{1,0},{2,3},{3,2},{4,5},{5,4},{6,7},{7,6},{8,9},{9,8},{10,11... | collective-permute-start | bytes 1572872 | tf_op jit(solution)/shard_map/ppermute | solution.py:391
  1.1 0.1 collective-permute-start.1
  1.2 5.1 %layout_queries.1 = bf16[16,32,128]{2,1,0:T(8,128)(2,1)} custom-call(bf16[2,4,16,128]{3,2,1,0:T(8,128)(2,1)} %bitcast.15), custom_call_target="tpu_custom_call" | custom-call | tf_op jit(solution)/shard_map/layout_queries/pallas_call | solution.py:55
  6.4 8.3 %all-to-all-start = ((bf16[16,32,128]{2,1,0:T(8,128)(2,1)}), bf16[16,32,128]{2,1,0:T(8,128)(2,1)S(1)}, u32[]{:S(2)}, u32[]{:S(2)}) async-start(bf16[16,32,128]{2,1,0:T(8,128)(2,1)} %layout_queries.1), calls=%async_computation | async-start | bytes 262144 | tf_op jit(solution)/shard_map/all_to_all | solution.py:388
  14.7 4.0 %suffix_attention_0.1 = (f32[64,128]{1,0:T(8,128)S(1)}, f32[64,128]{1,0:T(8,128)S(1)}, bf16[2048,128]{1,0:T(8,128)(2,1)S(1)}, bf16[2048,128]{1,0:T(8,128)(2,1)S(1)}) custom-call(s32[2]{0:T(128)} %refs_0_.3, s32[2]{0:T(128)} %refs_1_.3, bf16[2,64,128]{2,1,0:T(8,128)(2,1)} %refs_2_.3, bf16[2,8192,128]{2,1,0:T(8,128)(2,1)} %bitcast.7, ...), custom_call_target="tpu_custom_call" | custom-call | flops 268435456 | bytes 4194304 | tf_op jit(solution)/shard_map/suffix_attention_0/pallas_call | solution.py:170
  18.7 3.8 %all-to-all-done = bf16[16,32,128]{2,1,0:T(8,128)(2,1)S(1)} async-done(((bf16[16,32,128]{2,1,0:T(8,128)(2,1)}), bf16[16,32,128]{2,1,0:T(8,128)(2,1)S(1)}, u32[]{:S(2)}, u32[]{:S(2)}) %all-to-all-start) | async-done | bytes 131104 | tf_op jit(solution)/shard_map/all_to_all | solution.py:388
  22.5 0.0 collective-permute-done.k1_ref
  22.5 0.0 collective-permute-done.1.v1_ref
  22.5 3.8 %prefix_attention.1 = s32[16,24,128]{2,1,0:T(8,128)} custom-call(bf16[512,128]{1,0:T(8,128)(2,1)S(1)} %bitcast.6, bf16[2048,128]{1,0:T(8,128)(2,1)S(1)} %get-tuple-element.8.k0_ref, bf16[2048,128]{1,0:T(8,128)(2,1)S(1)} %get-tuple-element.9.v0_ref, bf16[2048,128]{1,0:T(8,128)(2,1)S(1)} %collective-permute-done.k1_ref, ...), custom_call_target="tpu_custom_call" | custom-call | flops 1073741824 | bytes 2490368 | tf_op jit(solution)/shard_map/prefix_attention/pallas_call | solution.py:299
  26.3 3.5 %all-to-all-start.1 = ((s32[16,24,128]{2,1,0:T(8,128)}), s32[16,24,128]{2,1,0:T(8,128)S(1)}, u32[]{:S(2)}, u32[]{:S(2)}) async-start(s32[16,24,128]{2,1,0:T(8,128)} %prefix_attention.1), calls=%async_computation.1 | async-start | bytes 393216 | tf_op jit(solution)/shard_map/all_to_all | solution.py:413
  29.8 3.7 %suffix_attention_1.1 = (f32[2,64,128]{2,1,0:T(8,128)S(1)}, f32[2,64,128]{2,1,0:T(8,128)S(1)}) custom-call(s32[2]{0:T(128)} %refs_0_.3, s32[2]{0:T(128)} %refs_1_.3, bf16[2,64,128]{2,1,0:T(8,128)(2,1)} %refs_2_.3, bf16[2,8192,128]{2,1,0:T(8,128)(2,1)} %bitcast.8, bf16[2,8192,128]{2,1,0:T(8,128)(2,1)} %bitcast.10, f32[64,128]{1,0:T(8,128)S(1)} %get-tuple-element.10.refs_5_, ...), custom_call_target="tpu_custom_call" | custom-call | flops 268435456 | bytes 4194304 | tf_op jit(solution)/shard_map/suffix_attention_1/pallas_call | solution.py:170
  33.5 4.4 %all-to-all-done.1.got_ref = s32[16,24,128]{2,1,0:T(8,128)S(1)} async-done(((s32[16,24,128]{2,1,0:T(8,128)}), s32[16,24,128]{2,1,0:T(8,128)S(1)}, u32[]{:S(2)}, u32[]{:S(2)}) %all-to-all-start.1) | async-done | bytes 196640 | tf_op jit(solution)/shard_map/all_to_all | solution.py:413
  37.8 0.9 %join_partials.1 = (f32[2,64,128]{2,1,0:T(8,128)}, f32[2,64]{1,0:T(2,128)}) custom-call(s32[16,24,128]{2,1,0:T(8,128)S(1)} %all-to-all-done.1.got_ref, f32[2,64,128]{2,1,0:T(8,128)S(1)} %get-tuple-element.12.suf_ref, f32[2,64,128]{2,1,0:T(8,128)S(1)} %get-tuple-element.13.suf_log_ref), custom_call_target="tpu_custom_call" | custom-call | tf_op jit(solution)/shard_map/join_partials/pallas_call | solution.py:367
Async XLA Ops:
  0.6 21.9 %collective-permute-start = (bf16[2048,128]{1,0:T(8,128)(2,1)}, bf16[2048,128]{1,0:T(8,128)(2,1)S(1)}, u32[]{:S(2)}, u32[]{:S(2)}) collective-permute-start(bf16[2048,128]{1,0:T(8,128)(2,1)} %bitcast.11), channel_id=1, source_target_pairs={{0,1},{1,0},{2,3},{3,2},{4,5},{5,4},{6,7},{7,6},{8,9},{9,8},{10,11... | collective-permute-start | bytes 1572872 | tf_op jit(solution)/shard_map/ppermute | solution.py:391
  1.1 21.3 %collective-permute-start.1 = (bf16[2048,128]{1,0:T(8,128)(2,1)}, bf16[2048,128]{1,0:T(8,128)(2,1)S(1)}, u32[]{:S(2)}, u32[]{:S(2)}) collective-permute-start(bf16[2048,128]{1,0:T(8,128)(2,1)} %bitcast.13), channel_id=1, source_target_pairs={{0,1},{1,0},{2,3},{3,2},{4,5},{5,4},{6,7},{7,6},{8,9},{9,8},{10,11... | collective-permute-start | bytes 1572872 | tf_op jit(solution)/shard_map/ppermute | solution.py:392
  6.4 16.1 %all-to-all-start = ((bf16[16,32,128]{2,1,0:T(8,128)(2,1)}), bf16[16,32,128]{2,1,0:T(8,128)(2,1)S(1)}, u32[]{:S(2)}, u32[]{:S(2)}) async-start(bf16[16,32,128]{2,1,0:T(8,128)(2,1)} %layout_queries.1), calls=%async_computation | async-start | bytes 262144 | tf_op jit(solution)/shard_map/all_to_all | solution.py:388
  26.3 11.6 %all-to-all-start.1 = ((s32[16,24,128]{2,1,0:T(8,128)}), s32[16,24,128]{2,1,0:T(8,128)S(1)}, u32[]{:S(2)}, u32[]{:S(2)}) async-start(s32[16,24,128]{2,1,0:T(8,128)} %prefix_attention.1), calls=%async_computation.1 | async-start | bytes 393216 | tf_op jit(solution)/shard_map/all_to_all | solution.py:413

commit v2 on v1

--- a/solution.py
+++ b/solution.py
@@ -8,7 +8,7 @@
 from jax.experimental.pallas import tpu as pltpu
 from jax.sharding import PartitionSpec as P
 
-ROW_TILE = 256
+ROW_TILE = 128
 STEP_ROWS = 512
 SUF_COPIES = 4
 IN_FLIGHT = 4
@@ -20,7 +20,7 @@
 LEAST = 1e-25
 PEAK_LEAST = 1e-33
 NT = (((1,), (1,)), ((), ()))
-PREFIX_VMEM = 24 * 1024 * 1024
+PREFIX_VMEM = 14 * 1024 * 1024
 SUFFIX_VMEM = 20 * 1024 * 1024
 SMALL_VMEM = 8 * 1024 * 1024
 IN_VMEM = pl.BlockSpec(memory_space=pltpu.VMEM)
@@ -31,48 +31,67 @@
     return pltpu.with_memory_space_constraint(array, pltpu.HBM)
 
 
-def layout_kernel(q_hbm, sent_hbm, sems):
-    count, groups, group, _ = q_hbm.shape
+def layout_kernel(*refs, carried):
+    q_hbm, carried_refs, refs = refs[0], refs[1 : 1 + carried], refs[1 + carried :]
+    sent_hbm, brought_refs = refs[0], refs[1 : 1 + carried]
+    buf, in_sems, out_sems, carry_sems = refs[1 + carried :]
+    groups, rows, _ = buf.shape
+    count = q_hbm.shape[0]
+    group = rows // count
     repeats = sent_hbm.shape[0] // groups
-    copies = [
+    reads = [
         pltpu.make_async_copy(
-            q_hbm.at[r],
-            sent_hbm.at[pl.ds(s * groups, groups), pl.ds(r * group, group)],
-            sems.at[s, r],
-        )
-        for s in range(repeats)
+            q_hbm.at[r, pl.ds(g * group, group)], buf.at[g, pl.ds(r * group, group)], in_sems.at[g, r]
+        )
+        for g in range(groups)
         for r in range(count)
     ]
-    for copy in copies:
+    carries = [
+        pltpu.make_async_copy(source, target, carry_sems.at[i])
+        for i, (source, target) in enumerate(zip(carried_refs, brought_refs))
+    ]
+    for copy in reads + carries:
         copy.start()
-    for copy in copies:
+    for read in reads:
+        read.wait()
+    writes = [
+        pltpu.make_async_copy(buf, sent_hbm.at[pl.ds(s * groups, groups)], out_sems.at[s])
+        for s in range(repeats)
+    ]
+    for write in writes:
+        write.start()
+    for copy in writes + carries:
         copy.wait()
 
 
-def layout_queries(queries, groups, repeats):
+def layout_queries(queries, groups, repeats, carried):
     count, heads, width = queries.shape
-    group = heads // groups
+    rows = count * heads // groups
     return pl.pallas_call(
-        layout_kernel,
-        in_specs=[IN_HBM],
-        out_specs=IN_HBM,
-        out_shape=pltpu.HBM((repeats * groups, count * group, width), queries.dtype),
-        scratch_shapes=[pltpu.SemaphoreType.DMA((repeats, count))],
+        functools.partial(layout_kernel, carried=len(carried)),
+        in_specs=[IN_HBM] * (1 + len(carried)),
+        out_specs=[IN_HBM] + [IN_VMEM] * len(carried),
+        out_shape=[pltpu.HBM((repeats * groups, rows, width), queries.dtype)]
+        + [pltpu.VMEM(array.shape, array.dtype) for array in carried],
+        scratch_shapes=[
+            pltpu.VMEM((groups, rows, width), queries.dtype),
+            pltpu.SemaphoreType.DMA((groups, count)),
+            pltpu.SemaphoreType.DMA((repeats,)),
+            pltpu.SemaphoreType.DMA((len(carried),)),
+        ],
         compiler_params=pltpu.CompilerParams(vmem_limit_bytes=SMALL_VMEM),
         name="layout_queries",
-    )(in_hbm(queries.reshape(count, groups, group, width)))
-
-
-def suffix_kernel(*refs, place, carried, kv_count, score_scale):
+    )(in_hbm(queries), *map(in_hbm, carried))
+
+
+def suffix_kernel(*refs, place, kv_count, score_scale):
     slot_hbm, length_hbm, q_hbm, k_hbm, v_hbm = refs[:5]
     refs = refs[5:]
     count, heads, width = q_hbm.shape
-    carried_refs, refs = refs[:carried], refs[carried:]
     last = place == count - 1
     earlier, refs = (refs[: 2 * place], refs[2 * place :]) if last else ((), refs)
     mixed_ref, log_ref = refs[:2]
-    brought_refs, refs = refs[2 : 2 + carried], refs[2 + carried :]
-    slot_ref, length_ref, q_ref, k_buf, v_buf, score_ref, sems, small_sems = refs
+    slot_ref, length_ref, q_ref, k_buf, v_buf, score_ref, sems, small_sems = refs[2:]
     rows = k_hbm.shape[1]
     copy_rows = rows // SUF_COPIES
     copies = []
@@ -86,21 +105,17 @@
         pltpu.make_async_copy(source, target, small_sems.at[i])
         for i, (source, target) in enumerate(
             [(slot_hbm, slot_ref), (length_hbm, length_ref), (q_hbm, q_ref)]
-            + list(zip(carried_refs, brought_refs))
         )
     ]
-    carries = small[3:]
-    for copy in small[:3] + copies[:IN_FLIGHT]:
+    for copy in small + copies[:IN_FLIGHT]:
         copy.start()
 
     def arrive(i):
         copies[i].wait()
         if i + IN_FLIGHT < len(copies):
             copies[i + IN_FLIGHT].start()
-        elif i + IN_FLIGHT - len(copies) < carried:
-            carries[i + IN_FLIGHT - len(copies)].start()
-
-    for copy in small[:3]:
+
+    for copy in small:
         copy.wait()
 
     def request_of(slot):
@@ -141,8 +156,6 @@
     total = jnp.sum(sums, axis=1, keepdims=True)
     mixed = acc / total
     log = jnp.broadcast_to(row_max * score_scale + jnp.log(total), (heads, width))
-    for carry in carries:
-        carry.wait()
     if not last:
         mixed_ref[...] = mixed
         log_ref[...] = log
@@ -154,7 +167,7 @@
         log_ref[request_of(slot)] = earlier[2 * slot + 1][...]
 
 
-def suffix_partials(place, queries, keys, values, lengths, slots, carried, earlier, score_scale):
+def suffix_partials(place, queries, keys, values, lengths, slots, earlier, score_scale):
     count, heads, width = queries.shape
     kv_count = keys.shape[2]
     rows = keys.shape[1] * kv_count
@@ -165,20 +178,17 @@
         queries,
         keys.reshape(count, rows, width),
         values.reshape(count, rows, width),
-        *carried,
     )
     return pl.pallas_call(
         functools.partial(
             suffix_kernel,
             place=place,
-            carried=len(carried),
             kv_count=kv_count,
             score_scale=score_scale,
         ),
         in_specs=[IN_HBM] * len(operands) + [IN_VMEM] * len(earlier),
-        out_specs=[IN_VMEM] * (2 + len(carried)),
-        out_shape=[pltpu.VMEM(result, jnp.float32)] * 2
-        + [pltpu.VMEM(array.shape, array.dtype) for array in carried],
+        out_specs=[IN_VMEM] * 2,
+        out_shape=[pltpu.VMEM(result, jnp.float32)] * 2,
         scratch_shapes=[
             pltpu.SMEM((count,), jnp.int32),
             pltpu.SMEM((count,), jnp.int32),
@@ -187,7 +197,7 @@
             pltpu.VMEM((rows, width), values.dtype),
             pltpu.VMEM((heads, rows), jnp.float32),
             pltpu.SemaphoreType.DMA((2, SUF_COPIES)),
-            pltpu.SemaphoreType.DMA((3 + len(carried),)),
+            pltpu.SemaphoreType.DMA((3,)),
         ],
         compiler_params=pltpu.CompilerParams(vmem_limit_bytes=SUFFIX_VMEM),
         cost_estimate=pl.CostEstimate(
@@ -204,7 +214,7 @@
 
 
 def prefix_kernel(
-    q_ref, k0_ref, v0_ref, k1_ref, v1_ref, out_hbm, out_ref, score_ref, sems, *, per_dest, score_scale
+    q_ref, k0_ref, v0_ref, k1_ref, v1_ref, _, out_hbm, out_ref, score_ref, sems, *, per_dest, score_scale
 ):
     width = q_ref.shape[1]
     tiles = q_ref.shape[0] // ROW_TILE
@@ -285,7 +295,7 @@
         copy.wait()
 
 
-def prefix_partials(rows_q, keys, values, far_keys, far_values, per_dest, score_scale):
+def prefix_partials(rows_q, keys, values, far_keys, far_values, after, per_dest, score_scale):
     rows, width = rows_q.shape
     length = keys.shape[0]
     step_rows = min(STEP_ROWS, rows)
@@ -296,6 +306,7 @@
         blocked["grid"] = (rows // step_rows,)
         blocked["in_specs"] = [pl.BlockSpec((step_rows, width), lambda i: (i, 0))]
         blocked["in_specs"] += [pl.BlockSpec((length, width), lambda i: (0, 0))] * 4
+    blocked["in_specs"] += [pl.BlockSpec(memory_space=pl.ANY)]
     return pl.pallas_call(
         functools.partial(prefix_kernel, per_dest=per_dest, score_scale=score_scale),
         **blocked,
@@ -313,7 +324,7 @@
             transcendentals=2 * rows * length,
         ),
         name="prefix_attention",
-    )(rows_q, keys, values, far_keys, far_values)
+    )(rows_q, keys, values, far_keys, far_values, after)
 
 
 def join_kernel(got_ref, suf_ref, suf_log_ref, out_ref, log_ref, *, kv_count):
@@ -384,31 +395,34 @@
     kv_count = suffix_keys.shape[2]
     per_dest = count * heads // kv_count
     score_scale = 1.0 / math.sqrt(width)
-    sent = layout_queries(queries, kv_count, lax.axis_size("seq"))
+    sent, near_keys, near_values = layout_queries(
+        queries, kv_count, lax.axis_size("seq"), (prefix_keys[:, 0, :], prefix_values[:, 0, :])
+    )
     got_q = lax.all_to_all(sent, ("seq", "head"), split_axis=0, concat_axis=0, tiled=True)
-    keys = prefix_keys[:, 0, :]
-    values = prefix_values[:, 0, :]
-    far_keys = lax.ppermute(keys, "rep", [(0, 1), (1, 0)])
-    far_values = lax.ppermute(values, "rep", [(0, 1), (1, 0)])
+    far_keys = lax.ppermute(near_keys, "rep", [(0, 1), (1, 0)])
+    far_values = lax.ppermute(near_values, "rep", [(0, 1), (1, 0)])
     earlier = []
     for place in range(count):
-        first, last = place == 0, place == count - 1
-        mixed, log, *brought = suffix_partials(
+        mixed, log = suffix_partials(
             place,
             queries,
             suffix_keys,
             suffix_values,
             suffix_lengths,
             slot_map,
-            (keys, values) if first else (),
-            earlier if last else (),
+            earlier if place == count - 1 else (),
             score_scale,
         )
         earlier += [mixed, log]
-        if first:
-            near_keys, near_values = brought
     partials = prefix_partials(
-        got_q.reshape(-1, width), near_keys, near_values, far_keys, far_values, per_dest, score_scale
+        got_q.reshape(-1, width),
+        near_keys,
+        near_values,
+        far_keys,
+        far_values,
+        earlier[0],
+        per_dest,
+        score_scale,
     )
     got = lax.all_to_all(partials, ("seq", "head"), split_axis=0, concat_axis=0, tiled=True)
     return join_partials(got, mixed, log, kv_count)

time: 39.1 us -> 35.6 us (0.910)
  Pallas kernels: 17.4 us -> 13.6 us
    pallas_call x3, Pallas kernels: 12.8 us -> 9.08 us  [the longest x2 7.34 us: suffix_partials(): pl.pallas_call(functools.partial(suffix_kernel, place=place, kv_count=kv_...]
  transfers between devices with their start and end apart: 4 -> 4, of which waited for: 2 -> 2; matrix products, arithmetic and copies ran while one was open for 0% -> 0% of each run, Pallas kernels for 33% -> 21%
where the time goes in v2:
time: 35.6 us; the launch traced here: 35.2 us
  Pallas kernels  13.6 us (38%)
  starting transfers between devices  12.4 us (35%)
  waiting for transfers between devices  8.49 us (24%)
  between operations  0.68 us (2%)
    all_to_all x1, starting transfers between devices, per_device(): lax.all_to_all(sent, ('seq', 'head'), split_axis=0, concat_axis=0, tiled=...  8.29 us
    pallas_call x2, Pallas kernels, suffix_partials(): pl.pallas_call(functools.partial(suffix_kernel, place=place, kv_count=kv_...  7.34 us
    all_to_all x1, waiting for transfers between devices, per_device(): lax.all_to_all(partials, ('seq', 'head'), split_axis=0, concat_axis=0, ti...  4.36 us
    all_to_all x1, waiting for transfers between devices, per_device(): lax.all_to_all(sent, ('seq', 'head'), split_axis=0, concat_axis=0, tiled=...  4.12 us
    pallas_call x1, Pallas kernels, prefix_partials(): pl.pallas_call(functools.partial(prefix_kernel, per_dest=per_dest, score_...  3.68 us
    all_to_all x1, starting transfers between devices, per_device(): lax.all_to_all(partials, ('seq', 'head'), split_axis=0, concat_axis=0, ti...  3.53 us
    pallas_call x1, Pallas kernels, layout_queries(): pl.pallas_call(functools.partial(layout_kernel, carried=len(carried)), in...  1.74 us
    pallas_call x1, Pallas kernels, join_partials(): pl.pallas_call(functools.partial(join_kernel, kv_count=kv_count), in_spec...  0.86 us
  transfers between devices with their start and end apart: 4, of which 2 were waited for; matrix products, arithmetic and copies ran while one was open for 0% of the time, Pallas kernels for 21%

profile of v2, /device:TPU:0, one launch (start us, length us, event | category | flops | bytes accessed | tf_op | source)
XLA Modules:
  0.0 35.2 jit_solution(11998455170209724240)
XLA Ops:
  0.6 1.7 %layout_queries.1 = (bf16[16,32,128]{2,1,0:T(8,128)(2,1)}, bf16[2048,128]{1,0:T(8,128)(2,1)S(1)}, bf16[2048,128]{1,0:T(8,128)(2,1)S(1)}) custom-call(bf16[2,64,128]{2,1,0:T(8,128)(2,1)} %refs_2_.3, bf16[2048,128]{1,0:T(8,128)(2,1)} %bitcast.10, bf16[2048,128]{1,0:T(8,128)(2,1)} %bitcast.11), custom_call_target="tpu_custom_call" | custom-call | tf_op jit(solution)/shard_map/layout_queries/pallas_call | solution.py:70
  2.4 0.5 %collective-permute-start = (bf16[2048,128]{1,0:T(8,128)(2,1)S(1)}, bf16[2048,128]{1,0:T(8,128)(2,1)S(1)}, u32[]{:S(2)}, u32[]{:S(2)}) collective-permute-start(bf16[2048,128]{1,0:T(8,128)(2,1)S(1)} %get-tuple-element.10.k0_ref), channel_id=1, source_target_pairs={{0,1},{1,0},{2,3},{3,2},{4,5},{5,4},{6,7},{7,6},{8,9},{9,8},{10,11... | collective-permute-start | bytes 1572872 | tf_op jit(solution)/shard_map/ppermute | solution.py:402
  2.9 0.1 collective-permute-start.1
  3.0 8.3 %all-to-all-start = ((bf16[16,32,128]{2,1,0:T(8,128)(2,1)}), bf16[16,32,128]{2,1,0:T(8,128)(2,1)S(1)}, u32[]{:S(2)}, u32[]{:S(2)}) async-start(bf16[16,32,128]{2,1,0:T(8,128)(2,1)} %get-tuple-element.9), calls=%async_computation | async-start | bytes 262144 | tf_op jit(solution)/shard_map/all_to_all | solution.py:401
  11.3 3.7 %suffix_attention_0.1 = (f32[64,128]{1,0:T(8,128)S(1)}, f32[64,128]{1,0:T(8,128)S(1)}) custom-call(s32[2]{0:T(128)} %refs_0_.5, s32[2]{0:T(128)} %refs_1_.3, bf16[2,64,128]{2,1,0:T(8,128)(2,1)} %refs_2_.3, bf16[2,8192,128]{2,1,0:T(8,128)(2,1)} %bitcast.6, bf16[2,8192,128]{2,1,0:T(8,128)(2,1)} %bitcast.8), custom_call_target="tpu_custom_call" | custom-call | flops 268435456 | bytes 4194304 | tf_op jit(solution)/shard_map/suffix_attention_0/pallas_call | solution.py:182
  14.9 4.1 %all-to-all-done = bf16[16,32,128]{2,1,0:T(8,128)(2,1)S(1)} async-done(((bf16[16,32,128]{2,1,0:T(8,128)(2,1)}), bf16[16,32,128]{2,1,0:T(8,128)(2,1)S(1)}, u32[]{:S(2)}, u32[]{:S(2)}) %all-to-all-start) | async-done | bytes 131104 | tf_op jit(solution)/shard_map/all_to_all | solution.py:401
  19.1 0.0 collective-permute-done.k1_ref
  19.1 0.0 collective-permute-done.1.v1_ref
  19.1 3.7 %prefix_attention.1 = s32[16,24,128]{2,1,0:T(8,128)} custom-call(bf16[512,128]{1,0:T(8,128)(2,1)S(1)} %bitcast.5, bf16[2048,128]{1,0:T(8,128)(2,1)S(1)} %get-tuple-element.10.k0_ref, bf16[2048,128]{1,0:T(8,128)(2,1)S(1)} %get-tuple-element.11.v0_ref, bf16[2048,128]{1,0:T(8,128)(2,1)S(1)} %collective-permute-done.k1_ref, ...), custom_call_target="tpu_custom_call" | custom-call | flops 1073741824 | bytes 2490368 | tf_op jit(solution)/shard_map/prefix_attention/pallas_call | solution.py:310
  22.8 3.5 %all-to-all-start.1 = ((s32[16,24,128]{2,1,0:T(8,128)}), s32[16,24,128]{2,1,0:T(8,128)S(1)}, u32[]{:S(2)}, u32[]{:S(2)}) async-start(s32[16,24,128]{2,1,0:T(8,128)} %prefix_attention.1), calls=%async_computation.1 | async-start | bytes 393216 | tf_op jit(solution)/shard_map/all_to_all | solution.py:427
  26.3 3.7 %suffix_attention_1.1 = (f32[2,64,128]{2,1,0:T(8,128)S(1)}, f32[2,64,128]{2,1,0:T(8,128)S(1)}) custom-call(s32[2]{0:T(128)} %refs_0_.5, s32[2]{0:T(128)} %refs_1_.3, bf16[2,64,128]{2,1,0:T(8,128)(2,1)} %refs_2_.3, bf16[2,8192,128]{2,1,0:T(8,128)(2,1)} %bitcast.7, bf16[2,8192,128]{2,1,0:T(8,128)(2,1)} %bitcast.9, f32[64,128]{1,0:T(8,128)S(1)} %get-tuple-element.12._.refs_5_, ...), custom_call_target="tpu_custom_call" | custom-call | flops 268435456 | bytes 4194304 | tf_op jit(solution)/shard_map/suffix_attention_1/pallas_call | solution.py:182
  30.0 4.4 %all-to-all-done.1.got_ref = s32[16,24,128]{2,1,0:T(8,128)S(1)} async-done(((s32[16,24,128]{2,1,0:T(8,128)}), s32[16,24,128]{2,1,0:T(8,128)S(1)}, u32[]{:S(2)}, u32[]{:S(2)}) %all-to-all-start.1) | async-done | bytes 196640 | tf_op jit(solution)/shard_map/all_to_all | solution.py:427
  34.4 0.9 %join_partials.1 = (f32[2,64,128]{2,1,0:T(8,128)}, f32[2,64]{1,0:T(2,128)}) custom-call(s32[16,24,128]{2,1,0:T(8,128)S(1)} %all-to-all-done.1.got_ref, f32[2,64,128]{2,1,0:T(8,128)S(1)} %get-tuple-element.14.suf_ref, f32[2,64,128]{2,1,0:T(8,128)S(1)} %get-tuple-element.15.suf_log_ref), custom_call_target="tpu_custom_call" | custom-call | tf_op jit(solution)/shard_map/join_partials/pallas_call | solution.py:378
Async XLA Ops:
  2.4 16.7 %collective-permute-start = (bf16[2048,128]{1,0:T(8,128)(2,1)S(1)}, bf16[2048,128]{1,0:T(8,128)(2,1)S(1)}, u32[]{:S(2)}, u32[]{:S(2)}) collective-permute-start(bf16[2048,128]{1,0:T(8,128)(2,1)S(1)} %get-tuple-element.10.k0_ref), channel_id=1, source_target_pairs={{0,1},{1,0},{2,3},{3,2},{4,5},{5,4},{6,7},{7,6},{8,9},{9,8},{10,11... | collective-permute-start | bytes 1572872 | tf_op jit(solution)/shard_map/ppermute | solution.py:402
  2.9 16.2 %collective-permute-start.1 = (bf16[2048,128]{1,0:T(8,128)(2,1)S(1)}, bf16[2048,128]{1,0:T(8,128)(2,1)S(1)}, u32[]{:S(2)}, u32[]{:S(2)}) collective-permute-start(bf16[2048,128]{1,0:T(8,128)(2,1)S(1)} %get-tuple-element.11.v0_ref), channel_id=1, source_target_pairs={{0,1},{1,0},{2,3},{3,2},{4,5},{5,4},{6,7},{7,6},{8,9},{9,8},{10,11... | collective-permute-start | bytes 1572872 | tf_op jit(solution)/shard_map/ppermute | solution.py:403
  3.0 16.1 %all-to-all-start = ((bf16[16,32,128]{2,1,0:T(8,128)(2,1)}), bf16[16,32,128]{2,1,0:T(8,128)(2,1)S(1)}, u32[]{:S(2)}, u32[]{:S(2)}) async-start(bf16[16,32,128]{2,1,0:T(8,128)(2,1)} %get-tuple-element.9), calls=%async_computation | async-start | bytes 262144 | tf_op jit(solution)/shard_map/all_to_all | solution.py:401
  22.8 11.6 %all-to-all-start.1 = ((s32[16,24,128]{2,1,0:T(8,128)}), s32[16,24,128]{2,1,0:T(8,128)S(1)}, u32[]{:S(2)}, u32[]{:S(2)}) async-start(s32[16,24,128]{2,1,0:T(8,128)} %prefix_attention.1), calls=%async_computation.1 | async-start | bytes 393216 | tf_op jit(solution)/shard_map/all_to_all | solution.py:427

commit v3 on v2

--- a/solution.py
+++ b/solution.py
@@ -388,6 +388,27 @@
     )(got, suf_mixed, suf_log)
 
 
+def exchange(pieces):
+    seq, head, rep = lax.axis_size("seq"), lax.axis_size("head"), lax.axis_size("rep")
+    order = seq_order(seq)
+    groups = [
+        [(s * head + h) * rep + r for s in order for h in range(head)] for r in range(rep)
+    ]
+    return lax.all_to_all(
+        pieces,
+        ("seq", "head", "rep"),
+        split_axis=0,
+        concat_axis=0,
+        axis_index_groups=groups,
+        tiled=True,
+    )
+
+
+def seq_order(count):
+    middle = count // 2
+    return [middle] + [s for s in range(count) if s != middle]
+
+
 def per_device(
     queries, prefix_keys, prefix_values, suffix_keys, suffix_values, suffix_lengths, slot_map
 ):
@@ -398,7 +419,7 @@
     sent, near_keys, near_values = layout_queries(
         queries, kv_count, lax.axis_size("seq"), (prefix_keys[:, 0, :], prefix_values[:, 0, :])
     )
-    got_q = lax.all_to_all(sent, ("seq", "head"), split_axis=0, concat_axis=0, tiled=True)
+    got_q = exchange(sent)
     far_keys = lax.ppermute(near_keys, "rep", [(0, 1), (1, 0)])
     far_values = lax.ppermute(near_values, "rep", [(0, 1), (1, 0)])
     earlier = []
@@ -424,7 +445,7 @@
         per_dest,
         score_scale,
     )
-    got = lax.all_to_all(partials, ("seq", "head"), split_axis=0, concat_axis=0, tiled=True)
+    got = exchange(partials)
     return join_partials(got, mixed, log, kv_count)
 
 

time: 35.6 us -> 33.5 us (0.941)
  waiting for transfers between devices: 8.49 us -> 4.49 us
  starting transfers between devices: 12.4 us -> 14.3 us
    all_to_all x2, waiting for transfers between devices: 8.49 us -> 4.49 us  [exchange(): lax.all_to_all(pieces, ('seq', 'head', 'rep'), split_axis=0, concat_axis=...]
    all_to_all x2, starting transfers between devices: 11.8 us -> 13.7 us  [exchange(): lax.all_to_all(pieces, ('seq', 'head', 'rep'), split_axis=0, concat_axis=...]
  transfers between devices with their start and end apart: 4 -> 4, of which waited for: 2 -> 2; matrix products, arithmetic and copies ran while one was open for 0% -> 0% of each run, Pallas kernels for 21% -> 22%
where the time goes in v3:
time: 33.5 us; the launch traced here: 33.1 us
  starting transfers between devices  14.3 us (43%)
  Pallas kernels  13.6 us (41%)
  waiting for transfers between devices  4.49 us (13%)
  between operations  0.67 us (2%)
    all_to_all x2, starting transfers between devices, exchange(): lax.all_to_all(pieces, ('seq', 'head', 'rep'), split_axis=0, concat_axis=...  13.7 us
    pallas_call x2, Pallas kernels, suffix_partials(): pl.pallas_call(functools.partial(suffix_kernel, place=place, kv_count=kv_...  7.34 us
    all_to_all x2, waiting for transfers between devices, exchange(): lax.all_to_all(pieces, ('seq', 'head', 'rep'), split_axis=0, concat_axis=...  4.49 us
    pallas_call x1, Pallas kernels, prefix_partials(): pl.pallas_call(functools.partial(prefix_kernel, per_dest=per_dest, score_...  3.68 us
    pallas_call x1, Pallas kernels, layout_queries(): pl.pallas_call(functools.partial(layout_kernel, carried=len(carried)), in...  1.74 us
    pallas_call x1, Pallas kernels, join_partials(): pl.pallas_call(functools.partial(join_kernel, kv_count=kv_count), in_spec...  0.86 us
  transfers between devices with their start and end apart: 4, of which 2 were waited for; matrix products, arithmetic and copies ran while one was open for 0% of the time, Pallas kernels for 22%

profile of v3, /device:TPU:0, one launch (start us, length us, event | category | flops | bytes accessed | tf_op | source)
XLA Modules:
  0.0 33.1 jit_solution(7876876872799878240)
XLA Ops:
  0.6 1.7 %layout_queries.1 = (bf16[16,32,128]{2,1,0:T(8,128)(2,1)}, bf16[2048,128]{1,0:T(8,128)(2,1)S(1)}, bf16[2048,128]{1,0:T(8,128)(2,1)S(1)}) custom-call(bf16[2,64,128]{2,1,0:T(8,128)(2,1)} %refs_2_.3, bf16[2048,128]{1,0:T(8,128)(2,1)} %bitcast.10, bf16[2048,128]{1,0:T(8,128)(2,1)} %bitcast.11), custom_call_target="tpu_custom_call" | custom-call | tf_op jit(solution)/shard_map/layout_queries/pallas_call | solution.py:70
  2.4 0.5 %collective-permute-start = (bf16[2048,128]{1,0:T(8,128)(2,1)S(1)}, bf16[2048,128]{1,0:T(8,128)(2,1)S(1)}, u32[]{:S(2)}, u32[]{:S(2)}) collective-permute-start(bf16[2048,128]{1,0:T(8,128)(2,1)S(1)} %get-tuple-element.10.k0_ref), channel_id=1, source_target_pairs={{0,1},{1,0},{2,3},{3,2},{4,5},{5,4},{6,7},{7,6},{8,9},{9,8},{10,11... | collective-permute-start | bytes 1572872 | tf_op jit(solution)/shard_map/ppermute | solution.py:423
  2.9 0.1 collective-permute-start.1
  3.0 8.8 %all-to-all-start = ((bf16[16,32,128]{2,1,0:T(8,128)(2,1)}), bf16[16,32,128]{2,1,0:T(8,128)(2,1)S(1)}, u32[]{:S(2)}, u32[]{:S(2)}) async-start(bf16[16,32,128]{2,1,0:T(8,128)(2,1)} %get-tuple-element.9), calls=%async_computation | async-start | bytes 262144 | tf_op jit(solution)/shard_map/all_to_all | solution.py:397
  11.7 3.7 %suffix_attention_0.1 = (f32[64,128]{1,0:T(8,128)S(1)}, f32[64,128]{1,0:T(8,128)S(1)}) custom-call(s32[2]{0:T(128)} %refs_0_.5, s32[2]{0:T(128)} %refs_1_.3, bf16[2,64,128]{2,1,0:T(8,128)(2,1)} %refs_2_.3, bf16[2,8192,128]{2,1,0:T(8,128)(2,1)} %bitcast.6, bf16[2,8192,128]{2,1,0:T(8,128)(2,1)} %bitcast.8), custom_call_target="tpu_custom_call" | custom-call | flops 268435456 | bytes 4194304 | tf_op jit(solution)/shard_map/suffix_attention_0/pallas_call | solution.py:182
  15.4 2.0 %all-to-all-done = bf16[16,32,128]{2,1,0:T(8,128)(2,1)S(1)} async-done(((bf16[16,32,128]{2,1,0:T(8,128)(2,1)}), bf16[16,32,128]{2,1,0:T(8,128)(2,1)S(1)}, u32[]{:S(2)}, u32[]{:S(2)}) %all-to-all-start) | async-done | bytes 131104 | tf_op jit(solution)/shard_map/all_to_all | solution.py:397
  17.4 0.0 collective-permute-done.k1_ref
  17.4 0.0 collective-permute-done.1.v1_ref
  17.5 3.7 %prefix_attention.1 = s32[16,24,128]{2,1,0:T(8,128)} custom-call(bf16[512,128]{1,0:T(8,128)(2,1)S(1)} %bitcast.5, bf16[2048,128]{1,0:T(8,128)(2,1)S(1)} %get-tuple-element.10.k0_ref, bf16[2048,128]{1,0:T(8,128)(2,1)S(1)} %get-tuple-element.11.v0_ref, bf16[2048,128]{1,0:T(8,128)(2,1)S(1)} %collective-permute-done.k1_ref, ...), custom_call_target="tpu_custom_call" | custom-call | flops 1073741824 | bytes 2490368 | tf_op jit(solution)/shard_map/prefix_attention/pallas_call | solution.py:310
  21.1 5.0 %all-to-all-start.1 = ((s32[16,24,128]{2,1,0:T(8,128)}), s32[16,24,128]{2,1,0:T(8,128)S(1)}, u32[]{:S(2)}, u32[]{:S(2)}) async-start(s32[16,24,128]{2,1,0:T(8,128)} %prefix_attention.1), calls=%async_computation.1 | async-start | bytes 393216 | tf_op jit(solution)/shard_map/all_to_all | solution.py:397
  26.1 3.7 %suffix_attention_1.1 = (f32[2,64,128]{2,1,0:T(8,128)S(1)}, f32[2,64,128]{2,1,0:T(8,128)S(1)}) custom-call(s32[2]{0:T(128)} %refs_0_.5, s32[2]{0:T(128)} %refs_1_.3, bf16[2,64,128]{2,1,0:T(8,128)(2,1)} %refs_2_.3, bf16[2,8192,128]{2,1,0:T(8,128)(2,1)} %bitcast.7, bf16[2,8192,128]{2,1,0:T(8,128)(2,1)} %bitcast.9, f32[64,128]{1,0:T(8,128)S(1)} %get-tuple-element.12._.refs_5_, ...), custom_call_target="tpu_custom_call" | custom-call | flops 268435456 | bytes 4194304 | tf_op jit(solution)/shard_map/suffix_attention_1/pallas_call | solution.py:182
  29.8 2.5 %all-to-all-done.1.got_ref = s32[16,24,128]{2,1,0:T(8,128)S(1)} async-done(((s32[16,24,128]{2,1,0:T(8,128)}), s32[16,24,128]{2,1,0:T(8,128)S(1)}, u32[]{:S(2)}, u32[]{:S(2)}) %all-to-all-start.1) | async-done | bytes 196640 | tf_op jit(solution)/shard_map/all_to_all | solution.py:397
  32.2 0.9 %join_partials.1 = (f32[2,64,128]{2,1,0:T(8,128)}, f32[2,64]{1,0:T(2,128)}) custom-call(s32[16,24,128]{2,1,0:T(8,128)S(1)} %all-to-all-done.1.got_ref, f32[2,64,128]{2,1,0:T(8,128)S(1)} %get-tuple-element.14.suf_ref, f32[2,64,128]{2,1,0:T(8,128)S(1)} %get-tuple-element.15.suf_log_ref), custom_call_target="tpu_custom_call" | custom-call | tf_op jit(solution)/shard_map/join_partials/pallas_call | solution.py:378
Async XLA Ops:
  2.4 15.1 %collective-permute-start = (bf16[2048,128]{1,0:T(8,128)(2,1)S(1)}, bf16[2048,128]{1,0:T(8,128)(2,1)S(1)}, u32[]{:S(2)}, u32[]{:S(2)}) collective-permute-start(bf16[2048,128]{1,0:T(8,128)(2,1)S(1)} %get-tuple-element.10.k0_ref), channel_id=1, source_target_pairs={{0,1},{1,0},{2,3},{3,2},{4,5},{5,4},{6,7},{7,6},{8,9},{9,8},{10,11... | collective-permute-start | bytes 1572872 | tf_op jit(solution)/shard_map/ppermute | solution.py:423
  2.9 14.6 %collective-permute-start.1 = (bf16[2048,128]{1,0:T(8,128)(2,1)S(1)}, bf16[2048,128]{1,0:T(8,128)(2,1)S(1)}, u32[]{:S(2)}, u32[]{:S(2)}) collective-permute-start(bf16[2048,128]{1,0:T(8,128)(2,1)S(1)} %get-tuple-element.11.v0_ref), channel_id=1, source_target_pairs={{0,1},{1,0},{2,3},{3,2},{4,5},{5,4},{6,7},{7,6},{8,9},{9,8},{10,11... | collective-permute-start | bytes 1572872 | tf_op jit(solution)/shard_map/ppermute | solution.py:424
  3.0 14.5 %all-to-all-start = ((bf16[16,32,128]{2,1,0:T(8,128)(2,1)}), bf16[16,32,128]{2,1,0:T(8,128)(2,1)S(1)}, u32[]{:S(2)}, u32[]{:S(2)}) async-start(bf16[16,32,128]{2,1,0:T(8,128)(2,1)} %get-tuple-element.9), calls=%async_computation | async-start | bytes 262144 | tf_op jit(solution)/shard_map/all_to_all | solution.py:397
  21.1 11.1 %all-to-all-start.1 = ((s32[16,24,128]{2,1,0:T(8,128)}), s32[16,24,128]{2,1,0:T(8,128)S(1)}, u32[]{:S(2)}, u32[]{:S(2)}) async-start(s32[16,24,128]{2,1,0:T(8,128)} %prefix_attention.1), calls=%async_computation.1 | async-start | bytes 393216 | tf_op jit(solution)/shard_map/all_to_all | solution.py:397

commit v4 on v3

--- a/solution.py
+++ b/solution.py
@@ -41,7 +41,9 @@
     repeats = sent_hbm.shape[0] // groups
     reads = [
         pltpu.make_async_copy(
-            q_hbm.at[r, pl.ds(g * group, group)], buf.at[g, pl.ds(r * group, group)], in_sems.at[g, r]
+            q_hbm.at[r, pl.ds(g * group, group)],
+            buf.at[groups - 1 - g, pl.ds(r * group, group)],
+            in_sems.at[g, r],
         )
         for g in range(groups)
         for r in range(count)
@@ -202,7 +204,7 @@
         compiler_params=pltpu.CompilerParams(vmem_limit_bytes=SUFFIX_VMEM),
         cost_estimate=pl.CostEstimate(
             flops=4 * heads * rows * width,
-            bytes_accessed=4 * rows * width,
+            bytes_accessed=4 * rows * width * (16 if place == 0 else 1),
             transcendentals=heads * rows,
         ),
         name=f"suffix_attention_{place}",
@@ -214,14 +216,15 @@
 
 
 def prefix_kernel(
-    q_ref, k0_ref, v0_ref, k1_ref, v1_ref, _, out_hbm, out_ref, score_ref, sems, *, per_dest, score_scale
+    q_ref, k0_ref, v0_ref, k1_ref, v1_ref, _, out_hbm, out_ref, score_ref, sems, *, per_dest, turn, score_scale
 ):
     width = q_ref.shape[1]
     tiles = q_ref.shape[0] // ROW_TILE
     dests = ROW_TILE // per_dest
     keys, values = (k0_ref, k1_ref), (v0_ref, v1_ref)
     units = [(tile, block) for tile in range(tiles) for block in range(2)]
-    first_dest = 0 if out_hbm.shape == out_ref.shape else pl.program_id(0) * (tiles * dests)
+    places = out_hbm.shape[0] // dests
+    first_place = turn + (0 if out_hbm.shape == out_ref.shape else pl.program_id(0) * tiles)
     copies = []
     lane = lax.broadcasted_iota(jnp.int32, (per_dest, width), 1)
     row = lax.broadcasted_iota(jnp.int32, (per_dest, width), 0)
@@ -286,7 +289,7 @@
         copies.append(
             pltpu.make_async_copy(
                 out_ref.at[ready],
-                out_hbm.at[pl.ds(first_dest + tile * dests, dests)],
+                out_hbm.at[pl.ds(lax.rem(first_place + tile, places) * dests, dests)],
                 sems.at[tile],
             )
         )
@@ -295,7 +298,9 @@
         copy.wait()
 
 
-def prefix_partials(rows_q, keys, values, far_keys, far_values, after, per_dest, score_scale):
+def prefix_partials(
+    rows_q, keys, values, far_keys, far_values, after, per_dest, turn, score_scale
+):
     rows, width = rows_q.shape
     length = keys.shape[0]
     step_rows = min(STEP_ROWS, rows)
@@ -308,7 +313,9 @@
         blocked["in_specs"] += [pl.BlockSpec((length, width), lambda i: (0, 0))] * 4
     blocked["in_specs"] += [pl.BlockSpec(memory_space=pl.ANY)]
     return pl.pallas_call(
-        functools.partial(prefix_kernel, per_dest=per_dest, score_scale=score_scale),
+        functools.partial(
+            prefix_kernel, per_dest=per_dest, turn=turn, score_scale=score_scale
+        ),
         **blocked,
         out_specs=IN_HBM,
         out_shape=pltpu.HBM((rows // per_dest, out_rows, width), jnp.int32),
@@ -341,14 +348,15 @@
         return jnp.sum(jnp.where(diagonal, line, 0.0), axis=1, keepdims=True)
 
     lines = [jnp.zeros((1, width), jnp.float32) for _ in range(count)]
-    for g in range(kv_count):
+    for place in range(kv_count):
+        g = kv_count - 1 - place
         heads_of = slice(g * group, (g + 1) * group)
         suf_mixed = jnp.concatenate([suf_ref[r, heads_of] for r in range(count)], axis=0)
         suf_log = jnp.concatenate([suf_log_ref[r, heads_of] for r in range(count)], axis=0)
         logs, scales = [], []
         top = suf_log
         for s in range(parts):
-            tail = got_ref[s * kv_count + g, half:].astype(jnp.float32)
+            tail = got_ref[s * kv_count + place, half:].astype(jnp.float32)
             log_line = tail[0:1] * jnp.exp2(tail[1:2] - LOG_BITS)
             logs.append(jnp.broadcast_to(column(log_line), (per_dest, width)))
             scales.append(column(jnp.exp2(tail[2:3] - VALUE_BITS)))
@@ -357,7 +365,7 @@
         acc = weight * suf_mixed
         total = weight
         for s in range(parts):
-            words = got_ref[s * kv_count + g, :half]
+            words = got_ref[s * kv_count + place, :half]
             coded = jnp.concatenate([words >> 16, (words << 16) >> 16], axis=0)
             weight = jnp.exp(logs[s] - top)
             acc = acc + (weight * scales[s]) * coded.astype(jnp.float32)
@@ -367,8 +375,8 @@
         for r in range(count):
             rows = slice(r * group, (r + 1) * group)
             out_ref[r, heads_of] = acc[rows]
-            place = lane[:group] == row[:group] + g * group
-            lines[r] = lines[r] + jnp.sum(jnp.where(place, logged[rows], 0.0), axis=0, keepdims=True)
+            spot = lane[:group] == row[:group] + g * group
+            lines[r] = lines[r] + jnp.sum(jnp.where(spot, logged[rows], 0.0), axis=0, keepdims=True)
     for r in range(count):
         log_ref[r : r + 1] = lines[r][:, :heads]
 
@@ -388,11 +396,12 @@
     )(got, suf_mixed, suf_log)
 
 
-def exchange(pieces):
+def exchange(pieces, first):
     seq, head, rep = lax.axis_size("seq"), lax.axis_size("head"), lax.axis_size("rep")
-    order = seq_order(seq)
+    order = [(first - s) % seq for s in range(seq)]
     groups = [
-        [(s * head + h) * rep + r for s in order for h in range(head)] for r in range(rep)
+        [(s * head + h) * rep + r for s in order for h in reversed(range(head))]
+        for r in range(rep)
     ]
     return lax.all_to_all(
         pieces,
@@ -402,11 +411,6 @@
         axis_index_groups=groups,
         tiled=True,
     )
-
-
-def seq_order(count):
-    middle = count // 2
-    return [middle] + [s for s in range(count) if s != middle]
 
 
 def per_device(
@@ -419,7 +423,9 @@
     sent, near_keys, near_values = layout_queries(
         queries, kv_count, lax.axis_size("seq"), (prefix_keys[:, 0, :], prefix_values[:, 0, :])
     )
-    got_q = exchange(sent)
+    seq = lax.axis_size("seq")
+    last, middle = seq - 1, seq // 2
+    got_q = exchange(sent, last)
     far_keys = lax.ppermute(near_keys, "rep", [(0, 1), (1, 0)])
     far_values = lax.ppermute(near_values, "rep", [(0, 1), (1, 0)])
     earlier = []
@@ -443,9 +449,10 @@
         far_values,
         earlier[0],
         per_dest,
+        (middle - last) % seq,
         score_scale,
     )
-    got = exchange(partials)
+    got = exchange(partials, middle)
     return join_partials(got, mixed, log, kv_count)
 
 

time: 33.5 us -> 33.9 us (1.012)
  starting transfers between devices: 14.3 us -> 17.6 us
  waiting for transfers between devices: 4.49 us -> 1.59 us
    all_to_all x2, starting transfers between devices: 13.7 us -> 17 us  [exchange(): lax.all_to_all(pieces, ('seq', 'head', 'rep'), split_axis=0, concat_axis=...]
    all_to_all x2, waiting for transfers between devices: 4.49 us -> 1.59 us  [exchange(): lax.all_to_all(pieces, ('seq', 'head', 'rep'), split_axis=0, concat_axis=...]
where the time goes in v4:
time: 33.9 us; the launch traced here: 33.5 us
  starting transfers between devices  17.6 us (52%)
  Pallas kernels  13.6 us (40%)
  waiting for transfers between devices  1.59 us (5%)
  between operations  0.67 us (2%)
    all_to_all x2, starting transfers between devices, exchange(): lax.all_to_all(pieces, ('seq', 'head', 'rep'), split_axis=0, concat_axis=...  17 us
    pallas_call x2, Pallas kernels, suffix_partials(): pl.pallas_call(functools.partial(suffix_kernel, place=place, kv_count=kv_...  7.31 us
    pallas_call x1, Pallas kernels, prefix_partials(): pl.pallas_call(functools.partial(prefix_kernel, per_dest=per_dest, turn=t...  3.68 us
    pallas_call x1, Pallas kernels, layout_queries(): pl.pallas_call(functools.partial(layout_kernel, carried=len(carried)), in...  1.74 us
    all_to_all x2, waiting for transfers between devices, exchange(): lax.all_to_all(pieces, ('seq', 'head', 'rep'), split_axis=0, concat_axis=...  1.59 us
    pallas_call x1, Pallas kernels, join_partials(): pl.pallas_call(functools.partial(join_kernel, kv_count=kv_count), in_spec...  0.86 us
  transfers between devices with their start and end apart: 4, of which 2 were waited for; matrix products, arithmetic and copies ran while one was open for 0% of the time, Pallas kernels for 22%

profile of v4, /device:TPU:0, one launch (start us, length us, event | category | flops | bytes accessed | tf_op | source)
XLA Modules:
  0.0 33.5 jit_solution(16603328999859185612)
XLA Ops:
  0.6 1.7 %layout_queries.1 = (bf16[16,32,128]{2,1,0:T(8,128)(2,1)}, bf16[2048,128]{1,0:T(8,128)(2,1)S(1)}, bf16[2048,128]{1,0:T(8,128)(2,1)S(1)}) custom-call(bf16[2,64,128]{2,1,0:T(8,128)(2,1)} %refs_2_.3, bf16[2048,128]{1,0:T(8,128)(2,1)} %bitcast.10, bf16[2048,128]{1,0:T(8,128)(2,1)} %bitcast.11), custom_call_target="tpu_custom_call" | custom-call | tf_op jit(solution)/shard_map/layout_queries/pallas_call | solution.py:72
  2.4 0.5 %collective-permute-start = (bf16[2048,128]{1,0:T(8,128)(2,1)S(1)}, bf16[2048,128]{1,0:T(8,128)(2,1)S(1)}, u32[]{:S(2)}, u32[]{:S(2)}) collective-permute-start(bf16[2048,128]{1,0:T(8,128)(2,1)S(1)} %get-tuple-element.10.k0_ref), channel_id=1, source_target_pairs={{0,1},{1,0},{2,3},{3,2},{4,5},{5,4},{6,7},{7,6},{8,9},{9,8},{10,11... | collective-permute-start | bytes 1572872 | tf_op jit(solution)/shard_map/ppermute | solution.py:429
  2.9 0.1 collective-permute-start.1
  3.0 10.3 %all-to-all-start = ((bf16[16,32,128]{2,1,0:T(8,128)(2,1)}), bf16[16,32,128]{2,1,0:T(8,128)(2,1)S(1)}, u32[]{:S(2)}, u32[]{:S(2)}) async-start(bf16[16,32,128]{2,1,0:T(8,128)(2,1)} %get-tuple-element.9), calls=%async_computation | async-start | bytes 262144 | tf_op jit(solution)/shard_map/all_to_all | solution.py:406
  13.3 3.7 %suffix_attention_0.1 = (f32[64,128]{1,0:T(8,128)S(1)}, f32[64,128]{1,0:T(8,128)S(1)}) custom-call(s32[2]{0:T(128)} %refs_0_.5, s32[2]{0:T(128)} %refs_1_.3, bf16[2,64,128]{2,1,0:T(8,128)(2,1)} %refs_2_.3, bf16[2,8192,128]{2,1,0:T(8,128)(2,1)} %bitcast.6, bf16[2,8192,128]{2,1,0:T(8,128)(2,1)} %bitcast.8), custom_call_target="tpu_custom_call" | custom-call | flops 268435456 | bytes 67108864 | tf_op jit(solution)/shard_map/suffix_attention_0/pallas_call | solution.py:184
  17.0 0.5 %all-to-all-done = bf16[16,32,128]{2,1,0:T(8,128)(2,1)S(1)} async-done(((bf16[16,32,128]{2,1,0:T(8,128)(2,1)}), bf16[16,32,128]{2,1,0:T(8,128)(2,1)S(1)}, u32[]{:S(2)}, u32[]{:S(2)}) %all-to-all-start) | async-done | bytes 131104 | tf_op jit(solution)/shard_map/all_to_all | solution.py:406
  17.4 0.0 collective-permute-done.k1_ref
  17.4 0.0 collective-permute-done.1.v1_ref
  17.4 3.7 %prefix_attention.1 = s32[16,24,128]{2,1,0:T(8,128)} custom-call(bf16[512,128]{1,0:T(8,128)(2,1)S(1)} %bitcast.5, bf16[2048,128]{1,0:T(8,128)(2,1)S(1)} %get-tuple-element.10.k0_ref, bf16[2048,128]{1,0:T(8,128)(2,1)S(1)} %get-tuple-element.11.v0_ref, bf16[2048,128]{1,0:T(8,128)(2,1)S(1)} %collective-permute-done.k1_ref, ...), custom_call_target="tpu_custom_call" | custom-call | flops 1073741824 | bytes 2490368 | tf_op jit(solution)/shard_map/prefix_attention/pallas_call | solution.py:315
  21.1 6.7 %all-to-all-start.1 = ((s32[16,24,128]{2,1,0:T(8,128)}), s32[16,24,128]{2,1,0:T(8,128)S(1)}, u32[]{:S(2)}, u32[]{:S(2)}) async-start(s32[16,24,128]{2,1,0:T(8,128)} %prefix_attention.1), calls=%async_computation.1 | async-start | bytes 393216 | tf_op jit(solution)/shard_map/all_to_all | solution.py:406
  27.8 3.6 %suffix_attention_1.1 = (f32[2,64,128]{2,1,0:T(8,128)S(1)}, f32[2,64,128]{2,1,0:T(8,128)S(1)}) custom-call(s32[2]{0:T(128)} %refs_0_.5, s32[2]{0:T(128)} %refs_1_.3, bf16[2,64,128]{2,1,0:T(8,128)(2,1)} %refs_2_.3, bf16[2,8192,128]{2,1,0:T(8,128)(2,1)} %bitcast.7, bf16[2,8192,128]{2,1,0:T(8,128)(2,1)} %bitcast.9, f32[64,128]{1,0:T(8,128)S(1)} %get-tuple-element.12._.refs_5_, ...), custom_call_target="tpu_custom_call" | custom-call | flops 268435456 | bytes 4194304 | tf_op jit(solution)/shard_map/suffix_attention_1/pallas_call | solution.py:184
  31.5 1.1 %all-to-all-done.1.got_ref = s32[16,24,128]{2,1,0:T(8,128)S(1)} async-done(((s32[16,24,128]{2,1,0:T(8,128)}), s32[16,24,128]{2,1,0:T(8,128)S(1)}, u32[]{:S(2)}, u32[]{:S(2)}) %all-to-all-start.1) | async-done | bytes 196640 | tf_op jit(solution)/shard_map/all_to_all | solution.py:406
  32.6 0.9 %join_partials.1 = (f32[2,64,128]{2,1,0:T(8,128)}, f32[2,64]{1,0:T(2,128)}) custom-call(s32[16,24,128]{2,1,0:T(8,128)S(1)} %all-to-all-done.1.got_ref, f32[2,64,128]{2,1,0:T(8,128)S(1)} %get-tuple-element.14.suf_ref, f32[2,64,128]{2,1,0:T(8,128)S(1)} %get-tuple-element.15.suf_log_ref), custom_call_target="tpu_custom_call" | custom-call | tf_op jit(solution)/shard_map/join_partials/pallas_call | solution.py:386
Async XLA Ops:
  2.4 15.0 %collective-permute-start = (bf16[2048,128]{1,0:T(8,128)(2,1)S(1)}, bf16[2048,128]{1,0:T(8,128)(2,1)S(1)}, u32[]{:S(2)}, u32[]{:S(2)}) collective-permute-start(bf16[2048,128]{1,0:T(8,128)(2,1)S(1)} %get-tuple-element.10.k0_ref), channel_id=1, source_target_pairs={{0,1},{1,0},{2,3},{3,2},{4,5},{5,4},{6,7},{7,6},{8,9},{9,8},{10,11... | collective-permute-start | bytes 1572872 | tf_op jit(solution)/shard_map/ppermute | solution.py:429
  2.9 14.5 %collective-permute-start.1 = (bf16[2048,128]{1,0:T(8,128)(2,1)S(1)}, bf16[2048,128]{1,0:T(8,128)(2,1)S(1)}, u32[]{:S(2)}, u32[]{:S(2)}) collective-permute-start(bf16[2048,128]{1,0:T(8,128)(2,1)S(1)} %get-tuple-element.11.v0_ref), channel_id=1, source_target_pairs={{0,1},{1,0},{2,3},{3,2},{4,5},{5,4},{6,7},{7,6},{8,9},{9,8},{10,11... | collective-permute-start | bytes 1572872 | tf_op jit(solution)/shard_map/ppermute | solution.py:430
  3.0 14.4 %all-to-all-start = ((bf16[16,32,128]{2,1,0:T(8,128)(2,1)}), bf16[16,32,128]{2,1,0:T(8,128)(2,1)S(1)}, u32[]{:S(2)}, u32[]{:S(2)}) async-start(bf16[16,32,128]{2,1,0:T(8,128)(2,1)} %get-tuple-element.9), calls=%async_computation | async-start | bytes 262144 | tf_op jit(solution)/shard_map/all_to_all | solution.py:406
  21.1 11.5 %all-to-all-start.1 = ((s32[16,24,128]{2,1,0:T(8,128)}), s32[16,24,128]{2,1,0:T(8,128)S(1)}, u32[]{:S(2)}, u32[]{:S(2)}) async-start(s32[16,24,128]{2,1,0:T(8,128)} %prefix_attention.1), calls=%async_computation.1 | async-start | bytes 393216 | tf_op jit(solution)/shard_map/all_to_all | solution.py:406

commit v5 on v4

--- a/solution.py
+++ b/solution.py
@@ -10,8 +10,8 @@
 
 ROW_TILE = 128
 STEP_ROWS = 512
-SUF_COPIES = 4
-IN_FLIGHT = 4
+SUF_COPIES = 8
+AT_ONCE = 4
 LANES = 128
 LOG_ROWS = 8
 VALUE_BITS = 15
@@ -93,7 +93,7 @@
     last = place == count - 1
     earlier, refs = (refs[: 2 * place], refs[2 * place :]) if last else ((), refs)
     mixed_ref, log_ref = refs[:2]
-    slot_ref, length_ref, q_ref, k_buf, v_buf, score_ref, sems, small_sems = refs[2:]
+    slot_ref, length_ref, q_ref, k_buf, v_buf, score_ref, peak_ref, sum_ref, acc_ref, sems, small_sems = refs[2:]
     rows = k_hbm.shape[1]
     copy_rows = rows // SUF_COPIES
     copies = []
@@ -103,20 +103,15 @@
             copies.append(
                 pltpu.make_async_copy(source.at[place, part], target.at[part], sems.at[which, c])
             )
+    k_copies, v_copies = copies[:SUF_COPIES], copies[SUF_COPIES:]
     small = [
         pltpu.make_async_copy(source, target, small_sems.at[i])
         for i, (source, target) in enumerate(
             [(slot_hbm, slot_ref), (length_hbm, length_ref), (q_hbm, q_ref)]
         )
     ]
-    for copy in small + copies[:IN_FLIGHT]:
+    for copy in small + k_copies[:AT_ONCE]:
         copy.start()
-
-    def arrive(i):
-        copies[i].wait()
-        if i + IN_FLIGHT < len(copies):
-            copies[i + IN_FLIGHT].start()
-
     for copy in small:
         copy.wait()
 
@@ -128,33 +123,56 @@
 
     request = request_of(place)
     limit = length_ref[request] * kv_count
+
+    def live(c):
+        return limit > c * copy_rows
+
+    for c in range(AT_ONCE, SUF_COPIES):
+        pl.when(live(c))(k_copies[c].start)
     query = q_ref[request]
     lane = lax.broadcasted_iota(jnp.int32, (heads, LANES), 1)
     group = lax.broadcasted_iota(jnp.int32, (heads, LANES), 0) // (heads // kv_count)
     lane = jnp.where((lane % kv_count) == group, lane, rows)
-    peak = jnp.full((heads, LANES), -1e30, jnp.float32)
+    peak_ref[...] = jnp.full((heads, LANES), -1e30, jnp.float32)
     for c in range(SUF_COPIES):
-        arrive(c)
-        part = lax.dot_general(
-            query, k_buf[c * copy_rows : (c + 1) * copy_rows], NT, preferred_element_type=jnp.float32
-        )
-        for begin in range(0, copy_rows, LANES):
-            at = c * copy_rows + begin
-            tile = jnp.where(lane < limit - at, part[:, begin : begin + LANES], -1e30)
-            score_ref[:, at : at + LANES] = tile
-            peak = jnp.maximum(peak, tile)
-    row_max = jnp.max(peak, axis=1, keepdims=True)
-    sums = jnp.zeros((heads, LANES), jnp.float32)
-    acc = jnp.zeros((heads, width), jnp.float32)
+        if c < AT_ONCE:
+            k_copies[c].wait()
+
+        @pl.when(live(c))
+        def _(c=c):
+            if c >= AT_ONCE:
+                k_copies[c].wait()
+            v_copies[c].start()
+            part = lax.dot_general(
+                query, k_buf[c * copy_rows : (c + 1) * copy_rows], NT, preferred_element_type=jnp.float32
+            )
+            peak = peak_ref[...]
+            for begin in range(0, copy_rows, LANES):
+                at = c * copy_rows + begin
+                tile = jnp.where(lane < limit - at, part[:, begin : begin + LANES], -1e30)
+                score_ref[:, at : at + LANES] = tile
+                peak = jnp.maximum(peak, tile)
+            peak_ref[...] = peak
+
+    row_max = jnp.max(peak_ref[...], axis=1, keepdims=True)
+    sum_ref[...] = jnp.zeros((heads, LANES), jnp.float32)
+    acc_ref[...] = jnp.zeros((heads, width), jnp.float32)
     for c in range(SUF_COPIES):
-        arrive(SUF_COPIES + c)
-        part = slice(c * copy_rows, (c + 1) * copy_rows)
-        terms = jnp.exp2((score_ref[:, part] - row_max) * (score_scale * LOG2E))
-        for begin in range(0, copy_rows, LANES):
-            sums = sums + terms[:, begin : begin + LANES]
-        acc = acc + jnp.dot(
-            terms.astype(jnp.bfloat16), v_buf[part], preferred_element_type=jnp.float32
-        )
+
+        @pl.when(live(c))
+        def _(c=c):
+            v_copies[c].wait()
+            part = slice(c * copy_rows, (c + 1) * copy_rows)
+            terms = jnp.exp2((score_ref[:, part] - row_max) * (score_scale * LOG2E))
+            sums = sum_ref[...]
+            for begin in range(0, copy_rows, LANES):
+                sums = sums + terms[:, begin : begin + LANES]
+            sum_ref[...] = sums
+            acc_ref[...] += jnp.dot(
+                terms.astype(jnp.bfloat16), v_buf[part], preferred_element_type=jnp.float32
+            )
+
+    sums, acc = sum_ref[...], acc_ref[...]
     total = jnp.sum(sums, axis=1, keepdims=True)
     mixed = acc / total
     log = jnp.broadcast_to(row_max * score_scale + jnp.log(total), (heads, width))
@@ -198,13 +216,16 @@
             pltpu.VMEM((rows, width), keys.dtype),
             pltpu.VMEM((rows, width), values.dtype),
             pltpu.VMEM((heads, rows), jnp.float32),
+            pltpu.VMEM((heads, LANES), jnp.float32),
+            pltpu.VMEM((heads, LANES), jnp.float32),
+            pltpu.VMEM((heads, width), jnp.float32),
             pltpu.SemaphoreType.DMA((2, SUF_COPIES)),
             pltpu.SemaphoreType.DMA((3,)),
         ],
         compiler_params=pltpu.CompilerParams(vmem_limit_bytes=SUFFIX_VMEM),
         cost_estimate=pl.CostEstimate(
             flops=4 * heads * rows * width,
-            bytes_accessed=4 * rows * width * (16 if place == 0 else 1),
+            bytes_accessed=4 * rows * width,
             transcendentals=heads * rows,
         ),
         name=f"suffix_attention_{place}",
@@ -216,15 +237,14 @@
 
 
 def prefix_kernel(
-    q_ref, k0_ref, v0_ref, k1_ref, v1_ref, _, out_hbm, out_ref, score_ref, sems, *, per_dest, turn, score_scale
+    q_ref, k0_ref, v0_ref, k1_ref, v1_ref, _, out_hbm, out_ref, score_ref, sems, *, per_dest, score_scale
 ):
     width = q_ref.shape[1]
     tiles = q_ref.shape[0] // ROW_TILE
     dests = ROW_TILE // per_dest
     keys, values = (k0_ref, k1_ref), (v0_ref, v1_ref)
     units = [(tile, block) for tile in range(tiles) for block in range(2)]
-    places = out_hbm.shape[0] // dests
-    first_place = turn + (0 if out_hbm.shape == out_ref.shape else pl.program_id(0) * tiles)
+    first_dest = 0 if out_hbm.shape == out_ref.shape else pl.program_id(0) * (tiles * dests)
     copies = []
     lane = lax.broadcasted_iota(jnp.int32, (per_dest, width), 1)
     row = lax.broadcasted_iota(jnp.int32, (per_dest, width), 0)
@@ -289,7 +309,7 @@
         copies.append(
             pltpu.make_async_copy(
                 out_ref.at[ready],
-                out_hbm.at[pl.ds(lax.rem(first_place + tile, places) * dests, dests)],
+                out_hbm.at[pl.ds(first_dest + tile * dests, dests)],
                 sems.at[tile],
             )
         )
@@ -299,7 +319,7 @@
 
 
 def prefix_partials(
-    rows_q, keys, values, far_keys, far_values, after, per_dest, turn, score_scale
+    rows_q, keys, values, far_keys, far_values, after, per_dest, score_scale
 ):
     rows, width = rows_q.shape
     length = keys.shape[0]
@@ -314,7 +334,7 @@
     blocked["in_specs"] += [pl.BlockSpec(memory_space=pl.ANY)]
     return pl.pallas_call(
         functools.partial(
-            prefix_kernel, per_dest=per_dest, turn=turn, score_scale=score_scale
+            prefix_kernel, per_dest=per_dest, score_scale=score_scale
         ),
         **blocked,
         out_specs=IN_HBM,
@@ -424,8 +444,8 @@
         queries, kv_count, lax.axis_size("seq"), (prefix_keys[:, 0, :], prefix_values[:, 0, :])
     )
     seq = lax.axis_size("seq")
-    last, middle = seq - 1, seq // 2
-    got_q = exchange(sent, last)
+    middle = seq // 2
+    got_q = exchange(sent, middle)
     far_keys = lax.ppermute(near_keys, "rep", [(0, 1), (1, 0)])
     far_values = lax.ppermute(near_values, "rep", [(0, 1), (1, 0)])
     earlier = []
@@ -449,7 +469,6 @@
         far_values,
         earlier[0],
         per_dest,
-        (middle - last) % seq,
         score_scale,
     )
     got = exchange(partials, middle)

time: 33.9 us -> 32.8 us (0.968)
  starting transfers between devices: 17.6 us -> 16.3 us
    all_to_all x2, starting transfers between devices: 17 us -> 15.7 us  [exchange(): lax.all_to_all(pieces, ('seq', 'head', 'rep'), split_axis=0, concat_axis=...]
  transfers between devices with their start and end apart: 4 -> 4, of which waited for: 2 -> 1; matrix products, arithmetic and copies ran while one was open for 0% -> 0% of each run, Pallas kernels for 22% -> 23%
where the time goes in v5:
time: 32.8 us; the launch traced here: 32.4 us
  starting transfers between devices  16.3 us (50%)
  Pallas kernels  13.7 us (42%)
  waiting for transfers between devices  1.8 us (5%)
  between operations  0.67 us (2%)
    all_to_all x2, starting transfers between devices, exchange(): lax.all_to_all(pieces, ('seq', 'head', 'rep'), split_axis=0, concat_axis=...  15.7 us
    pallas_call x2, Pallas kernels, suffix_partials(): pl.pallas_call(functools.partial(suffix_kernel, place=place, kv_count=kv_...  7.4 us
    pallas_call x1, Pallas kernels, prefix_partials(): pl.pallas_call(functools.partial(prefix_kernel, per_dest=per_dest, score_...  3.68 us
    all_to_all x2, waiting for transfers between devices, exchange(): lax.all_to_all(pieces, ('seq', 'head', 'rep'), split_axis=0, concat_axis=...  1.79 us
    pallas_call x1, Pallas kernels, layout_queries(): pl.pallas_call(functools.partial(layout_kernel, carried=len(carried)), in...  1.74 us
    pallas_call x1, Pallas kernels, join_partials(): pl.pallas_call(functools.partial(join_kernel, kv_count=kv_count), in_spec...  0.86 us
  transfers between devices with their start and end apart: 4, of which 1 were waited for; matrix products, arithmetic and copies ran while one was open for 0% of the time, Pallas kernels for 23%

profile of v5, /device:TPU:0, one launch (start us, length us, event | category | flops | bytes accessed | tf_op | source)
XLA Modules:
  0.0 32.4 jit_solution(4488543517482214277)
XLA Ops:
  0.6 1.7 %layout_queries.1 = (bf16[16,32,128]{2,1,0:T(8,128)(2,1)}, bf16[2048,128]{1,0:T(8,128)(2,1)S(1)}, bf16[2048,128]{1,0:T(8,128)(2,1)S(1)}) custom-call(bf16[2,64,128]{2,1,0:T(8,128)(2,1)} %refs_2_.3, bf16[2048,128]{1,0:T(8,128)(2,1)} %bitcast.10, bf16[2048,128]{1,0:T(8,128)(2,1)} %bitcast.11), custom_call_target="tpu_custom_call" | custom-call | tf_op jit(solution)/shard_map/layout_queries/pallas_call | solution.py:72
  2.4 0.5 %collective-permute-start = (bf16[2048,128]{1,0:T(8,128)(2,1)S(1)}, bf16[2048,128]{1,0:T(8,128)(2,1)S(1)}, u32[]{:S(2)}, u32[]{:S(2)}) collective-permute-start(bf16[2048,128]{1,0:T(8,128)(2,1)S(1)} %get-tuple-element.10.k0_ref), channel_id=1, source_target_pairs={{0,1},{1,0},{2,3},{3,2},{4,5},{5,4},{6,7},{7,6},{8,9},{9,8},{10,11... | collective-permute-start | bytes 1572872 | tf_op jit(solution)/shard_map/ppermute | solution.py:449
  2.9 0.1 collective-permute-start.1
  3.0 9.3 %all-to-all-start = ((bf16[16,32,128]{2,1,0:T(8,128)(2,1)}), bf16[16,32,128]{2,1,0:T(8,128)(2,1)S(1)}, u32[]{:S(2)}, u32[]{:S(2)}) async-start(bf16[16,32,128]{2,1,0:T(8,128)(2,1)} %get-tuple-element.9), calls=%async_computation | async-start | bytes 262144 | tf_op jit(solution)/shard_map/all_to_all | solution.py:426
  12.2 2.7 %suffix_attention_0.1 = (f32[64,128]{1,0:T(8,128)S(1)}, f32[64,128]{1,0:T(8,128)S(1)}) custom-call(s32[2]{0:T(128)} %refs_0_.5, s32[2]{0:T(128)} %refs_1_.3, bf16[2,64,128]{2,1,0:T(8,128)(2,1)} %refs_2_.3, bf16[2,8192,128]{2,1,0:T(8,128)(2,1)} %bitcast.6, bf16[2,8192,128]{2,1,0:T(8,128)(2,1)} %bitcast.8), custom_call_target="tpu_custom_call" | custom-call | flops 268435456 | bytes 4194304 | tf_op jit(solution)/shard_map/suffix_attention_0/pallas_call | solution.py:202
  14.9 1.8 %all-to-all-done = bf16[16,32,128]{2,1,0:T(8,128)(2,1)S(1)} async-done(((bf16[16,32,128]{2,1,0:T(8,128)(2,1)}), bf16[16,32,128]{2,1,0:T(8,128)(2,1)S(1)}, u32[]{:S(2)}, u32[]{:S(2)}) %all-to-all-start) | async-done | bytes 131104 | tf_op jit(solution)/shard_map/all_to_all | solution.py:426
  16.7 0.0 collective-permute-done.k1_ref
  16.7 0.0 collective-permute-done.1.v1_ref
  16.7 3.7 %prefix_attention.1 = s32[16,24,128]{2,1,0:T(8,128)} custom-call(bf16[512,128]{1,0:T(8,128)(2,1)S(1)} %bitcast.5, bf16[2048,128]{1,0:T(8,128)(2,1)S(1)} %get-tuple-element.10.k0_ref, bf16[2048,128]{1,0:T(8,128)(2,1)S(1)} %get-tuple-element.11.v0_ref, bf16[2048,128]{1,0:T(8,128)(2,1)S(1)} %collective-permute-done.k1_ref, ...), custom_call_target="tpu_custom_call" | custom-call | flops 1073741824 | bytes 2490368 | tf_op jit(solution)/shard_map/prefix_attention/pallas_call | solution.py:335
  20.4 6.4 %all-to-all-start.1 = ((s32[16,24,128]{2,1,0:T(8,128)}), s32[16,24,128]{2,1,0:T(8,128)S(1)}, u32[]{:S(2)}, u32[]{:S(2)}) async-start(s32[16,24,128]{2,1,0:T(8,128)} %prefix_attention.1), calls=%async_computation.1 | async-start | bytes 393216 | tf_op jit(solution)/shard_map/all_to_all | solution.py:426
  26.8 4.7 %suffix_attention_1.1 = (f32[2,64,128]{2,1,0:T(8,128)S(1)}, f32[2,64,128]{2,1,0:T(8,128)S(1)}) custom-call(s32[2]{0:T(128)} %refs_0_.5, s32[2]{0:T(128)} %refs_1_.3, bf16[2,64,128]{2,1,0:T(8,128)(2,1)} %refs_2_.3, bf16[2,8192,128]{2,1,0:T(8,128)(2,1)} %bitcast.7, bf16[2,8192,128]{2,1,0:T(8,128)(2,1)} %bitcast.9, f32[64,128]{1,0:T(8,128)S(1)} %get-tuple-element.12._.refs_5_, ...), custom_call_target="tpu_custom_call" | custom-call | flops 268435456 | bytes 4194304 | tf_op jit(solution)/shard_map/suffix_attention_1/pallas_call | solution.py:202
  31.5 0.0 all-to-all-done.1.got_ref
  31.6 0.9 %join_partials.1 = (f32[2,64,128]{2,1,0:T(8,128)}, f32[2,64]{1,0:T(2,128)}) custom-call(s32[16,24,128]{2,1,0:T(8,128)S(1)} %all-to-all-done.1.got_ref, f32[2,64,128]{2,1,0:T(8,128)S(1)} %get-tuple-element.14.suf_ref, f32[2,64,128]{2,1,0:T(8,128)S(1)} %get-tuple-element.15.suf_log_ref), custom_call_target="tpu_custom_call" | custom-call | tf_op jit(solution)/shard_map/join_partials/pallas_call | solution.py:406
Async XLA Ops:
  2.4 14.3 %collective-permute-start = (bf16[2048,128]{1,0:T(8,128)(2,1)S(1)}, bf16[2048,128]{1,0:T(8,128)(2,1)S(1)}, u32[]{:S(2)}, u32[]{:S(2)}) collective-permute-start(bf16[2048,128]{1,0:T(8,128)(2,1)S(1)} %get-tuple-element.10.k0_ref), channel_id=1, source_target_pairs={{0,1},{1,0},{2,3},{3,2},{4,5},{5,4},{6,7},{7,6},{8,9},{9,8},{10,11... | collective-permute-start | bytes 1572872 | tf_op jit(solution)/shard_map/ppermute | solution.py:449
  2.9 13.8 %collective-permute-start.1 = (bf16[2048,128]{1,0:T(8,128)(2,1)S(1)}, bf16[2048,128]{1,0:T(8,128)(2,1)S(1)}, u32[]{:S(2)}, u32[]{:S(2)}) collective-permute-start(bf16[2048,128]{1,0:T(8,128)(2,1)S(1)} %get-tuple-element.11.v0_ref), channel_id=1, source_target_pairs={{0,1},{1,0},{2,3},{3,2},{4,5},{5,4},{6,7},{7,6},{8,9},{9,8},{10,11... | collective-permute-start | bytes 1572872 | tf_op jit(solution)/shard_map/ppermute | solution.py:450
  3.0 13.7 %all-to-all-start = ((bf16[16,32,128]{2,1,0:T(8,128)(2,1)}), bf16[16,32,128]{2,1,0:T(8,128)(2,1)S(1)}, u32[]{:S(2)}, u32[]{:S(2)}) async-start(bf16[16,32,128]{2,1,0:T(8,128)(2,1)} %get-tuple-element.9), calls=%async_computation | async-start | bytes 262144 | tf_op jit(solution)/shard_map/all_to_all | solution.py:426
  20.4 11.2 %all-to-all-start.1 = ((s32[16,24,128]{2,1,0:T(8,128)}), s32[16,24,128]{2,1,0:T(8,128)S(1)}, u32[]{:S(2)}, u32[]{:S(2)}) async-start(s32[16,24,128]{2,1,0:T(8,128)} %prefix_attention.1), calls=%async_computation.1 | async-start | bytes 393216 | tf_op jit(solution)/shard_map/all_to_all | solution.py:426

commit v6 on v5

--- a/solution.py
+++ b/solution.py
@@ -10,8 +10,9 @@
 
 ROW_TILE = 128
 STEP_ROWS = 512
-SUF_COPIES = 8
-AT_ONCE = 4
+SUF_COPIES = 4
+AT_ONCE = 2
+BRING_PARTS = 2
 LANES = 128
 LOG_ROWS = 8
 VALUE_BITS = 15
@@ -31,10 +32,7 @@
     return pltpu.with_memory_space_constraint(array, pltpu.HBM)
 
 
-def layout_kernel(*refs, carried):
-    q_hbm, carried_refs, refs = refs[0], refs[1 : 1 + carried], refs[1 + carried :]
-    sent_hbm, brought_refs = refs[0], refs[1 : 1 + carried]
-    buf, in_sems, out_sems, carry_sems = refs[1 + carried :]
+def layout_kernel(q_hbm, sent_hbm, buf, in_sems, out_sems):
     groups, rows, _ = buf.shape
     count = q_hbm.shape[0]
     group = rows // count
@@ -48,12 +46,8 @@
         for g in range(groups)
         for r in range(count)
     ]
-    carries = [
-        pltpu.make_async_copy(source, target, carry_sems.at[i])
-        for i, (source, target) in enumerate(zip(carried_refs, brought_refs))
-    ]
-    for copy in reads + carries:
-        copy.start()
+    for read in reads:
+        read.start()
     for read in reads:
         read.wait()
     writes = [
@@ -62,28 +56,55 @@
     ]
     for write in writes:
         write.start()
-    for copy in writes + carries:
-        copy.wait()
-
-
-def layout_queries(queries, groups, repeats, carried):
+    for write in writes:
+        write.wait()
+
+
+def layout_queries(queries, groups, repeats):
     count, heads, width = queries.shape
     rows = count * heads // groups
     return pl.pallas_call(
-        functools.partial(layout_kernel, carried=len(carried)),
-        in_specs=[IN_HBM] * (1 + len(carried)),
-        out_specs=[IN_HBM] + [IN_VMEM] * len(carried),
-        out_shape=[pltpu.HBM((repeats * groups, rows, width), queries.dtype)]
-        + [pltpu.VMEM(array.shape, array.dtype) for array in carried],
+        layout_kernel,
+        in_specs=[IN_HBM],
+        out_specs=IN_HBM,
+        out_shape=pltpu.HBM((repeats * groups, rows, width), queries.dtype),
         scratch_shapes=[
             pltpu.VMEM((groups, rows, width), queries.dtype),
             pltpu.SemaphoreType.DMA((groups, count)),
             pltpu.SemaphoreType.DMA((repeats,)),
-            pltpu.SemaphoreType.DMA((len(carried),)),
         ],
         compiler_params=pltpu.CompilerParams(vmem_limit_bytes=SMALL_VMEM),
         name="layout_queries",
-    )(in_hbm(queries), *map(in_hbm, carried))
+    )(in_hbm(queries))
+
+
+def bring_kernel(*refs):
+    sources, targets, sems = refs[: len(refs) // 2], refs[len(refs) // 2 : -1], refs[-1]
+    parts = sems.shape[1]
+    copies = []
+    for i, (source, target) in enumerate(zip(sources, targets)):
+        rows = source.shape[0] // parts
+        for c in range(parts):
+            part = pl.ds(c * rows, rows)
+            copies.append(pltpu.make_async_copy(source.at[part], target.at[part], sems.at[i, c]))
+            copies[-1].start()
+    for copy in copies:
+        copy.wait()
+
+
+def bring(*arrays):
+    return pl.pallas_call(
+        bring_kernel,
+        in_specs=[IN_HBM] * len(arrays),
+        out_specs=[IN_VMEM] * len(arrays),
+        out_shape=[pltpu.VMEM(array.shape, array.dtype) for array in arrays],
+        scratch_shapes=[pltpu.SemaphoreType.DMA((len(arrays), BRING_PARTS))],
+        compiler_params=pltpu.CompilerParams(vmem_limit_bytes=SMALL_VMEM),
+        cost_estimate=pl.CostEstimate(
+            flops=0, bytes_accessed=sum(2 * 2 * array.size for array in arrays), transcendentals=0
+        ),
+        name="bring_prefix",
+    )(*map(in_hbm, arrays))
 
 
 def suffix_kernel(*refs, place, kv_count, score_scale):
@@ -440,12 +461,11 @@
     kv_count = suffix_keys.shape[2]
     per_dest = count * heads // kv_count
     score_scale = 1.0 / math.sqrt(width)
-    sent, near_keys, near_values = layout_queries(
-        queries, kv_count, lax.axis_size("seq"), (prefix_keys[:, 0, :], prefix_values[:, 0, :])
-    )
+    sent = layout_queries(queries, kv_count, lax.axis_size("seq"))
     seq = lax.axis_size("seq")
     middle = seq // 2
     got_q = exchange(sent, middle)
+    near_keys, near_values = bring(prefix_keys[:, 0, :], prefix_values[:, 0, :])
     far_keys = lax.ppermute(near_keys, "rep", [(0, 1), (1, 0)])
     far_values = lax.ppermute(near_values, "rep", [(0, 1), (1, 0)])
     earlier = []

time: 32.8 us -> 33.9 us (1.034)
  waiting for transfers between devices: 1.8 us -> 2.43 us
  Pallas kernels: 13.7 us -> 14.1 us
    pallas_call x1 -> x2, Pallas kernels: 1.74 us -> 2.78 us  [the longest x1 1.55 us: layout_queries(): pl.pallas_call(layout_kernel, in_specs=[IN_HBM], out_specs=IN_HBM, out_sh...]
    pallas_call x2, Pallas kernels: 7.4 us -> 6.77 us  [suffix_partials(): pl.pallas_call(functools.partial(suffix_kernel, place=place, kv_count=kv_...]
    all_to_all x2, waiting for transfers between devices: 1.79 us -> 2.42 us  [exchange(): lax.all_to_all(pieces, ('seq', 'head', 'rep'), split_axis=0, concat_axis=...]
  transfers between devices with their start and end apart: 4 -> 4, of which waited for: 1 -> 2; matrix products, arithmetic and copies ran while one was open for 0% -> 0% of each run, Pallas kernels for 23% -> 25%
where the time goes in v6:
time: 33.9 us; the launch traced here: 33.5 us
  starting transfers between devices  16.3 us (48%)
  Pallas kernels  14.1 us (42%)
  waiting for transfers between devices  2.43 us (7%)
  between operations  0.67 us (2%)
    all_to_all x2, starting transfers between devices, exchange(): lax.all_to_all(pieces, ('seq', 'head', 'rep'), split_axis=0, concat_axis=...  15.7 us
    pallas_call x2, Pallas kernels, suffix_partials(): pl.pallas_call(functools.partial(suffix_kernel, place=place, kv_count=kv_...  6.77 us
    pallas_call x1, Pallas kernels, prefix_partials(): pl.pallas_call(functools.partial(prefix_kernel, per_dest=per_dest, score_...  3.68 us
    all_to_all x2, waiting for transfers between devices, exchange(): lax.all_to_all(pieces, ('seq', 'head', 'rep'), split_axis=0, concat_axis=...  2.42 us
    pallas_call x1, Pallas kernels, layout_queries(): pl.pallas_call(layout_kernel, in_specs=[IN_HBM], out_specs=IN_HBM, out_sh...  1.55 us
    pallas_call x1, Pallas kernels, bring(): pl.pallas_call(bring_kernel, in_specs=[IN_HBM] * len(arrays), out_specs=[...  1.22 us
    pallas_call x1, Pallas kernels, join_partials(): pl.pallas_call(functools.partial(join_kernel, kv_count=kv_count), in_spec...  0.86 us
  transfers between devices with their start and end apart: 4, of which 2 were waited for; matrix products, arithmetic and copies ran while one was open for 0% of the time, Pallas kernels for 25%

profile of v6, /device:TPU:0, one launch (start us, length us, event | category | flops | bytes accessed | tf_op | source)
XLA Modules:
  0.0 33.5 jit_solution(13434103078867608321)
XLA Ops:
  0.6 1.2 %bring_prefix.1 = (bf16[2048,128]{1,0:T(8,128)(2,1)S(1)}, bf16[2048,128]{1,0:T(8,128)(2,1)S(1)}) custom-call(bf16[2048,128]{1,0:T(8,128)(2,1)} %bitcast.10, bf16[2048,128]{1,0:T(8,128)(2,1)} %bitcast.11), custom_call_target="tpu_custom_call" | custom-call | bytes 2097152 | tf_op jit(solution)/shard_map/bring_prefix/pallas_call | solution.py:96
  1.9 0.5 %collective-permute-start = (bf16[2048,128]{1,0:T(8,128)(2,1)S(1)}, bf16[2048,128]{1,0:T(8,128)(2,1)S(1)}, u32[]{:S(2)}, u32[]{:S(2)}) collective-permute-start(bf16[2048,128]{1,0:T(8,128)(2,1)S(1)} %get-tuple-element.8.k0_ref), channel_id=1, source_target_pairs={{0,1},{1,0},{2,3},{3,2},{4,5},{5,4},{6,7},{7,6},{8,9},{9,8},{10,11... | collective-permute-start | bytes 1572872 | tf_op jit(solution)/shard_map/ppermute | solution.py:469
  2.4 0.1 collective-permute-start.1
  2.5 1.6 %layout_queries.1 = bf16[16,32,128]{2,1,0:T(8,128)(2,1)} custom-call(bf16[2,64,128]{2,1,0:T(8,128)(2,1)} %refs_2_.3), custom_call_target="tpu_custom_call" | custom-call | tf_op jit(solution)/shard_map/layout_queries/pallas_call | solution.py:66
  4.0 9.3 %all-to-all-start = ((bf16[16,32,128]{2,1,0:T(8,128)(2,1)}), bf16[16,32,128]{2,1,0:T(8,128)(2,1)S(1)}, u32[]{:S(2)}, u32[]{:S(2)}) async-start(bf16[16,32,128]{2,1,0:T(8,128)(2,1)} %layout_queries.1), calls=%async_computation | async-start | bytes 262144 | tf_op jit(solution)/shard_map/all_to_all | solution.py:447
  13.3 2.9 %suffix_attention_0.1 = (f32[64,128]{1,0:T(8,128)S(1)}, f32[64,128]{1,0:T(8,128)S(1)}) custom-call(s32[2]{0:T(128)} %refs_0_.3, s32[2]{0:T(128)} %refs_1_.3, bf16[2,64,128]{2,1,0:T(8,128)(2,1)} %refs_2_.3, bf16[2,8192,128]{2,1,0:T(8,128)(2,1)} %bitcast.6, bf16[2,8192,128]{2,1,0:T(8,128)(2,1)} %bitcast.8), custom_call_target="tpu_custom_call" | custom-call | flops 268435456 | bytes 4194304 | tf_op jit(solution)/shard_map/suffix_attention_0/pallas_call | solution.py:223
  16.2 1.6 %all-to-all-done = bf16[16,32,128]{2,1,0:T(8,128)(2,1)S(1)} async-done(((bf16[16,32,128]{2,1,0:T(8,128)(2,1)}), bf16[16,32,128]{2,1,0:T(8,128)(2,1)S(1)}, u32[]{:S(2)}, u32[]{:S(2)}) %all-to-all-start) | async-done | bytes 131104 | tf_op jit(solution)/shard_map/all_to_all | solution.py:447
  17.7 0.0 collective-permute-done.k1_ref
  17.7 0.0 collective-permute-done.1.v1_ref
  17.7 3.7 %prefix_attention.1 = s32[16,24,128]{2,1,0:T(8,128)} custom-call(bf16[512,128]{1,0:T(8,128)(2,1)S(1)} %bitcast.5, bf16[2048,128]{1,0:T(8,128)(2,1)S(1)} %get-tuple-element.8.k0_ref, bf16[2048,128]{1,0:T(8,128)(2,1)S(1)} %get-tuple-element.9.v0_ref, bf16[2048,128]{1,0:T(8,128)(2,1)S(1)} %collective-permute-done.k1_ref, ...), custom_call_target="tpu_custom_call" | custom-call | flops 1073741824 | bytes 2490368 | tf_op jit(solution)/shard_map/prefix_attention/pallas_call | solution.py:356
  21.4 6.4 %all-to-all-start.1 = ((s32[16,24,128]{2,1,0:T(8,128)}), s32[16,24,128]{2,1,0:T(8,128)S(1)}, u32[]{:S(2)}, u32[]{:S(2)}) async-start(s32[16,24,128]{2,1,0:T(8,128)} %prefix_attention.1), calls=%async_computation.1 | async-start | bytes 393216 | tf_op jit(solution)/shard_map/all_to_all | solution.py:447
  27.9 3.9 %suffix_attention_1.1 = (f32[2,64,128]{2,1,0:T(8,128)S(1)}, f32[2,64,128]{2,1,0:T(8,128)S(1)}) custom-call(s32[2]{0:T(128)} %refs_0_.3, s32[2]{0:T(128)} %refs_1_.3, bf16[2,64,128]{2,1,0:T(8,128)(2,1)} %refs_2_.3, bf16[2,8192,128]{2,1,0:T(8,128)(2,1)} %bitcast.7, bf16[2,8192,128]{2,1,0:T(8,128)(2,1)} %bitcast.9, f32[64,128]{1,0:T(8,128)S(1)} %get-tuple-element.10._.refs_5_, ...), custom_call_target="tpu_custom_call" | custom-call | flops 268435456 | bytes 4194304 | tf_op jit(solution)/shard_map/suffix_attention_1/pallas_call | solution.py:223
  31.8 0.9 %all-to-all-done.1.got_ref = s32[16,24,128]{2,1,0:T(8,128)S(1)} async-done(((s32[16,24,128]{2,1,0:T(8,128)}), s32[16,24,128]{2,1,0:T(8,128)S(1)}, u32[]{:S(2)}, u32[]{:S(2)}) %all-to-all-start.1) | async-done | bytes 196640 | tf_op jit(solution)/shard_map/all_to_all | solution.py:447
  32.6 0.9 %join_partials.1 = (f32[2,64,128]{2,1,0:T(8,128)}, f32[2,64]{1,0:T(2,128)}) custom-call(s32[16,24,128]{2,1,0:T(8,128)S(1)} %all-to-all-done.1.got_ref, f32[2,64,128]{2,1,0:T(8,128)S(1)} %get-tuple-element.12.suf_ref, f32[2,64,128]{2,1,0:T(8,128)S(1)} %get-tuple-element.13.suf_log_ref), custom_call_target="tpu_custom_call" | custom-call | tf_op jit(solution)/shard_map/join_partials/pallas_call | solution.py:427
Async XLA Ops:
  1.9 15.9 %collective-permute-start = (bf16[2048,128]{1,0:T(8,128)(2,1)S(1)}, bf16[2048,128]{1,0:T(8,128)(2,1)S(1)}, u32[]{:S(2)}, u32[]{:S(2)}) collective-permute-start(bf16[2048,128]{1,0:T(8,128)(2,1)S(1)} %get-tuple-element.8.k0_ref), channel_id=1, source_target_pairs={{0,1},{1,0},{2,3},{3,2},{4,5},{5,4},{6,7},{7,6},{8,9},{9,8},{10,11... | collective-permute-start | bytes 1572872 | tf_op jit(solution)/shard_map/ppermute | solution.py:469
  2.4 15.3 %collective-permute-start.1 = (bf16[2048,128]{1,0:T(8,128)(2,1)S(1)}, bf16[2048,128]{1,0:T(8,128)(2,1)S(1)}, u32[]{:S(2)}, u32[]{:S(2)}) collective-permute-start(bf16[2048,128]{1,0:T(8,128)(2,1)S(1)} %get-tuple-element.9.v0_ref), channel_id=1, source_target_pairs={{0,1},{1,0},{2,3},{3,2},{4,5},{5,4},{6,7},{7,6},{8,9},{9,8},{10,11... | collective-permute-start | bytes 1572872 | tf_op jit(solution)/shard_map/ppermute | solution.py:470
  4.0 13.7 %all-to-all-start = ((bf16[16,32,128]{2,1,0:T(8,128)(2,1)}), bf16[16,32,128]{2,1,0:T(8,128)(2,1)S(1)}, u32[]{:S(2)}, u32[]{:S(2)}) async-start(bf16[16,32,128]{2,1,0:T(8,128)(2,1)} %layout_queries.1), calls=%async_computation | async-start | bytes 262144 | tf_op jit(solution)/shard_map/all_to_all | solution.py:447
  21.4 11.2 %all-to-all-start.1 = ((s32[16,24,128]{2,1,0:T(8,128)}), s32[16,24,128]{2,1,0:T(8,128)S(1)}, u32[]{:S(2)}, u32[]{:S(2)}) async-start(s32[16,24,128]{2,1,0:T(8,128)} %prefix_attention.1), calls=%async_computation.1 | async-start | bytes 393216 | tf_op jit(solution)/shard_map/all_to_all | solution.py:447

commit v7 on v6

--- a/solution.py
+++ b/solution.py
@@ -12,9 +12,9 @@
 STEP_ROWS = 512
 SUF_COPIES = 4
 AT_ONCE = 2
-BRING_PARTS = 2
 LANES = 128
-LOG_ROWS = 8
+PIECE = 256
+TILE_ROWS = 2
 VALUE_BITS = 15
 LOG_BITS = 30
 LOG2E = math.log2(math.e)
@@ -33,18 +33,11 @@
 
 
 def layout_kernel(q_hbm, sent_hbm, buf, in_sems, out_sems):
-    groups, rows, _ = buf.shape
-    count = q_hbm.shape[0]
-    group = rows // count
+    groups = buf.shape[0]
     repeats = sent_hbm.shape[0] // groups
     reads = [
-        pltpu.make_async_copy(
-            q_hbm.at[r, pl.ds(g * group, group)],
-            buf.at[groups - 1 - g, pl.ds(r * group, group)],
-            in_sems.at[g, r],
-        )
+        pltpu.make_async_copy(q_hbm.at[:, g], buf.at[groups - 1 - g], in_sems.at[g])
         for g in range(groups)
-        for r in range(count)
     ]
     for read in reads:
         read.start()
@@ -62,59 +55,44 @@
 
 def layout_queries(queries, groups, repeats):
     count, heads, width = queries.shape
-    rows = count * heads // groups
+    group = heads // groups
     return pl.pallas_call(
         layout_kernel,
         in_specs=[IN_HBM],
         out_specs=IN_HBM,
-        out_shape=pltpu.HBM((repeats * groups, rows, width), queries.dtype),
+        out_shape=pltpu.HBM((repeats * groups, count, group, width), queries.dtype),
         scratch_shapes=[
-            pltpu.VMEM((groups, rows, width), queries.dtype),
-            pltpu.SemaphoreType.DMA((groups, count)),
+            pltpu.VMEM((groups, count, group, width), queries.dtype),
+            pltpu.SemaphoreType.DMA((groups,)),
             pltpu.SemaphoreType.DMA((repeats,)),
         ],
         compiler_params=pltpu.CompilerParams(vmem_limit_bytes=SMALL_VMEM),
         name="layout_queries",
-    )(in_hbm(queries))
-
-
-def bring_kernel(*refs):
-    sources, targets, sems = refs[: len(refs) // 2], refs[len(refs) // 2 : -1], refs[-1]
-    parts = sems.shape[1]
-    copies = []
-    for i, (source, target) in enumerate(zip(sources, targets)):
-        rows = source.shape[0] // parts
-        for c in range(parts):
-            part = pl.ds(c * rows, rows)
-            copies.append(pltpu.make_async_copy(source.at[part], target.at[part], sems.at[i, c]))
-            copies[-1].start()
-    for copy in copies:
-        copy.wait()
-
-
-def bring(*arrays):
-    return pl.pallas_call(
-        bring_kernel,
-        in_specs=[IN_HBM] * len(arrays),
-        out_specs=[IN_VMEM] * len(arrays),
-        out_shape=[pltpu.VMEM(array.shape, array.dtype) for array in arrays],
-        scratch_shapes=[pltpu.SemaphoreType.DMA((len(arrays), BRING_PARTS))],
-        compiler_params=pltpu.CompilerParams(vmem_limit_bytes=SMALL_VMEM),
-        cost_estimate=pl.CostEstimate(
-            flops=0, bytes_accessed=sum(2 * 2 * array.size for array in arrays), transcendentals=0
-        ),
-        name="bring_prefix",
-    )(*map(in_hbm, arrays))
-
-
-def suffix_kernel(*refs, place, kv_count, score_scale):
+    )(in_hbm(queries.reshape(count, groups, group, width)))
+
+
+def weigh(scores, weights, part, row_max, factor):
+    sums = jnp.zeros((scores.shape[0], LANES), jnp.float32)
+    for begin in range(part.start, part.stop, PIECE):
+        piece = slice(begin, begin + PIECE)
+        terms = jnp.exp2((scores[:, piece] - row_max) * factor)
+        weights[:, piece] = terms.astype(jnp.bfloat16)
+        for lane in range(0, PIECE, LANES):
+            sums = sums + terms[:, lane : lane + LANES]
+    return sums
+
+
+def suffix_kernel(*refs, place, carried, kv_count, score_scale):
     slot_hbm, length_hbm, q_hbm, k_hbm, v_hbm = refs[:5]
     refs = refs[5:]
     count, heads, width = q_hbm.shape
+    carried_refs, refs = refs[:carried], refs[carried:]
     last = place == count - 1
     earlier, refs = (refs[: 2 * place], refs[2 * place :]) if last else ((), refs)
     mixed_ref, log_ref = refs[:2]
-    slot_ref, length_ref, q_ref, k_buf, v_buf, score_ref, peak_ref, sum_ref, acc_ref, sems, small_sems = refs[2:]
+    brought_refs, refs = refs[2 : 2 + carried], refs[2 + carried :]
+    slot_ref, length_ref, q_ref, k_buf, v_buf, score_ref, weight_ref = refs[:7]
+    peak_ref, sum_ref, acc_ref, sems, small_sems = refs[7:]
     rows = k_hbm.shape[1]
     copy_rows = rows // SUF_COPIES
     copies = []
@@ -129,9 +107,11 @@
         pltpu.make_async_copy(source, target, small_sems.at[i])
         for i, (source, target) in enumerate(
             [(slot_hbm, slot_ref), (length_hbm, length_ref), (q_hbm, q_ref)]
+            + list(zip(carried_refs, brought_refs))
         )
     ]
-    for copy in small + k_copies[:AT_ONCE]:
+    small, carries = small[:3], small[3:]
+    for copy in small + k_copies[:AT_ONCE] + carries:
         copy.start()
     for copy in small:
         copy.wait()
@@ -164,15 +144,15 @@
             if c >= AT_ONCE:
                 k_copies[c].wait()
             v_copies[c].start()
-            part = lax.dot_general(
-                query, k_buf[c * copy_rows : (c + 1) * copy_rows], NT, preferred_element_type=jnp.float32
-            )
             peak = peak_ref[...]
-            for begin in range(0, copy_rows, LANES):
-                at = c * copy_rows + begin
-                tile = jnp.where(lane < limit - at, part[:, begin : begin + LANES], -1e30)
-                score_ref[:, at : at + LANES] = tile
-                peak = jnp.maximum(peak, tile)
+            for at in range(c * copy_rows, (c + 1) * copy_rows, 2 * PIECE):
+                part = lax.dot_general(
+                    query, k_buf[at : at + 2 * PIECE], NT, preferred_element_type=jnp.float32
+                )
+                for begin in range(0, 2 * PIECE, LANES):
+                    tile = jnp.where(lane < limit - (at + begin), part[:, begin : begin + LANES], -1e30)
+                    score_ref[:, at + begin : at + begin + LANES] = tile
+                    peak = jnp.maximum(peak, tile)
             peak_ref[...] = peak
 
     row_max = jnp.max(peak_ref[...], axis=1, keepdims=True)
@@ -184,19 +164,17 @@
         def _(c=c):
             v_copies[c].wait()
             part = slice(c * copy_rows, (c + 1) * copy_rows)
-            terms = jnp.exp2((score_ref[:, part] - row_max) * (score_scale * LOG2E))
-            sums = sum_ref[...]
-            for begin in range(0, copy_rows, LANES):
-                sums = sums + terms[:, begin : begin + LANES]
-            sum_ref[...] = sums
+            sum_ref[...] += weigh(score_ref, weight_ref, part, row_max, score_scale * LOG2E)
             acc_ref[...] += jnp.dot(
-                terms.astype(jnp.bfloat16), v_buf[part], preferred_element_type=jnp.float32
+                weight_ref[:, part], v_buf[part], preferred_element_type=jnp.float32
             )
 
     sums, acc = sum_ref[...], acc_ref[...]
     total = jnp.sum(sums, axis=1, keepdims=True)
     mixed = acc / total
     log = jnp.broadcast_to(row_max * score_scale + jnp.log(total), (heads, width))
+    for carry in carries:
+        carry.wait()
     if not last:
         mixed_ref[...] = mixed
         log_ref[...] = log
@@ -208,7 +186,9 @@
         log_ref[request_of(slot)] = earlier[2 * slot + 1][...]
 
 
-def suffix_partials(place, queries, keys, values, lengths, slots, earlier, score_scale):
+def suffix_partials(
+    place, queries, keys, values, lengths, slots, carried, earlier, score_scale
+):
     count, heads, width = queries.shape
     kv_count = keys.shape[2]
     rows = keys.shape[1] * kv_count
@@ -219,17 +199,20 @@
         queries,
         keys.reshape(count, rows, width),
         values.reshape(count, rows, width),
+        *carried,
     )
     return pl.pallas_call(
         functools.partial(
             suffix_kernel,
             place=place,
+            carried=len(carried),
             kv_count=kv_count,
             score_scale=score_scale,
         ),
         in_specs=[IN_HBM] * len(operands) + [IN_VMEM] * len(earlier),
-        out_specs=[IN_VMEM] * 2,
-        out_shape=[pltpu.VMEM(result, jnp.float32)] * 2,
+        out_specs=[IN_VMEM] * (2 + len(carried)),
+        out_shape=[pltpu.VMEM(result, jnp.float32)] * 2
+        + [pltpu.VMEM(array.shape, array.dtype) for array in carried],
         scratch_shapes=[
             pltpu.SMEM((count,), jnp.int32),
             pltpu.SMEM((count,), jnp.int32),
@@ -237,11 +220,12 @@
             pltpu.VMEM((rows, width), keys.dtype),
             pltpu.VMEM((rows, width), values.dtype),
             pltpu.VMEM((heads, rows), jnp.float32),
+            pltpu.VMEM((heads, rows), jnp.bfloat16),
             pltpu.VMEM((heads, LANES), jnp.float32),
             pltpu.VMEM((heads, LANES), jnp.float32),
             pltpu.VMEM((heads, width), jnp.float32),
             pltpu.SemaphoreType.DMA((2, SUF_COPIES)),
-            pltpu.SemaphoreType.DMA((3,)),
+            pltpu.SemaphoreType.DMA((3 + len(carried),)),
         ],
         compiler_params=pltpu.CompilerParams(vmem_limit_bytes=SUFFIX_VMEM),
         cost_estimate=pl.CostEstimate(
@@ -258,7 +242,7 @@
 
 
 def prefix_kernel(
-    q_ref, k0_ref, v0_ref, k1_ref, v1_ref, _, out_hbm, out_ref, score_ref, sems, *, per_dest, score_scale
+    q_ref, k0_ref, v0_ref, k1_ref, v1_ref, _, out_hbm, out_ref, score_ref, weight_ref, sems, *, per_dest, score_scale
 ):
     width = q_ref.shape[1]
     tiles = q_ref.shape[0] // ROW_TILE
@@ -271,27 +255,34 @@
     row = lax.broadcasted_iota(jnp.int32, (per_dest, width), 0)
     diagonal = lane == row
 
+    length = k0_ref.shape[0]
+
     def score(unit, slot):
         tile, block = unit
-        score_ref[slot] = lax.dot_general(
-            q_ref[tile * ROW_TILE : (tile + 1) * ROW_TILE],
-            keys[block][...],
-            NT,
-            preferred_element_type=jnp.float32,
-        )
-
-    score(units[0], 0)
+        query = q_ref[tile * ROW_TILE : (tile + 1) * ROW_TILE]
+        peak = None
+        for at in range(0, length, PIECE):
+            part = lax.dot_general(
+                query, keys[block][at : at + PIECE], NT, preferred_element_type=jnp.float32
+            )
+            score_ref[slot, :, at : at + PIECE] = part
+            for begin in range(0, PIECE, LANES):
+                lanes = part[:, begin : begin + LANES]
+                peak = lanes if peak is None else jnp.maximum(peak, lanes)
+        return jnp.max(peak, axis=1, keepdims=True)
+
+    later_max = score(units[0], 0)
     held = None
     for step, (tile, block) in enumerate(units):
+        row_max = later_max
         if step + 1 < len(units):
-            score(units[step + 1], (step + 1) % 2)
-        scores = score_ref[step % 2]
-        row_max = jnp.max(scores, axis=1, keepdims=True)
-        terms = jnp.exp2((scores - row_max) * (score_scale * LOG2E))
-        total = jnp.sum(terms, axis=1, keepdims=True)
-        acc = jnp.dot(
-            terms.astype(jnp.bfloat16), values[block][...], preferred_element_type=jnp.float32
+            later_max = score(units[step + 1], (step + 1) % 2)
+        slot = step % 2
+        sums = weigh(
+            score_ref.at[slot], weight_ref.at[slot], slice(0, length), row_max, score_scale * LOG2E
         )
+        total = jnp.sum(sums, axis=1, keepdims=True)
+        acc = jnp.dot(weight_ref[slot], values[block][...], preferred_element_type=jnp.float32)
         if block == 0:
             held = (row_max, total, acc)
             continue
@@ -312,20 +303,16 @@
             rows = slice(k * per_dest, (k + 1) * per_dest)
             dest = tile * dests + k
             high, low = coded[k * per_dest : k * per_dest + half], coded[k * per_dest + half : rows.stop]
-            out_ref[dest, :half] = (high << 16) | (low & 0xFFFF)
+            words = (high << 16) | (low & 0xFFFF)
+            for j in range(half // TILE_ROWS):
+                out_ref[dest, j] = words[j * TILE_ROWS : (j + 1) * TILE_ROWS]
             log_line = jnp.sum(jnp.where(diagonal, logs[rows], 0.0), axis=0, keepdims=True)
             peak_line = jnp.sum(jnp.where(diagonal, peaks[rows], 0.0), axis=0, keepdims=True)
             log_power = exponent(jnp.abs(log_line), LEAST)
-            lines = jnp.concatenate(
-                [
-                    jnp.round(log_line * jnp.exp2(LOG_BITS - log_power)),
-                    log_power,
-                    exponent(peak_line, PEAK_LEAST),
-                    jnp.zeros((LOG_ROWS - 3, width), jnp.float32),
-                ],
-                axis=0,
-            )
-            out_ref[dest, half:] = lines.astype(jnp.int32)
+            mantissa = jnp.round(log_line * jnp.exp2(LOG_BITS - log_power)).astype(jnp.int32)
+            powers = log_power.astype(jnp.int32) << 16
+            powers = powers | (exponent(peak_line, PEAK_LEAST).astype(jnp.int32) & 0xFFFF)
+            out_ref[dest, half // TILE_ROWS] = jnp.concatenate([mantissa, powers], axis=0)
         ready = pl.ds(tile * dests, dests)
         copies.append(
             pltpu.make_async_copy(
@@ -346,7 +333,7 @@
     length = keys.shape[0]
     step_rows = min(STEP_ROWS, rows)
     dests = step_rows // per_dest
-    out_rows = per_dest // 2 + LOG_ROWS
+    out_piece = (per_dest // 2 // TILE_ROWS + 1, TILE_ROWS, width)
     blocked = {"in_specs": [IN_VMEM] * 5}
     if step_rows < rows:
         blocked["grid"] = (rows // step_rows,)
@@ -359,10 +346,11 @@
         ),
         **blocked,
         out_specs=IN_HBM,
-        out_shape=pltpu.HBM((rows // per_dest, out_rows, width), jnp.int32),
+        out_shape=pltpu.HBM((rows // per_dest, *out_piece), jnp.int32),
         scratch_shapes=[
-            pltpu.VMEM((dests, out_rows, width), jnp.int32),
+            pltpu.VMEM((dests, *out_piece), jnp.int32),
             pltpu.VMEM((2, ROW_TILE, length), jnp.float32),
+            pltpu.VMEM((2, ROW_TILE, length), jnp.bfloat16),
             pltpu.SemaphoreType.DMA((step_rows // ROW_TILE,)),
         ],
         compiler_params=pltpu.CompilerParams(vmem_limit_bytes=PREFIX_VMEM),
@@ -397,16 +385,21 @@
         logs, scales = [], []
         top = suf_log
         for s in range(parts):
-            tail = got_ref[s * kv_count + place, half:].astype(jnp.float32)
-            log_line = tail[0:1] * jnp.exp2(tail[1:2] - LOG_BITS)
+            tail = got_ref[s * kv_count + place, half // TILE_ROWS]
+            mantissa, powers = tail[0:1], tail[1:2]
+            log_power = (powers >> 16).astype(jnp.float32)
+            peak_power = ((powers << 16) >> 16).astype(jnp.float32)
+            log_line = mantissa.astype(jnp.float32) * jnp.exp2(log_power - LOG_BITS)
             logs.append(jnp.broadcast_to(column(log_line), (per_dest, width)))
-            scales.append(column(jnp.exp2(tail[2:3] - VALUE_BITS)))
+            scales.append(column(jnp.exp2(peak_power - VALUE_BITS)))
             top = jnp.maximum(top, logs[-1])
         weight = jnp.exp(suf_log - top)
         acc = weight * suf_mixed
         total = weight
         for s in range(parts):
-            words = got_ref[s * kv_count + place, :half]
+            words = jnp.concatenate(
+                [got_ref[s * kv_count + place, j] for j in range(half // TILE_ROWS)], axis=0
+            )
             coded = jnp.concatenate([words >> 16, (words << 16) >> 16], axis=0)
             weight = jnp.exp(logs[s] - top)
             acc = acc + (weight * scales[s]) * coded.astype(jnp.float32)
@@ -465,22 +458,26 @@
     seq = lax.axis_size("seq")
     middle = seq // 2
     got_q = exchange(sent, middle)
-    near_keys, near_values = bring(prefix_keys[:, 0, :], prefix_values[:, 0, :])
-    far_keys = lax.ppermute(near_keys, "rep", [(0, 1), (1, 0)])
-    far_values = lax.ppermute(near_values, "rep", [(0, 1), (1, 0)])
+    keys = prefix_keys[:, 0, :]
+    values = prefix_values[:, 0, :]
+    far_keys = lax.ppermute(keys, "rep", [(0, 1), (1, 0)])
+    far_values = lax.ppermute(values, "rep", [(0, 1), (1, 0)])
     earlier = []
     for place in range(count):
-        mixed, log = suffix_partials(
+        mixed, log, *brought = suffix_partials(
             place,
             queries,
             suffix_keys,
             suffix_values,
             suffix_lengths,
             slot_map,
+            (keys, values) if place == 0 else (),
             earlier if place == count - 1 else (),
             score_scale,
         )
         earlier += [mixed, log]
+        if brought:
+            near_keys, near_values = brought
     partials = prefix_partials(
         got_q.reshape(-1, width),
         near_keys,

time: 33.9 us -> 32.2 us (0.950)
  Pallas kernels: 14.1 us -> 12.4 us
    pallas_call x3 -> x2, Pallas kernels: 8 us -> 6.38 us  [suffix_partials(): pl.pallas_call(functools.partial(suffix_kernel, place=place, carried=len(...]
where the time goes in v7:
time: 32.2 us; the launch traced here: 31.8 us
  starting transfers between devices  16.3 us (51%)
  Pallas kernels  12.4 us (39%)
  waiting for transfers between devices  2.43 us (8%)
  between operations  0.66 us (2%)
    all_to_all x2, starting transfers between devices, exchange(): lax.all_to_all(pieces, ('seq', 'head', 'rep'), split_axis=0, concat_axis=...  15.7 us
    pallas_call x2, Pallas kernels, suffix_partials(): pl.pallas_call(functools.partial(suffix_kernel, place=place, carried=len(...  6.38 us
    pallas_call x1, Pallas kernels, prefix_partials(): pl.pallas_call(functools.partial(prefix_kernel, per_dest=per_dest, score_...  3.66 us
    all_to_all x2, waiting for transfers between devices, exchange(): lax.all_to_all(pieces, ('seq', 'head', 'rep'), split_axis=0, concat_axis=...  2.42 us
    pallas_call x1, Pallas kernels, layout_queries(): pl.pallas_call(layout_kernel, in_specs=[IN_HBM], out_specs=IN_HBM, out_sh...  1.47 us
    pallas_call x1, Pallas kernels, join_partials(): pl.pallas_call(functools.partial(join_kernel, kv_count=kv_count), in_spec...  0.87 us
  transfers between devices with their start and end apart: 4, of which 2 were waited for; matrix products, arithmetic and copies ran while one was open for 0% of the time, Pallas kernels for 25%

profile of v7, /device:TPU:0, one launch (start us, length us, event | category | flops | bytes accessed | tf_op | source)
XLA Modules:
  0.0 31.8 jit_solution(9221133102139181145)
XLA Ops:
  0.6 0.5 %collective-permute-start = (bf16[2048,128]{1,0:T(8,128)(2,1)}, bf16[2048,128]{1,0:T(8,128)(2,1)S(1)}, u32[]{:S(2)}, u32[]{:S(2)}) collective-permute-start(bf16[2048,128]{1,0:T(8,128)(2,1)} %bitcast.11), channel_id=1, source_target_pairs={{0,1},{1,0},{2,3},{3,2},{4,5},{5,4},{6,7},{7,6},{8,9},{9,8},{10,11... | collective-permute-start | bytes 1572872 | tf_op jit(solution)/shard_map/ppermute | solution.py:463
  1.1 0.1 collective-permute-start.1
  1.2 1.5 %layout_queries.1 = bf16[16,2,16,128]{3,2,1,0:T(8,128)(2,1)} custom-call(bf16[2,4,16,128]{3,2,1,0:T(8,128)(2,1)} %bitcast.15), custom_call_target="tpu_custom_call" | custom-call | tf_op jit(solution)/shard_map/layout_queries/pallas_call | solution.py:59
  2.7 9.3 %all-to-all-start = ((bf16[16,2,16,128]{3,2,1,0:T(8,128)(2,1)}), bf16[16,2,16,128]{3,2,1,0:T(8,128)(2,1)S(1)}, u32[]{:S(2)}, u32[]{:S(2)}) async-start(bf16[16,2,16,128]{3,2,1,0:T(8,128)(2,1)} %layout_queries.1), calls=%async_computation | async-start | bytes 262144 | tf_op jit(solution)/shard_map/all_to_all | solution.py:440
  12.0 3.5 %suffix_attention_0.1 = (f32[64,128]{1,0:T(8,128)S(1)}, f32[64,128]{1,0:T(8,128)S(1)}, bf16[2048,128]{1,0:T(8,128)(2,1)S(1)}, bf16[2048,128]{1,0:T(8,128)(2,1)S(1)}) custom-call(s32[2]{0:T(128)} %refs_0_.3, s32[2]{0:T(128)} %refs_1_.3, bf16[2,64,128]{2,1,0:T(8,128)(2,1)} %refs_2_.3, bf16[2,8192,128]{2,1,0:T(8,128)(2,1)} %bitcast.7, ...), custom_call_target="tpu_custom_call" | custom-call | flops 268435456 | bytes 4194304 | tf_op jit(solution)/shard_map/suffix_attention_0/pallas_call | solution.py:204
  15.5 0.9 %all-to-all-done = bf16[16,2,16,128]{3,2,1,0:T(8,128)(2,1)S(1)} async-done(((bf16[16,2,16,128]{3,2,1,0:T(8,128)(2,1)}), bf16[16,2,16,128]{3,2,1,0:T(8,128)(2,1)S(1)}, u32[]{:S(2)}, u32[]{:S(2)}) %all-to-all-start) | async-done | bytes 131104 | tf_op jit(solution)/shard_map/all_to_all | solution.py:440
  16.4 0.0 collective-permute-done.k1_ref
  16.4 0.0 collective-permute-done.1.v1_ref
  16.4 3.7 %prefix_attention.1 = s32[16,9,2,128]{3,2,1,0:T(2,128)} custom-call(bf16[512,128]{1,0:T(8,128)(2,1)S(1)} %bitcast.6, bf16[2048,128]{1,0:T(8,128)(2,1)S(1)} %get-tuple-element.8.k0_ref, bf16[2048,128]{1,0:T(8,128)(2,1)S(1)} %get-tuple-element.9.v0_ref, bf16[2048,128]{1,0:T(8,128)(2,1)S(1)} %collective-permute-done.k1_ref, ...), custom_call_target="tpu_custom_call" | custom-call | flops 1073741824 | bytes 2490368 | tf_op jit(solution)/shard_map/prefix_attention/pallas_call | solution.py:343
  20.1 6.4 %all-to-all-start.1 = ((s32[16,9,2,128]{3,2,1,0:T(2,128)}), s32[16,9,2,128]{3,2,1,0:T(2,128)S(1)}, u32[]{:S(2)}, u32[]{:S(2)}) async-start(s32[16,9,2,128]{3,2,1,0:T(2,128)} %prefix_attention.1), calls=%async_computation.1 | async-start | bytes 294912 | tf_op jit(solution)/shard_map/all_to_all | solution.py:440
  26.5 2.9 %suffix_attention_1.1 = (f32[2,64,128]{2,1,0:T(8,128)S(1)}, f32[2,64,128]{2,1,0:T(8,128)S(1)}) custom-call(s32[2]{0:T(128)} %refs_0_.3, s32[2]{0:T(128)} %refs_1_.3, bf16[2,64,128]{2,1,0:T(8,128)(2,1)} %refs_2_.3, bf16[2,8192,128]{2,1,0:T(8,128)(2,1)} %bitcast.8, bf16[2,8192,128]{2,1,0:T(8,128)(2,1)} %bitcast.10, f32[64,128]{1,0:T(8,128)S(1)} %get-tuple-element.10._.refs_5_, ...), custom_call_target="tpu_custom_call" | custom-call | flops 268435456 | bytes 4194304 | tf_op jit(solution)/shard_map/suffix_attention_1/pallas_call | solution.py:204
  29.4 1.5 %all-to-all-done.1.got_ref = s32[16,9,2,128]{3,2,1,0:T(2,128)S(1)} async-done(((s32[16,9,2,128]{3,2,1,0:T(2,128)}), s32[16,9,2,128]{3,2,1,0:T(2,128)S(1)}, u32[]{:S(2)}, u32[]{:S(2)}) %all-to-all-start.1) | async-done | bytes 147488 | tf_op jit(solution)/shard_map/all_to_all | solution.py:440
  30.9 0.9 %join_partials.1 = (f32[2,64,128]{2,1,0:T(8,128)}, f32[2,64]{1,0:T(2,128)}) custom-call(s32[16,9,2,128]{3,2,1,0:T(2,128)S(1)} %all-to-all-done.1.got_ref, f32[2,64,128]{2,1,0:T(8,128)S(1)} %get-tuple-element.12.suf_ref, f32[2,64,128]{2,1,0:T(8,128)S(1)} %get-tuple-element.13.suf_log_ref), custom_call_target="tpu_custom_call" | custom-call | tf_op jit(solution)/shard_map/join_partials/pallas_call | solution.py:420
Async XLA Ops:
  0.6 15.8 %collective-permute-start = (bf16[2048,128]{1,0:T(8,128)(2,1)}, bf16[2048,128]{1,0:T(8,128)(2,1)S(1)}, u32[]{:S(2)}, u32[]{:S(2)}) collective-permute-start(bf16[2048,128]{1,0:T(8,128)(2,1)} %bitcast.11), channel_id=1, source_target_pairs={{0,1},{1,0},{2,3},{3,2},{4,5},{5,4},{6,7},{7,6},{8,9},{9,8},{10,11... | collective-permute-start | bytes 1572872 | tf_op jit(solution)/shard_map/ppermute | solution.py:463
  1.1 15.3 %collective-permute-start.1 = (bf16[2048,128]{1,0:T(8,128)(2,1)}, bf16[2048,128]{1,0:T(8,128)(2,1)S(1)}, u32[]{:S(2)}, u32[]{:S(2)}) collective-permute-start(bf16[2048,128]{1,0:T(8,128)(2,1)} %bitcast.13), channel_id=1, source_target_pairs={{0,1},{1,0},{2,3},{3,2},{4,5},{5,4},{6,7},{7,6},{8,9},{9,8},{10,11... | collective-permute-start | bytes 1572872 | tf_op jit(solution)/shard_map/ppermute | solution.py:464
  2.7 13.7 %all-to-all-start = ((bf16[16,2,16,128]{3,2,1,0:T(8,128)(2,1)}), bf16[16,2,16,128]{3,2,1,0:T(8,128)(2,1)S(1)}, u32[]{:S(2)}, u32[]{:S(2)}) async-start(bf16[16,2,16,128]{3,2,1,0:T(8,128)(2,1)} %layout_queries.1), calls=%async_computation | async-start | bytes 262144 | tf_op jit(solution)/shard_map/all_to_all | solution.py:440
  20.1 10.8 %all-to-all-start.1 = ((s32[16,9,2,128]{3,2,1,0:T(2,128)}), s32[16,9,2,128]{3,2,1,0:T(2,128)S(1)}, u32[]{:S(2)}, u32[]{:S(2)}) async-start(s32[16,9,2,128]{3,2,1,0:T(2,128)} %prefix_attention.1), calls=%async_computation.1 | async-start | bytes 294912 | tf_op jit(solution)/shard_map/all_to_all | solution.py:440

commit v8 on v7

--- a/solution.py
+++ b/solution.py
@@ -32,25 +32,19 @@
     return pltpu.with_memory_space_constraint(array, pltpu.HBM)
 
 
-def layout_kernel(q_hbm, sent_hbm, buf, in_sems, out_sems):
-    groups = buf.shape[0]
-    repeats = sent_hbm.shape[0] // groups
+def layout_kernel(q_hbm, sent_ref, in_sems):
+    groups = q_hbm.shape[1]
+    repeats = sent_ref.shape[0] // groups
     reads = [
-        pltpu.make_async_copy(q_hbm.at[:, g], buf.at[groups - 1 - g], in_sems.at[g])
+        pltpu.make_async_copy(q_hbm.at[:, g], sent_ref.at[groups - 1 - g], in_sems.at[g])
         for g in range(groups)
     ]
     for read in reads:
         read.start()
     for read in reads:
         read.wait()
-    writes = [
-        pltpu.make_async_copy(buf, sent_hbm.at[pl.ds(s * groups, groups)], out_sems.at[s])
-        for s in range(repeats)
-    ]
-    for write in writes:
-        write.start()
-    for write in writes:
-        write.wait()
+    for s in range(1, repeats):
+        sent_ref[s * groups : (s + 1) * groups] = sent_ref[:groups]
 
 
 def layout_queries(queries, groups, repeats):
@@ -59,13 +53,9 @@
     return pl.pallas_call(
         layout_kernel,
         in_specs=[IN_HBM],
-        out_specs=IN_HBM,
-        out_shape=pltpu.HBM((repeats * groups, count, group, width), queries.dtype),
-        scratch_shapes=[
-            pltpu.VMEM((groups, count, group, width), queries.dtype),
-            pltpu.SemaphoreType.DMA((groups,)),
-            pltpu.SemaphoreType.DMA((repeats,)),
-        ],
+        out_specs=IN_VMEM,
+        out_shape=pltpu.VMEM((repeats * groups, count, group, width), queries.dtype),
+        scratch_shapes=[pltpu.SemaphoreType.DMA((groups,))],
         compiler_params=pltpu.CompilerParams(vmem_limit_bytes=SMALL_VMEM),
         name="layout_queries",
     )(in_hbm(queries.reshape(count, groups, group, width)))
@@ -242,15 +232,15 @@
 
 
 def prefix_kernel(
-    q_ref, k0_ref, v0_ref, k1_ref, v1_ref, _, out_hbm, out_ref, score_ref, weight_ref, sems, *, per_dest, score_scale
+    q_ref, k0_ref, v0_ref, k1_ref, v1_ref, _, out_ref, score_ref, weight_ref, *, per_dest, score_scale
 ):
     width = q_ref.shape[1]
     tiles = q_ref.shape[0] // ROW_TILE
     dests = ROW_TILE // per_dest
     keys, values = (k0_ref, k1_ref), (v0_ref, v1_ref)
     units = [(tile, block) for tile in range(tiles) for block in range(2)]
-    first_dest = 0 if out_hbm.shape == out_ref.shape else pl.program_id(0) * (tiles * dests)
-    copies = []
+    steps = out_ref.shape[0] // (tiles * dests)
+    first_dest = 0 if steps == 1 else pl.program_id(0) * (tiles * dests)
     lane = lax.broadcasted_iota(jnp.int32, (per_dest, width), 1)
     row = lax.broadcasted_iota(jnp.int32, (per_dest, width), 0)
     diagonal = lane == row
@@ -301,7 +291,7 @@
         half = per_dest // 2
         for k in range(dests):
             rows = slice(k * per_dest, (k + 1) * per_dest)
-            dest = tile * dests + k
+            dest = first_dest + tile * dests + k
             high, low = coded[k * per_dest : k * per_dest + half], coded[k * per_dest + half : rows.stop]
             words = (high << 16) | (low & 0xFFFF)
             for j in range(half // TILE_ROWS):
@@ -313,17 +303,6 @@
             powers = log_power.astype(jnp.int32) << 16
             powers = powers | (exponent(peak_line, PEAK_LEAST).astype(jnp.int32) & 0xFFFF)
             out_ref[dest, half // TILE_ROWS] = jnp.concatenate([mantissa, powers], axis=0)
-        ready = pl.ds(tile * dests, dests)
-        copies.append(
-            pltpu.make_async_copy(
-                out_ref.at[ready],
-                out_hbm.at[pl.ds(first_dest + tile * dests, dests)],
-                sems.at[tile],
-            )
-        )
-        copies[-1].start()
-    for copy in copies:
-        copy.wait()
 
 
 def prefix_partials(
@@ -332,7 +311,6 @@
     rows, width = rows_q.shape
     length = keys.shape[0]
     step_rows = min(STEP_ROWS, rows)
-    dests = step_rows // per_dest
     out_piece = (per_dest // 2 // TILE_ROWS + 1, TILE_ROWS, width)
     blocked = {"in_specs": [IN_VMEM] * 5}
     if step_rows < rows:
@@ -345,13 +323,11 @@
             prefix_kernel, per_dest=per_dest, score_scale=score_scale
         ),
         **blocked,
-        out_specs=IN_HBM,
-        out_shape=pltpu.HBM((rows // per_dest, *out_piece), jnp.int32),
+        out_specs=IN_VMEM,
+        out_shape=pltpu.VMEM((rows // per_dest, *out_piece), jnp.int32),
         scratch_shapes=[
-            pltpu.VMEM((dests, *out_piece), jnp.int32),
             pltpu.VMEM((2, ROW_TILE, length), jnp.float32),
             pltpu.VMEM((2, ROW_TILE, length), jnp.bfloat16),
-            pltpu.SemaphoreType.DMA((step_rows // ROW_TILE,)),
         ],
         compiler_params=pltpu.CompilerParams(vmem_limit_bytes=PREFIX_VMEM),
         cost_estimate=pl.CostEstimate(

time: 32.2 us -> 32.2 us (level)
  Pallas kernels: 12.4 us -> 11.5 us
  waiting for transfers between devices: 2.43 us -> 3.29 us
    all_to_all x2, waiting for transfers between devices: 2.42 us -> 3.28 us  [exchange(): lax.all_to_all(pieces, ('seq', 'head', 'rep'), split_axis=0, concat_axis=...]
    pallas_call x2, Pallas kernels: 6.38 us -> 5.52 us  [suffix_partials(): pl.pallas_call(functools.partial(suffix_kernel, place=place, carried=len(...]
  transfers between devices with their start and end apart: 4 -> 4, of which waited for: 2 -> 2; matrix products, arithmetic and copies ran while one was open for 0% -> 0% of each run, Pallas kernels for 25% -> 22%
where the time goes in v8:
time: 32.2 us; the launch traced here: 31.8 us
  starting transfers between devices  16.3 us (51%)
  Pallas kernels  11.5 us (36%)
  waiting for transfers between devices  3.29 us (10%)
  between operations  0.66 us (2%)
    all_to_all x2, starting transfers between devices, exchange(): lax.all_to_all(pieces, ('seq', 'head', 'rep'), split_axis=0, concat_axis=...  15.7 us
    pallas_call x2, Pallas kernels, suffix_partials(): pl.pallas_call(functools.partial(suffix_kernel, place=place, carried=len(...  5.52 us
    pallas_call x1, Pallas kernels, prefix_partials(): pl.pallas_call(functools.partial(prefix_kernel, per_dest=per_dest, score_...  3.68 us
    all_to_all x2, waiting for transfers between devices, exchange(): lax.all_to_all(pieces, ('seq', 'head', 'rep'), split_axis=0, concat_axis=...  3.28 us
    pallas_call x1, Pallas kernels, layout_queries(): pl.pallas_call(layout_kernel, in_specs=[IN_HBM], out_specs=IN_VMEM, out_s...  1.44 us
    pallas_call x1, Pallas kernels, join_partials(): pl.pallas_call(functools.partial(join_kernel, kv_count=kv_count), in_spec...  0.87 us
  transfers between devices with their start and end apart: 4, of which 2 were waited for; matrix products, arithmetic and copies ran while one was open for 0% of the time, Pallas kernels for 22%

profile of v8, /device:TPU:0, one launch (start us, length us, event | category | flops | bytes accessed | tf_op | source)
XLA Modules:
  0.0 31.8 jit_solution(16052248002896478971)
XLA Ops:
  0.6 0.5 %collective-permute-start = (bf16[2048,128]{1,0:T(8,128)(2,1)}, bf16[2048,128]{1,0:T(8,128)(2,1)S(1)}, u32[]{:S(2)}, u32[]{:S(2)}) collective-permute-start(bf16[2048,128]{1,0:T(8,128)(2,1)} %bitcast.11), channel_id=1, source_target_pairs={{0,1},{1,0},{2,3},{3,2},{4,5},{5,4},{6,7},{7,6},{8,9},{9,8},{10,11... | collective-permute-start | bytes 1572872 | tf_op jit(solution)/shard_map/ppermute | solution.py:439
  1.1 0.1 collective-permute-start.1
  1.2 1.4 %layout_queries.1 = bf16[16,2,16,128]{3,2,1,0:T(8,128)(2,1)} custom-call(bf16[2,4,16,128]{3,2,1,0:T(8,128)(2,1)} %bitcast.15), custom_call_target="tpu_custom_call" | custom-call | tf_op jit(solution)/shard_map/layout_queries/pallas_call | solution.py:53
  2.7 9.3 %all-to-all-start = ((bf16[16,2,16,128]{3,2,1,0:T(8,128)(2,1)}), bf16[16,2,16,128]{3,2,1,0:T(8,128)(2,1)S(1)}, u32[]{:S(2)}, u32[]{:S(2)}) async-start(bf16[16,2,16,128]{3,2,1,0:T(8,128)(2,1)} %layout_queries.1), calls=%async_computation | async-start | bytes 262144 | tf_op jit(solution)/shard_map/all_to_all | solution.py:416
  12.0 2.7 %suffix_attention_0.1 = (f32[64,128]{1,0:T(8,128)S(1)}, f32[64,128]{1,0:T(8,128)S(1)}, bf16[2048,128]{1,0:T(8,128)(2,1)S(1)}, bf16[2048,128]{1,0:T(8,128)(2,1)S(1)}) custom-call(s32[2]{0:T(128)} %refs_0_.3, s32[2]{0:T(128)} %refs_1_.3, bf16[2,64,128]{2,1,0:T(8,128)(2,1)} %refs_2_.3, bf16[2,8192,128]{2,1,0:T(8,128)(2,1)} %bitcast.7, ...), custom_call_target="tpu_custom_call" | custom-call | flops 268435456 | bytes 4194304 | tf_op jit(solution)/shard_map/suffix_attention_0/pallas_call | solution.py:194
  14.6 1.8 %all-to-all-done = bf16[16,2,16,128]{3,2,1,0:T(8,128)(2,1)S(1)} async-done(((bf16[16,2,16,128]{3,2,1,0:T(8,128)(2,1)}), bf16[16,2,16,128]{3,2,1,0:T(8,128)(2,1)S(1)}, u32[]{:S(2)}, u32[]{:S(2)}) %all-to-all-start) | async-done | bytes 131104 | tf_op jit(solution)/shard_map/all_to_all | solution.py:416
  16.4 0.0 collective-permute-done.k1_ref
  16.4 0.0 collective-permute-done.1.v1_ref
  16.4 3.7 %prefix_attention.1 = s32[16,9,2,128]{3,2,1,0:T(2,128)} custom-call(bf16[512,128]{1,0:T(8,128)(2,1)S(1)} %bitcast.6, bf16[2048,128]{1,0:T(8,128)(2,1)S(1)} %get-tuple-element.8.k0_ref, bf16[2048,128]{1,0:T(8,128)(2,1)S(1)} %get-tuple-element.9.v0_ref, bf16[2048,128]{1,0:T(8,128)(2,1)S(1)} %collective-permute-done.k1_ref, ...), custom_call_target="tpu_custom_call" | custom-call | flops 1073741824 | bytes 2490368 | tf_op jit(solution)/shard_map/prefix_attention/pallas_call | solution.py:321
  20.1 6.4 %all-to-all-start.1 = ((s32[16,9,2,128]{3,2,1,0:T(2,128)}), s32[16,9,2,128]{3,2,1,0:T(2,128)S(1)}, u32[]{:S(2)}, u32[]{:S(2)}) async-start(s32[16,9,2,128]{3,2,1,0:T(2,128)} %prefix_attention.1), calls=%async_computation.1 | async-start | bytes 294912 | tf_op jit(solution)/shard_map/all_to_all | solution.py:416
  26.5 2.9 %suffix_attention_1.1 = (f32[2,64,128]{2,1,0:T(8,128)S(1)}, f32[2,64,128]{2,1,0:T(8,128)S(1)}) custom-call(s32[2]{0:T(128)} %refs_0_.3, s32[2]{0:T(128)} %refs_1_.3, bf16[2,64,128]{2,1,0:T(8,128)(2,1)} %refs_2_.3, bf16[2,8192,128]{2,1,0:T(8,128)(2,1)} %bitcast.8, bf16[2,8192,128]{2,1,0:T(8,128)(2,1)} %bitcast.10, f32[64,128]{1,0:T(8,128)S(1)} %get-tuple-element.10._.refs_5_, ...), custom_call_target="tpu_custom_call" | custom-call | flops 268435456 | bytes 4194304 | tf_op jit(solution)/shard_map/suffix_attention_1/pallas_call | solution.py:194
  29.3 1.5 %all-to-all-done.1.got_ref = s32[16,9,2,128]{3,2,1,0:T(2,128)S(1)} async-done(((s32[16,9,2,128]{3,2,1,0:T(2,128)}), s32[16,9,2,128]{3,2,1,0:T(2,128)S(1)}, u32[]{:S(2)}, u32[]{:S(2)}) %all-to-all-start.1) | async-done | bytes 147488 | tf_op jit(solution)/shard_map/all_to_all | solution.py:416
  30.9 0.9 %join_partials.1 = (f32[2,64,128]{2,1,0:T(8,128)}, f32[2,64]{1,0:T(2,128)}) custom-call(s32[16,9,2,128]{3,2,1,0:T(2,128)S(1)} %all-to-all-done.1.got_ref, f32[2,64,128]{2,1,0:T(8,128)S(1)} %get-tuple-element.12.suf_ref, f32[2,64,128]{2,1,0:T(8,128)S(1)} %get-tuple-element.13.suf_log_ref), custom_call_target="tpu_custom_call" | custom-call | tf_op jit(solution)/shard_map/join_partials/pallas_call | solution.py:396
Async XLA Ops:
  0.6 15.8 %collective-permute-start = (bf16[2048,128]{1,0:T(8,128)(2,1)}, bf16[2048,128]{1,0:T(8,128)(2,1)S(1)}, u32[]{:S(2)}, u32[]{:S(2)}) collective-permute-start(bf16[2048,128]{1,0:T(8,128)(2,1)} %bitcast.11), channel_id=1, source_target_pairs={{0,1},{1,0},{2,3},{3,2},{4,5},{5,4},{6,7},{7,6},{8,9},{9,8},{10,11... | collective-permute-start | bytes 1572872 | tf_op jit(solution)/shard_map/ppermute | solution.py:439
  1.1 15.2 %collective-permute-start.1 = (bf16[2048,128]{1,0:T(8,128)(2,1)}, bf16[2048,128]{1,0:T(8,128)(2,1)S(1)}, u32[]{:S(2)}, u32[]{:S(2)}) collective-permute-start(bf16[2048,128]{1,0:T(8,128)(2,1)} %bitcast.13), channel_id=1, source_target_pairs={{0,1},{1,0},{2,3},{3,2},{4,5},{5,4},{6,7},{7,6},{8,9},{9,8},{10,11... | collective-permute-start | bytes 1572872 | tf_op jit(solution)/shard_map/ppermute | solution.py:440
  2.7 13.7 %all-to-all-start = ((bf16[16,2,16,128]{3,2,1,0:T(8,128)(2,1)}), bf16[16,2,16,128]{3,2,1,0:T(8,128)(2,1)S(1)}, u32[]{:S(2)}, u32[]{:S(2)}) async-start(bf16[16,2,16,128]{3,2,1,0:T(8,128)(2,1)} %layout_queries.1), calls=%async_computation | async-start | bytes 262144 | tf_op jit(solution)/shard_map/all_to_all | solution.py:416
  20.1 10.8 %all-to-all-start.1 = ((s32[16,9,2,128]{3,2,1,0:T(2,128)}), s32[16,9,2,128]{3,2,1,0:T(2,128)S(1)}, u32[]{:S(2)}, u32[]{:S(2)}) async-start(s32[16,9,2,128]{3,2,1,0:T(2,128)} %prefix_attention.1), calls=%async_computation.1 | async-start | bytes 294912 | tf_op jit(solution)/shard_map/all_to_all | solution.py:416

commit v9 on v7

--- a/solution.py
+++ b/solution.py
@@ -456,7 +456,7 @@
     score_scale = 1.0 / math.sqrt(width)
     sent = layout_queries(queries, kv_count, lax.axis_size("seq"))
     seq = lax.axis_size("seq")
-    middle = seq // 2
+    middle = (seq - 1) // 2
     got_q = exchange(sent, middle)
     keys = prefix_keys[:, 0, :]
     values = prefix_values[:, 0, :]

time: 32.2 us -> 32.3 us (level)
  waiting for transfers between devices: 2.43 us -> 4.97 us
  starting transfers between devices: 16.3 us -> 14.7 us
  Pallas kernels: 12.4 us -> 11.5 us
    all_to_all x2, waiting for transfers between devices: 2.42 us -> 4.97 us  [exchange(): lax.all_to_all(pieces, ('seq', 'head', 'rep'), split_axis=0, concat_axis=...]
    all_to_all x2, starting transfers between devices: 15.7 us -> 14.1 us  [exchange(): lax.all_to_all(pieces, ('seq', 'head', 'rep'), split_axis=0, concat_axis=...]
    pallas_call x2, Pallas kernels: 6.38 us -> 5.52 us  [suffix_partials(): pl.pallas_call(functools.partial(suffix_kernel, place=place, carried=len(...]
  transfers between devices with their start and end apart: 4 -> 4, of which waited for: 2 -> 2; matrix products, arithmetic and copies ran while one was open for 0% -> 0% of each run, Pallas kernels for 25% -> 22%
where the time goes in v9:
time: 32.3 us; the launch traced here: 31.8 us
  starting transfers between devices  14.7 us (46%)
  Pallas kernels  11.5 us (36%)
  waiting for transfers between devices  4.97 us (15%)
  between operations  0.66 us (2%)
    all_to_all x2, starting transfers between devices, exchange(): lax.all_to_all(pieces, ('seq', 'head', 'rep'), split_axis=0, concat_axis=...  14.1 us
    pallas_call x2, Pallas kernels, suffix_partials(): pl.pallas_call(functools.partial(suffix_kernel, place=place, carried=len(...  5.52 us
    all_to_all x2, waiting for transfers between devices, exchange(): lax.all_to_all(pieces, ('seq', 'head', 'rep'), split_axis=0, concat_axis=...  4.97 us
    pallas_call x1, Pallas kernels, prefix_partials(): pl.pallas_call(functools.partial(prefix_kernel, per_dest=per_dest, score_...  3.66 us
    pallas_call x1, Pallas kernels, layout_queries(): pl.pallas_call(layout_kernel, in_specs=[IN_HBM], out_specs=IN_HBM, out_sh...  1.47 us
    pallas_call x1, Pallas kernels, join_partials(): pl.pallas_call(functools.partial(join_kernel, kv_count=kv_count), in_spec...  0.87 us
  transfers between devices with their start and end apart: 4, of which 2 were waited for; matrix products, arithmetic and copies ran while one was open for 0% of the time, Pallas kernels for 22%

profile of v9, /device:TPU:0, one launch (start us, length us, event | category | flops | bytes accessed | tf_op | source)
XLA Modules:
  0.0 31.8 jit_solution(11343470410773580046)
XLA Ops:
  0.6 0.5 %collective-permute-start = (bf16[2048,128]{1,0:T(8,128)(2,1)}, bf16[2048,128]{1,0:T(8,128)(2,1)S(1)}, u32[]{:S(2)}, u32[]{:S(2)}) collective-permute-start(bf16[2048,128]{1,0:T(8,128)(2,1)} %bitcast.11), channel_id=1, source_target_pairs={{0,1},{1,0},{2,3},{3,2},{4,5},{5,4},{6,7},{7,6},{8,9},{9,8},{10,11... | collective-permute-start | bytes 1572872 | tf_op jit(solution)/shard_map/ppermute | solution.py:463
  1.1 0.1 collective-permute-start.1
  1.2 1.5 %layout_queries.1 = bf16[16,2,16,128]{3,2,1,0:T(8,128)(2,1)} custom-call(bf16[2,4,16,128]{3,2,1,0:T(8,128)(2,1)} %bitcast.15), custom_call_target="tpu_custom_call" | custom-call | tf_op jit(solution)/shard_map/layout_queries/pallas_call | solution.py:59
  2.7 8.8 %all-to-all-start = ((bf16[16,2,16,128]{3,2,1,0:T(8,128)(2,1)}), bf16[16,2,16,128]{3,2,1,0:T(8,128)(2,1)S(1)}, u32[]{:S(2)}, u32[]{:S(2)}) async-start(bf16[16,2,16,128]{3,2,1,0:T(8,128)(2,1)} %layout_queries.1), calls=%async_computation | async-start | bytes 262144 | tf_op jit(solution)/shard_map/all_to_all | solution.py:440
  11.5 2.7 %suffix_attention_0.1 = (f32[64,128]{1,0:T(8,128)S(1)}, f32[64,128]{1,0:T(8,128)S(1)}, bf16[2048,128]{1,0:T(8,128)(2,1)S(1)}, bf16[2048,128]{1,0:T(8,128)(2,1)S(1)}) custom-call(s32[2]{0:T(128)} %refs_0_.3, s32[2]{0:T(128)} %refs_1_.3, bf16[2,64,128]{2,1,0:T(8,128)(2,1)} %refs_2_.3, bf16[2,8192,128]{2,1,0:T(8,128)(2,1)} %bitcast.7, ...), custom_call_target="tpu_custom_call" | custom-call | flops 268435456 | bytes 4194304 | tf_op jit(solution)/shard_map/suffix_attention_0/pallas_call | solution.py:204
  14.2 2.5 %all-to-all-done = bf16[16,2,16,128]{3,2,1,0:T(8,128)(2,1)S(1)} async-done(((bf16[16,2,16,128]{3,2,1,0:T(8,128)(2,1)}), bf16[16,2,16,128]{3,2,1,0:T(8,128)(2,1)S(1)}, u32[]{:S(2)}, u32[]{:S(2)}) %all-to-all-start) | async-done | bytes 131104 | tf_op jit(solution)/shard_map/all_to_all | solution.py:440
  16.7 0.0 collective-permute-done.k1_ref
  16.7 0.0 collective-permute-done.1.v1_ref
  16.7 3.7 %prefix_attention.1 = s32[16,9,2,128]{3,2,1,0:T(2,128)} custom-call(bf16[512,128]{1,0:T(8,128)(2,1)S(1)} %bitcast.6, bf16[2048,128]{1,0:T(8,128)(2,1)S(1)} %get-tuple-element.8.k0_ref, bf16[2048,128]{1,0:T(8,128)(2,1)S(1)} %get-tuple-element.9.v0_ref, bf16[2048,128]{1,0:T(8,128)(2,1)S(1)} %collective-permute-done.k1_ref, ...), custom_call_target="tpu_custom_call" | custom-call | flops 1073741824 | bytes 2490368 | tf_op jit(solution)/shard_map/prefix_attention/pallas_call | solution.py:343
  20.4 5.3 %all-to-all-start.1 = ((s32[16,9,2,128]{3,2,1,0:T(2,128)}), s32[16,9,2,128]{3,2,1,0:T(2,128)S(1)}, u32[]{:S(2)}, u32[]{:S(2)}) async-start(s32[16,9,2,128]{3,2,1,0:T(2,128)} %prefix_attention.1), calls=%async_computation.1 | async-start | bytes 294912 | tf_op jit(solution)/shard_map/all_to_all | solution.py:440
  25.7 2.9 %suffix_attention_1.1 = (f32[2,64,128]{2,1,0:T(8,128)S(1)}, f32[2,64,128]{2,1,0:T(8,128)S(1)}) custom-call(s32[2]{0:T(128)} %refs_0_.3, s32[2]{0:T(128)} %refs_1_.3, bf16[2,64,128]{2,1,0:T(8,128)(2,1)} %refs_2_.3, bf16[2,8192,128]{2,1,0:T(8,128)(2,1)} %bitcast.8, bf16[2,8192,128]{2,1,0:T(8,128)(2,1)} %bitcast.10, f32[64,128]{1,0:T(8,128)S(1)} %get-tuple-element.10._.refs_5_, ...), custom_call_target="tpu_custom_call" | custom-call | flops 268435456 | bytes 4194304 | tf_op jit(solution)/shard_map/suffix_attention_1/pallas_call | solution.py:204
  28.5 2.4 %all-to-all-done.1.got_ref = s32[16,9,2,128]{3,2,1,0:T(2,128)S(1)} async-done(((s32[16,9,2,128]{3,2,1,0:T(2,128)}), s32[16,9,2,128]{3,2,1,0:T(2,128)S(1)}, u32[]{:S(2)}, u32[]{:S(2)}) %all-to-all-start.1) | async-done | bytes 147488 | tf_op jit(solution)/shard_map/all_to_all | solution.py:440
  31.0 0.9 %join_partials.1 = (f32[2,64,128]{2,1,0:T(8,128)}, f32[2,64]{1,0:T(2,128)}) custom-call(s32[16,9,2,128]{3,2,1,0:T(2,128)S(1)} %all-to-all-done.1.got_ref, f32[2,64,128]{2,1,0:T(8,128)S(1)} %get-tuple-element.12.suf_ref, f32[2,64,128]{2,1,0:T(8,128)S(1)} %get-tuple-element.13.suf_log_ref), custom_call_target="tpu_custom_call" | custom-call | tf_op jit(solution)/shard_map/join_partials/pallas_call | solution.py:420
Async XLA Ops:
  0.6 16.1 %collective-permute-start = (bf16[2048,128]{1,0:T(8,128)(2,1)}, bf16[2048,128]{1,0:T(8,128)(2,1)S(1)}, u32[]{:S(2)}, u32[]{:S(2)}) collective-permute-start(bf16[2048,128]{1,0:T(8,128)(2,1)} %bitcast.11), channel_id=1, source_target_pairs={{0,1},{1,0},{2,3},{3,2},{4,5},{5,4},{6,7},{7,6},{8,9},{9,8},{10,11... | collective-permute-start | bytes 1572872 | tf_op jit(solution)/shard_map/ppermute | solution.py:463
  1.1 15.6 %collective-permute-start.1 = (bf16[2048,128]{1,0:T(8,128)(2,1)}, bf16[2048,128]{1,0:T(8,128)(2,1)S(1)}, u32[]{:S(2)}, u32[]{:S(2)}) collective-permute-start(bf16[2048,128]{1,0:T(8,128)(2,1)} %bitcast.13), channel_id=1, source_target_pairs={{0,1},{1,0},{2,3},{3,2},{4,5},{5,4},{6,7},{7,6},{8,9},{9,8},{10,11... | collective-permute-start | bytes 1572872 | tf_op jit(solution)/shard_map/ppermute | solution.py:464
  2.7 14.0 %all-to-all-start = ((bf16[16,2,16,128]{3,2,1,0:T(8,128)(2,1)}), bf16[16,2,16,128]{3,2,1,0:T(8,128)(2,1)S(1)}, u32[]{:S(2)}, u32[]{:S(2)}) async-start(bf16[16,2,16,128]{3,2,1,0:T(8,128)(2,1)} %layout_queries.1), calls=%async_computation | async-start | bytes 262144 | tf_op jit(solution)/shard_map/all_to_all | solution.py:440
  20.4 10.6 %all-to-all-start.1 = ((s32[16,9,2,128]{3,2,1,0:T(2,128)}), s32[16,9,2,128]{3,2,1,0:T(2,128)S(1)}, u32[]{:S(2)}, u32[]{:S(2)}) async-start(s32[16,9,2,128]{3,2,1,0:T(2,128)} %prefix_attention.1), calls=%async_computation.1 | async-start | bytes 294912 | tf_op jit(solution)/shard_map/all_to_all | solution.py:440

commit v10 on v9

--- a/solution.py
+++ b/solution.py
@@ -242,14 +242,15 @@
 
 
 def prefix_kernel(
-    q_ref, k0_ref, v0_ref, k1_ref, v1_ref, _, out_hbm, out_ref, score_ref, weight_ref, sems, *, per_dest, score_scale
+    q_ref, k0_ref, v0_ref, k1_ref, v1_ref, _, out_hbm, out_ref, score_ref, weight_ref, sems, *, per_dest, turn, score_scale
 ):
     width = q_ref.shape[1]
     tiles = q_ref.shape[0] // ROW_TILE
     dests = ROW_TILE // per_dest
     keys, values = (k0_ref, k1_ref), (v0_ref, v1_ref)
     units = [(tile, block) for tile in range(tiles) for block in range(2)]
-    first_dest = 0 if out_hbm.shape == out_ref.shape else pl.program_id(0) * (tiles * dests)
+    places = out_hbm.shape[0] // dests
+    first_place = turn + (0 if out_hbm.shape == out_ref.shape else pl.program_id(0) * tiles)
     copies = []
     lane = lax.broadcasted_iota(jnp.int32, (per_dest, width), 1)
     row = lax.broadcasted_iota(jnp.int32, (per_dest, width), 0)
@@ -317,7 +318,7 @@
         copies.append(
             pltpu.make_async_copy(
                 out_ref.at[ready],
-                out_hbm.at[pl.ds(first_dest + tile * dests, dests)],
+                out_hbm.at[pl.ds(lax.rem(first_place + tile, places) * dests, dests)],
                 sems.at[tile],
             )
         )
@@ -327,7 +328,7 @@
 
 
 def prefix_partials(
-    rows_q, keys, values, far_keys, far_values, after, per_dest, score_scale
+    rows_q, keys, values, far_keys, far_values, after, per_dest, turn, score_scale
 ):
     rows, width = rows_q.shape
     length = keys.shape[0]
@@ -342,7 +343,7 @@
     blocked["in_specs"] += [pl.BlockSpec(memory_space=pl.ANY)]
     return pl.pallas_call(
         functools.partial(
-            prefix_kernel, per_dest=per_dest, score_scale=score_scale
+            prefix_kernel, per_dest=per_dest, turn=turn, score_scale=score_scale
         ),
         **blocked,
         out_specs=IN_HBM,
@@ -456,8 +457,8 @@
     score_scale = 1.0 / math.sqrt(width)
     sent = layout_queries(queries, kv_count, lax.axis_size("seq"))
     seq = lax.axis_size("seq")
-    middle = (seq - 1) // 2
-    got_q = exchange(sent, middle)
+    out_first, back_first = (seq - 1) // 2, seq // 2
+    got_q = exchange(sent, out_first)
     keys = prefix_keys[:, 0, :]
     values = prefix_values[:, 0, :]
     far_keys = lax.ppermute(keys, "rep", [(0, 1), (1, 0)])
@@ -486,9 +487,10 @@
         far_values,
         earlier[0],
         per_dest,
+        (back_first - out_first) % seq,
         score_scale,
     )
-    got = exchange(partials, middle)
+    got = exchange(partials, back_first)
     return join_partials(got, mixed, log, kv_count)
 
 

time: 32.3 us -> 32.1 us (level)
  waiting for transfers between devices: 4.97 us -> 3.36 us
  starting transfers between devices: 14.7 us -> 15.4 us
  Pallas kernels: 11.5 us -> 12.2 us
    all_to_all x2, waiting for transfers between devices: 4.97 us -> 3.35 us  [exchange(): lax.all_to_all(pieces, ('seq', 'head', 'rep'), split_axis=0, concat_axis=...]
    all_to_all x2, starting transfers between devices: 14.1 us -> 14.8 us  [exchange(): lax.all_to_all(pieces, ('seq', 'head', 'rep'), split_axis=0, concat_axis=...]
    pallas_call x2, Pallas kernels: 5.52 us -> 6.24 us  [suffix_partials(): pl.pallas_call(functools.partial(suffix_kernel, place=place, carried=len(...]
  transfers between devices with their start and end apart: 4 -> 4, of which waited for: 2 -> 2; matrix products, arithmetic and copies ran while one was open for 0% -> 0% of each run, Pallas kernels for 22% -> 24%
where the time goes in v10:
time: 32.1 us; the launch traced here: 31.6 us
  starting transfers between devices  15.4 us (48%)
  Pallas kernels  12.2 us (38%)
  waiting for transfers between devices  3.36 us (10%)
  between operations  0.66 us (2%)
    all_to_all x2, starting transfers between devices, exchange(): lax.all_to_all(pieces, ('seq', 'head', 'rep'), split_axis=0, concat_axis=...  14.8 us
    pallas_call x2, Pallas kernels, suffix_partials(): pl.pallas_call(functools.partial(suffix_kernel, place=place, carried=len(...  6.24 us
    pallas_call x1, Pallas kernels, prefix_partials(): pl.pallas_call(functools.partial(prefix_kernel, per_dest=per_dest, turn=t...  3.65 us
    all_to_all x2, waiting for transfers between devices, exchange(): lax.all_to_all(pieces, ('seq', 'head', 'rep'), split_axis=0, concat_axis=...  3.35 us
    pallas_call x1, Pallas kernels, layout_queries(): pl.pallas_call(layout_kernel, in_specs=[IN_HBM], out_specs=IN_HBM, out_sh...  1.47 us
    pallas_call x1, Pallas kernels, join_partials(): pl.pallas_call(functools.partial(join_kernel, kv_count=kv_count), in_spec...  0.87 us
  transfers between devices with their start and end apart: 4, of which 2 were waited for; matrix products, arithmetic and copies ran while one was open for 0% of the time, Pallas kernels for 24%

profile of v10, /device:TPU:0, one launch (start us, length us, event | category | flops | bytes accessed | tf_op | source)
XLA Modules:
  0.0 31.6 jit_solution(16552938358563568835)
XLA Ops:
  0.6 0.5 %collective-permute-start = (bf16[2048,128]{1,0:T(8,128)(2,1)}, bf16[2048,128]{1,0:T(8,128)(2,1)S(1)}, u32[]{:S(2)}, u32[]{:S(2)}) collective-permute-start(bf16[2048,128]{1,0:T(8,128)(2,1)} %bitcast.11), channel_id=1, source_target_pairs={{0,1},{1,0},{2,3},{3,2},{4,5},{5,4},{6,7},{7,6},{8,9},{9,8},{10,11... | collective-permute-start | bytes 1572872 | tf_op jit(solution)/shard_map/ppermute | solution.py:464
  1.1 0.1 collective-permute-start.1
  1.2 1.5 %layout_queries.1 = bf16[16,2,16,128]{3,2,1,0:T(8,128)(2,1)} custom-call(bf16[2,4,16,128]{3,2,1,0:T(8,128)(2,1)} %bitcast.15), custom_call_target="tpu_custom_call" | custom-call | tf_op jit(solution)/shard_map/layout_queries/pallas_call | solution.py:59
  2.7 8.8 %all-to-all-start = ((bf16[16,2,16,128]{3,2,1,0:T(8,128)(2,1)}), bf16[16,2,16,128]{3,2,1,0:T(8,128)(2,1)S(1)}, u32[]{:S(2)}, u32[]{:S(2)}) async-start(bf16[16,2,16,128]{3,2,1,0:T(8,128)(2,1)} %layout_queries.1), calls=%async_computation | async-start | bytes 262144 | tf_op jit(solution)/shard_map/all_to_all | solution.py:441
  11.5 2.7 %suffix_attention_0.1 = (f32[64,128]{1,0:T(8,128)S(1)}, f32[64,128]{1,0:T(8,128)S(1)}, bf16[2048,128]{1,0:T(8,128)(2,1)S(1)}, bf16[2048,128]{1,0:T(8,128)(2,1)S(1)}) custom-call(s32[2]{0:T(128)} %refs_0_.3, s32[2]{0:T(128)} %refs_1_.3, bf16[2,64,128]{2,1,0:T(8,128)(2,1)} %refs_2_.3, bf16[2,8192,128]{2,1,0:T(8,128)(2,1)} %bitcast.7, ...), custom_call_target="tpu_custom_call" | custom-call | flops 268435456 | bytes 4194304 | tf_op jit(solution)/shard_map/suffix_attention_0/pallas_call | solution.py:204
  14.2 2.5 %all-to-all-done = bf16[16,2,16,128]{3,2,1,0:T(8,128)(2,1)S(1)} async-done(((bf16[16,2,16,128]{3,2,1,0:T(8,128)(2,1)}), bf16[16,2,16,128]{3,2,1,0:T(8,128)(2,1)S(1)}, u32[]{:S(2)}, u32[]{:S(2)}) %all-to-all-start) | async-done | bytes 131104 | tf_op jit(solution)/shard_map/all_to_all | solution.py:441
  16.7 0.0 collective-permute-done.k1_ref
  16.7 0.0 collective-permute-done.1.v1_ref
  16.7 3.7 %prefix_attention.1 = s32[16,9,2,128]{3,2,1,0:T(2,128)} custom-call(bf16[512,128]{1,0:T(8,128)(2,1)S(1)} %bitcast.6, bf16[2048,128]{1,0:T(8,128)(2,1)S(1)} %get-tuple-element.8.k0_ref, bf16[2048,128]{1,0:T(8,128)(2,1)S(1)} %get-tuple-element.9.v0_ref, bf16[2048,128]{1,0:T(8,128)(2,1)S(1)} %collective-permute-done.k1_ref, ...), custom_call_target="tpu_custom_call" | custom-call | flops 1073741824 | bytes 2490368 | tf_op jit(solution)/shard_map/prefix_attention/pallas_call | solution.py:344
  20.4 6.0 %all-to-all-start.1 = ((s32[16,9,2,128]{3,2,1,0:T(2,128)}), s32[16,9,2,128]{3,2,1,0:T(2,128)S(1)}, u32[]{:S(2)}, u32[]{:S(2)}) async-start(s32[16,9,2,128]{3,2,1,0:T(2,128)} %prefix_attention.1), calls=%async_computation.1 | async-start | bytes 294912 | tf_op jit(solution)/shard_map/all_to_all | solution.py:441
  26.4 3.6 %suffix_attention_1.1 = (f32[2,64,128]{2,1,0:T(8,128)S(1)}, f32[2,64,128]{2,1,0:T(8,128)S(1)}) custom-call(s32[2]{0:T(128)} %refs_0_.3, s32[2]{0:T(128)} %refs_1_.3, bf16[2,64,128]{2,1,0:T(8,128)(2,1)} %refs_2_.3, bf16[2,8192,128]{2,1,0:T(8,128)(2,1)} %bitcast.8, bf16[2,8192,128]{2,1,0:T(8,128)(2,1)} %bitcast.10, f32[64,128]{1,0:T(8,128)S(1)} %get-tuple-element.10._.refs_5_, ...), custom_call_target="tpu_custom_call" | custom-call | flops 268435456 | bytes 4194304 | tf_op jit(solution)/shard_map/suffix_attention_1/pallas_call | solution.py:204
  30.0 0.8 %all-to-all-done.1.got_ref = s32[16,9,2,128]{3,2,1,0:T(2,128)S(1)} async-done(((s32[16,9,2,128]{3,2,1,0:T(2,128)}), s32[16,9,2,128]{3,2,1,0:T(2,128)S(1)}, u32[]{:S(2)}, u32[]{:S(2)}) %all-to-all-start.1) | async-done | bytes 147488 | tf_op jit(solution)/shard_map/all_to_all | solution.py:441
  30.8 0.9 %join_partials.1 = (f32[2,64,128]{2,1,0:T(8,128)}, f32[2,64]{1,0:T(2,128)}) custom-call(s32[16,9,2,128]{3,2,1,0:T(2,128)S(1)} %all-to-all-done.1.got_ref, f32[2,64,128]{2,1,0:T(8,128)S(1)} %get-tuple-element.12.suf_ref, f32[2,64,128]{2,1,0:T(8,128)S(1)} %get-tuple-element.13.suf_log_ref), custom_call_target="tpu_custom_call" | custom-call | tf_op jit(solution)/shard_map/join_partials/pallas_call | solution.py:421
Async XLA Ops:
  0.6 16.1 %collective-permute-start = (bf16[2048,128]{1,0:T(8,128)(2,1)}, bf16[2048,128]{1,0:T(8,128)(2,1)S(1)}, u32[]{:S(2)}, u32[]{:S(2)}) collective-permute-start(bf16[2048,128]{1,0:T(8,128)(2,1)} %bitcast.11), channel_id=1, source_target_pairs={{0,1},{1,0},{2,3},{3,2},{4,5},{5,4},{6,7},{7,6},{8,9},{9,8},{10,11... | collective-permute-start | bytes 1572872 | tf_op jit(solution)/shard_map/ppermute | solution.py:464
  1.1 15.6 %collective-permute-start.1 = (bf16[2048,128]{1,0:T(8,128)(2,1)}, bf16[2048,128]{1,0:T(8,128)(2,1)S(1)}, u32[]{:S(2)}, u32[]{:S(2)}) collective-permute-start(bf16[2048,128]{1,0:T(8,128)(2,1)} %bitcast.13), channel_id=1, source_target_pairs={{0,1},{1,0},{2,3},{3,2},{4,5},{5,4},{6,7},{7,6},{8,9},{9,8},{10,11... | collective-permute-start | bytes 1572872 | tf_op jit(solution)/shard_map/ppermute | solution.py:465
  2.7 14.0 %all-to-all-start = ((bf16[16,2,16,128]{3,2,1,0:T(8,128)(2,1)}), bf16[16,2,16,128]{3,2,1,0:T(8,128)(2,1)S(1)}, u32[]{:S(2)}, u32[]{:S(2)}) async-start(bf16[16,2,16,128]{3,2,1,0:T(8,128)(2,1)} %layout_queries.1), calls=%async_computation | async-start | bytes 262144 | tf_op jit(solution)/shard_map/all_to_all | solution.py:441
  20.4 10.4 %all-to-all-start.1 = ((s32[16,9,2,128]{3,2,1,0:T(2,128)}), s32[16,9,2,128]{3,2,1,0:T(2,128)S(1)}, u32[]{:S(2)}, u32[]{:S(2)}) async-start(s32[16,9,2,128]{3,2,1,0:T(2,128)} %prefix_attention.1), calls=%async_computation.1 | async-start | bytes 294912 | tf_op jit(solution)/shard_map/all_to_all | solution.py:441

commit v11 on v10

--- a/solution.py
+++ b/solution.py
@@ -272,22 +272,16 @@
                 peak = lanes if peak is None else jnp.maximum(peak, lanes)
         return jnp.max(peak, axis=1, keepdims=True)
 
-    later_max = score(units[0], 0)
-    held = None
-    for step, (tile, block) in enumerate(units):
-        row_max = later_max
-        if step + 1 < len(units):
-            later_max = score(units[step + 1], (step + 1) % 2)
-        slot = step % 2
-        sums = weigh(
-            score_ref.at[slot], weight_ref.at[slot], slice(0, length), row_max, score_scale * LOG2E
-        )
+    held = []
+
+    def finish(step, row_max, sums):
+        tile, block = units[step]
         total = jnp.sum(sums, axis=1, keepdims=True)
-        acc = jnp.dot(weight_ref[slot], values[block][...], preferred_element_type=jnp.float32)
+        acc = jnp.dot(weight_ref[step % 2], values[block][...], preferred_element_type=jnp.float32)
         if block == 0:
-            held = (row_max, total, acc)
-            continue
-        max0, total0, acc0 = held
+            held.append((row_max, total, acc))
+            return
+        max0, total0, acc0 = held.pop()
         top = jnp.maximum(max0, row_max)
         weight0 = jnp.exp((max0 - top) * score_scale)
         weight1 = jnp.exp((row_max - top) * score_scale)
@@ -323,6 +317,19 @@
             )
         )
         copies[-1].start()
+    later_max = score(units[0], 0)
+    pending = None
+    for step in range(len(units)):
+        row_max, slot = later_max, step % 2
+        if step + 1 < len(units):
+            later_max = score(units[step + 1], (step + 1) % 2)
+        if pending is not None:
+            finish(*pending)
+        sums = weigh(
+            score_ref.at[slot], weight_ref.at[slot], slice(0, length), row_max, score_scale * LOG2E
+        )
+        pending = (step, row_max, sums)
+    finish(*pending)
     for copy in copies:
         copy.wait()
 

time: 32.1 us -> 32.1 us (level)
  Pallas kernels: 12.2 us -> 12.6 us
  transfers between devices with their start and end apart: 4 -> 4, of which waited for: 2 -> 2; matrix products, arithmetic and copies ran while one was open for 0% -> 0% of each run, Pallas kernels for 24% -> 25%
where the time goes in v11:
time: 32.1 us; the launch traced here: 31.7 us
  starting transfers between devices  15.4 us (48%)
  Pallas kernels  12.6 us (39%)
  waiting for transfers between devices  3.04 us (9%)
  between operations  0.66 us (2%)
    all_to_all x2, starting transfers between devices, exchange(): lax.all_to_all(pieces, ('seq', 'head', 'rep'), split_axis=0, concat_axis=...  14.8 us
    pallas_call x2, Pallas kernels, suffix_partials(): pl.pallas_call(functools.partial(suffix_kernel, place=place, carried=len(...  6.55 us
    pallas_call x1, Pallas kernels, prefix_partials(): pl.pallas_call(functools.partial(prefix_kernel, per_dest=per_dest, turn=t...  3.71 us
    all_to_all x2, waiting for transfers between devices, exchange(): lax.all_to_all(pieces, ('seq', 'head', 'rep'), split_axis=0, concat_axis=...  3.04 us
    pallas_call x1, Pallas kernels, layout_queries(): pl.pallas_call(layout_kernel, in_specs=[IN_HBM], out_specs=IN_HBM, out_sh...  1.47 us
    pallas_call x1, Pallas kernels, join_partials(): pl.pallas_call(functools.partial(join_kernel, kv_count=kv_count), in_spec...  0.87 us
  transfers between devices with their start and end apart: 4, of which 2 were waited for; matrix products, arithmetic and copies ran while one was open for 0% of the time, Pallas kernels for 25%

profile of v11, /device:TPU:0, one launch (start us, length us, event | category | flops | bytes accessed | tf_op | source)
XLA Modules:
  0.0 31.7 jit_solution(14269279397300737905)
XLA Ops:
  0.6 0.5 %collective-permute-start = (bf16[2048,128]{1,0:T(8,128)(2,1)}, bf16[2048,128]{1,0:T(8,128)(2,1)S(1)}, u32[]{:S(2)}, u32[]{:S(2)}) collective-permute-start(bf16[2048,128]{1,0:T(8,128)(2,1)} %bitcast.11), channel_id=1, source_target_pairs={{0,1},{1,0},{2,3},{3,2},{4,5},{5,4},{6,7},{7,6},{8,9},{9,8},{10,11... | collective-permute-start | bytes 1572872 | tf_op jit(solution)/shard_map/ppermute | solution.py:471
  1.1 0.1 collective-permute-start.1
  1.2 1.5 %layout_queries.1 = bf16[16,2,16,128]{3,2,1,0:T(8,128)(2,1)} custom-call(bf16[2,4,16,128]{3,2,1,0:T(8,128)(2,1)} %bitcast.15), custom_call_target="tpu_custom_call" | custom-call | tf_op jit(solution)/shard_map/layout_queries/pallas_call | solution.py:59
  2.7 8.8 %all-to-all-start = ((bf16[16,2,16,128]{3,2,1,0:T(8,128)(2,1)}), bf16[16,2,16,128]{3,2,1,0:T(8,128)(2,1)S(1)}, u32[]{:S(2)}, u32[]{:S(2)}) async-start(bf16[16,2,16,128]{3,2,1,0:T(8,128)(2,1)} %layout_queries.1), calls=%async_computation | async-start | bytes 262144 | tf_op jit(solution)/shard_map/all_to_all | solution.py:448
  11.5 2.7 %suffix_attention_0.1 = (f32[64,128]{1,0:T(8,128)S(1)}, f32[64,128]{1,0:T(8,128)S(1)}, bf16[2048,128]{1,0:T(8,128)(2,1)S(1)}, bf16[2048,128]{1,0:T(8,128)(2,1)S(1)}) custom-call(s32[2]{0:T(128)} %refs_0_.3, s32[2]{0:T(128)} %refs_1_.3, bf16[2,64,128]{2,1,0:T(8,128)(2,1)} %refs_2_.3, bf16[2,8192,128]{2,1,0:T(8,128)(2,1)} %bitcast.7, ...), custom_call_target="tpu_custom_call" | custom-call | flops 268435456 | bytes 4194304 | tf_op jit(solution)/shard_map/suffix_attention_0/pallas_call | solution.py:204
  14.2 2.5 %all-to-all-done = bf16[16,2,16,128]{3,2,1,0:T(8,128)(2,1)S(1)} async-done(((bf16[16,2,16,128]{3,2,1,0:T(8,128)(2,1)}), bf16[16,2,16,128]{3,2,1,0:T(8,128)(2,1)S(1)}, u32[]{:S(2)}, u32[]{:S(2)}) %all-to-all-start) | async-done | bytes 131104 | tf_op jit(solution)/shard_map/all_to_all | solution.py:448
  16.7 0.0 collective-permute-done.k1_ref
  16.7 0.0 collective-permute-done.1.v1_ref
  16.7 3.7 %prefix_attention.1 = s32[16,9,2,128]{3,2,1,0:T(2,128)} custom-call(bf16[512,128]{1,0:T(8,128)(2,1)S(1)} %bitcast.6, bf16[2048,128]{1,0:T(8,128)(2,1)S(1)} %get-tuple-element.8.k0_ref, bf16[2048,128]{1,0:T(8,128)(2,1)S(1)} %get-tuple-element.9.v0_ref, bf16[2048,128]{1,0:T(8,128)(2,1)S(1)} %collective-permute-done.k1_ref, ...), custom_call_target="tpu_custom_call" | custom-call | flops 1073741824 | bytes 2490368 | tf_op jit(solution)/shard_map/prefix_attention/pallas_call | solution.py:351
  20.4 6.0 %all-to-all-start.1 = ((s32[16,9,2,128]{3,2,1,0:T(2,128)}), s32[16,9,2,128]{3,2,1,0:T(2,128)S(1)}, u32[]{:S(2)}, u32[]{:S(2)}) async-start(s32[16,9,2,128]{3,2,1,0:T(2,128)} %prefix_attention.1), calls=%async_computation.1 | async-start | bytes 294912 | tf_op jit(solution)/shard_map/all_to_all | solution.py:448
  26.4 3.9 %suffix_attention_1.1 = (f32[2,64,128]{2,1,0:T(8,128)S(1)}, f32[2,64,128]{2,1,0:T(8,128)S(1)}) custom-call(s32[2]{0:T(128)} %refs_0_.3, s32[2]{0:T(128)} %refs_1_.3, bf16[2,64,128]{2,1,0:T(8,128)(2,1)} %refs_2_.3, bf16[2,8192,128]{2,1,0:T(8,128)(2,1)} %bitcast.8, bf16[2,8192,128]{2,1,0:T(8,128)(2,1)} %bitcast.10, f32[64,128]{1,0:T(8,128)S(1)} %get-tuple-element.10._.refs_5_, ...), custom_call_target="tpu_custom_call" | custom-call | flops 268435456 | bytes 4194304 | tf_op jit(solution)/shard_map/suffix_attention_1/pallas_call | solution.py:204
  30.3 0.5 %all-to-all-done.1.got_ref = s32[16,9,2,128]{3,2,1,0:T(2,128)S(1)} async-done(((s32[16,9,2,128]{3,2,1,0:T(2,128)}), s32[16,9,2,128]{3,2,1,0:T(2,128)S(1)}, u32[]{:S(2)}, u32[]{:S(2)}) %all-to-all-start.1) | async-done | bytes 147488 | tf_op jit(solution)/shard_map/all_to_all | solution.py:448
  30.8 0.9 %join_partials.1 = (f32[2,64,128]{2,1,0:T(8,128)}, f32[2,64]{1,0:T(2,128)}) custom-call(s32[16,9,2,128]{3,2,1,0:T(2,128)S(1)} %all-to-all-done.1.got_ref, f32[2,64,128]{2,1,0:T(8,128)S(1)} %get-tuple-element.12.suf_ref, f32[2,64,128]{2,1,0:T(8,128)S(1)} %get-tuple-element.13.suf_log_ref), custom_call_target="tpu_custom_call" | custom-call | tf_op jit(solution)/shard_map/join_partials/pallas_call | solution.py:428
Async XLA Ops:
  0.6 16.1 %collective-permute-start = (bf16[2048,128]{1,0:T(8,128)(2,1)}, bf16[2048,128]{1,0:T(8,128)(2,1)S(1)}, u32[]{:S(2)}, u32[]{:S(2)}) collective-permute-start(bf16[2048,128]{1,0:T(8,128)(2,1)} %bitcast.11), channel_id=1, source_target_pairs={{0,1},{1,0},{2,3},{3,2},{4,5},{5,4},{6,7},{7,6},{8,9},{9,8},{10,11... | collective-permute-start | bytes 1572872 | tf_op jit(solution)/shard_map/ppermute | solution.py:471
  1.1 15.6 %collective-permute-start.1 = (bf16[2048,128]{1,0:T(8,128)(2,1)}, bf16[2048,128]{1,0:T(8,128)(2,1)S(1)}, u32[]{:S(2)}, u32[]{:S(2)}) collective-permute-start(bf16[2048,128]{1,0:T(8,128)(2,1)} %bitcast.13), channel_id=1, source_target_pairs={{0,1},{1,0},{2,3},{3,2},{4,5},{5,4},{6,7},{7,6},{8,9},{9,8},{10,11... | collective-permute-start | bytes 1572872 | tf_op jit(solution)/shard_map/ppermute | solution.py:472
  2.7 14.0 %all-to-all-start = ((bf16[16,2,16,128]{3,2,1,0:T(8,128)(2,1)}), bf16[16,2,16,128]{3,2,1,0:T(8,128)(2,1)S(1)}, u32[]{:S(2)}, u32[]{:S(2)}) async-start(bf16[16,2,16,128]{3,2,1,0:T(8,128)(2,1)} %layout_queries.1), calls=%async_computation | async-start | bytes 262144 | tf_op jit(solution)/shard_map/all_to_all | solution.py:448
  20.4 10.4 %all-to-all-start.1 = ((s32[16,9,2,128]{3,2,1,0:T(2,128)}), s32[16,9,2,128]{3,2,1,0:T(2,128)S(1)}, u32[]{:S(2)}, u32[]{:S(2)}) async-start(s32[16,9,2,128]{3,2,1,0:T(2,128)} %prefix_attention.1), calls=%async_computation.1 | async-start | bytes 294912 | tf_op jit(solution)/shard_map/all_to_all | solution.py:448

commit v12 on v11

--- a/solution.py
+++ b/solution.py
@@ -21,7 +21,7 @@
 LEAST = 1e-25
 PEAK_LEAST = 1e-33
 NT = (((1,), (1,)), ((), ()))
-PREFIX_VMEM = 14 * 1024 * 1024
+PREFIX_VMEM = 20 * 1024 * 1024
 SUFFIX_VMEM = 20 * 1024 * 1024
 SMALL_VMEM = 8 * 1024 * 1024
 IN_VMEM = pl.BlockSpec(memory_space=pltpu.VMEM)
@@ -248,7 +248,9 @@
     tiles = q_ref.shape[0] // ROW_TILE
     dests = ROW_TILE // per_dest
     keys, values = (k0_ref, k1_ref), (v0_ref, v1_ref)
-    units = [(tile, block) for tile in range(tiles) for block in range(2)]
+    inner = tiles - 2
+    spans = [(0, 1), (1, inner), (tiles - 1, 1)] if inner == 2 else [(t, 1) for t in range(tiles)]
+    units = [(first, wide, block) for first, wide in spans for block in range(2)]
     places = out_hbm.shape[0] // dests
     first_place = turn + (0 if out_hbm.shape == out_ref.shape else pl.program_id(0) * tiles)
     copies = []
@@ -259,14 +261,14 @@
     length = k0_ref.shape[0]
 
     def score(unit, slot):
-        tile, block = unit
-        query = q_ref[tile * ROW_TILE : (tile + 1) * ROW_TILE]
+        first, wide, block = unit
+        query = q_ref[first * ROW_TILE : (first + wide) * ROW_TILE]
         peak = None
         for at in range(0, length, PIECE):
             part = lax.dot_general(
                 query, keys[block][at : at + PIECE], NT, preferred_element_type=jnp.float32
             )
-            score_ref[slot, :, at : at + PIECE] = part
+            score_ref[slot, : wide * ROW_TILE, at : at + PIECE] = part
             for begin in range(0, PIECE, LANES):
                 lanes = part[:, begin : begin + LANES]
                 peak = lanes if peak is None else jnp.maximum(peak, lanes)
@@ -275,9 +277,12 @@
     held = []
 
     def finish(step, row_max, sums):
-        tile, block = units[step]
+        first, wide, block = units[step]
+        row_count = wide * ROW_TILE
         total = jnp.sum(sums, axis=1, keepdims=True)
-        acc = jnp.dot(weight_ref[step % 2], values[block][...], preferred_element_type=jnp.float32)
+        acc = jnp.dot(
+            weight_ref[step % 2, :row_count], values[block][...], preferred_element_type=jnp.float32
+        )
         if block == 0:
             held.append((row_max, total, acc))
             return
@@ -287,16 +292,16 @@
         weight1 = jnp.exp((row_max - top) * score_scale)
         joined = weight0 * total0 + weight1 * total
         mixed = (weight0 * acc0 + weight1 * acc) / joined
-        logs = jnp.broadcast_to(top * score_scale + jnp.log(joined), (ROW_TILE, width))
+        logs = jnp.broadcast_to(top * score_scale + jnp.log(joined), (row_count, width))
         peak = jnp.max(jnp.abs(mixed), axis=1, keepdims=True)
         coded = jnp.round(mixed * jnp.exp2(VALUE_BITS - exponent(peak, PEAK_LEAST)))
         most = 2.0**VALUE_BITS - 1
         coded = jnp.clip(coded, -most, most).astype(jnp.int32)
-        peaks = jnp.broadcast_to(peak, (ROW_TILE, width))
+        peaks = jnp.broadcast_to(peak, (row_count, width))
         half = per_dest // 2
-        for k in range(dests):
+        for k in range(wide * dests):
             rows = slice(k * per_dest, (k + 1) * per_dest)
-            dest = tile * dests + k
+            dest = first * dests + k
             high, low = coded[k * per_dest : k * per_dest + half], coded[k * per_dest + half : rows.stop]
             words = (high << 16) | (low & 0xFFFF)
             for j in range(half // TILE_ROWS):
@@ -308,15 +313,16 @@
             powers = log_power.astype(jnp.int32) << 16
             powers = powers | (exponent(peak_line, PEAK_LEAST).astype(jnp.int32) & 0xFFFF)
             out_ref[dest, half // TILE_ROWS] = jnp.concatenate([mantissa, powers], axis=0)
-        ready = pl.ds(tile * dests, dests)
-        copies.append(
-            pltpu.make_async_copy(
-                out_ref.at[ready],
-                out_hbm.at[pl.ds(lax.rem(first_place + tile, places) * dests, dests)],
-                sems.at[tile],
+        for tile in range(first, first + wide):
+            copies.append(
+                pltpu.make_async_copy(
+                    out_ref.at[pl.ds(tile * dests, dests)],
+                    out_hbm.at[pl.ds(lax.rem(first_place + tile, places) * dests, dests)],
+                    sems.at[tile],
+                )
             )
-        )
-        copies[-1].start()
+            copies[-1].start()
+
     later_max = score(units[0], 0)
     pending = None
     for step in range(len(units)):
@@ -326,7 +332,11 @@
         if pending is not None:
             finish(*pending)
         sums = weigh(
-            score_ref.at[slot], weight_ref.at[slot], slice(0, length), row_max, score_scale * LOG2E
+            score_ref.at[slot, pl.ds(0, row_max.shape[0])],
+            weight_ref.at[slot, pl.ds(0, row_max.shape[0])],
+            slice(0, length),
+            row_max,
+            score_scale * LOG2E,
         )
         pending = (step, row_max, sums)
     finish(*pending)
@@ -357,8 +367,8 @@
         out_shape=pltpu.HBM((rows // per_dest, *out_piece), jnp.int32),
         scratch_shapes=[
             pltpu.VMEM((dests, *out_piece), jnp.int32),
-            pltpu.VMEM((2, ROW_TILE, length), jnp.float32),
-            pltpu.VMEM((2, ROW_TILE, length), jnp.bfloat16),
+            pltpu.VMEM((2, 2 * ROW_TILE, length), jnp.float32),
+            pltpu.VMEM((2, 2 * ROW_TILE, length), jnp.bfloat16),
             pltpu.SemaphoreType.DMA((step_rows // ROW_TILE,)),
         ],
         compiler_params=pltpu.CompilerParams(vmem_limit_bytes=PREFIX_VMEM),

time: 32.1 us -> 32.3 us (level)
  transfers between devices with their start and end apart: 4 -> 4, of which waited for: 2 -> 2; matrix products, arithmetic and copies ran while one was open for 0% -> 0% of each run, Pallas kernels for 25% -> 26%
where the time goes in v12:
time: 32.3 us; the launch traced here: 31.8 us
  starting transfers between devices  15.4 us (48%)
  Pallas kernels  12.9 us (40%)
  waiting for transfers between devices  2.9 us (9%)
  between operations  0.66 us (2%)
    all_to_all x2, starting transfers between devices, exchange(): lax.all_to_all(pieces, ('seq', 'head', 'rep'), split_axis=0, concat_axis=...  14.8 us
    pallas_call x2, Pallas kernels, suffix_partials(): pl.pallas_call(functools.partial(suffix_kernel, place=place, carried=len(...  6.69 us
    pallas_call x1, Pallas kernels, prefix_partials(): pl.pallas_call(functools.partial(prefix_kernel, per_dest=per_dest, turn=t...  3.83 us
    all_to_all x2, waiting for transfers between devices, exchange(): lax.all_to_all(pieces, ('seq', 'head', 'rep'), split_axis=0, concat_axis=...  2.89 us
    pallas_call x1, Pallas kernels, layout_queries(): pl.pallas_call(layout_kernel, in_specs=[IN_HBM], out_specs=IN_HBM, out_sh...  1.47 us
    pallas_call x1, Pallas kernels, join_partials(): pl.pallas_call(functools.partial(join_kernel, kv_count=kv_count), in_spec...  0.87 us
  transfers between devices with their start and end apart: 4, of which 2 were waited for; matrix products, arithmetic and copies ran while one was open for 0% of the time, Pallas kernels for 26%

profile of v12, /device:TPU:0, one launch (start us, length us, event | category | flops | bytes accessed | tf_op | source)
XLA Modules:
  0.0 31.8 jit_solution(1357723883849160199)
XLA Ops:
  0.6 0.5 %collective-permute-start = (bf16[2048,128]{1,0:T(8,128)(2,1)}, bf16[2048,128]{1,0:T(8,128)(2,1)S(1)}, u32[]{:S(2)}, u32[]{:S(2)}) collective-permute-start(bf16[2048,128]{1,0:T(8,128)(2,1)} %bitcast.11), channel_id=1, source_target_pairs={{0,1},{1,0},{2,3},{3,2},{4,5},{5,4},{6,7},{7,6},{8,9},{9,8},{10,11... | collective-permute-start | bytes 1572872 | tf_op jit(solution)/shard_map/ppermute | solution.py:481
  1.1 0.1 collective-permute-start.1
  1.2 1.5 %layout_queries.1 = bf16[16,2,16,128]{3,2,1,0:T(8,128)(2,1)} custom-call(bf16[2,4,16,128]{3,2,1,0:T(8,128)(2,1)} %bitcast.15), custom_call_target="tpu_custom_call" | custom-call | tf_op jit(solution)/shard_map/layout_queries/pallas_call | solution.py:59
  2.7 8.8 %all-to-all-start = ((bf16[16,2,16,128]{3,2,1,0:T(8,128)(2,1)}), bf16[16,2,16,128]{3,2,1,0:T(8,128)(2,1)S(1)}, u32[]{:S(2)}, u32[]{:S(2)}) async-start(bf16[16,2,16,128]{3,2,1,0:T(8,128)(2,1)} %layout_queries.1), calls=%async_computation | async-start | bytes 262144 | tf_op jit(solution)/shard_map/all_to_all | solution.py:458
  11.5 3.8 %suffix_attention_0.1 = (f32[64,128]{1,0:T(8,128)S(1)}, f32[64,128]{1,0:T(8,128)S(1)}, bf16[2048,128]{1,0:T(8,128)(2,1)S(1)}, bf16[2048,128]{1,0:T(8,128)(2,1)S(1)}) custom-call(s32[2]{0:T(128)} %refs_0_.3, s32[2]{0:T(128)} %refs_1_.3, bf16[2,64,128]{2,1,0:T(8,128)(2,1)} %refs_2_.3, bf16[2,8192,128]{2,1,0:T(8,128)(2,1)} %bitcast.7, ...), custom_call_target="tpu_custom_call" | custom-call | flops 268435456 | bytes 4194304 | tf_op jit(solution)/shard_map/suffix_attention_0/pallas_call | solution.py:204
  15.3 1.4 %all-to-all-done = bf16[16,2,16,128]{3,2,1,0:T(8,128)(2,1)S(1)} async-done(((bf16[16,2,16,128]{3,2,1,0:T(8,128)(2,1)}), bf16[16,2,16,128]{3,2,1,0:T(8,128)(2,1)S(1)}, u32[]{:S(2)}, u32[]{:S(2)}) %all-to-all-start) | async-done | bytes 131104 | tf_op jit(solution)/shard_map/all_to_all | solution.py:458
  16.7 0.0 collective-permute-done.k1_ref
  16.7 0.0 collective-permute-done.1.v1_ref
  16.7 3.8 %prefix_attention.1 = s32[16,9,2,128]{3,2,1,0:T(2,128)} custom-call(bf16[512,128]{1,0:T(8,128)(2,1)S(1)} %bitcast.6, bf16[2048,128]{1,0:T(8,128)(2,1)S(1)} %get-tuple-element.8.k0_ref, bf16[2048,128]{1,0:T(8,128)(2,1)S(1)} %get-tuple-element.9.v0_ref, bf16[2048,128]{1,0:T(8,128)(2,1)S(1)} %collective-permute-done.k1_ref, ...), custom_call_target="tpu_custom_call" | custom-call | flops 1073741824 | bytes 2490368 | tf_op jit(solution)/shard_map/prefix_attention/pallas_call | solution.py:361
  20.5 6.0 %all-to-all-start.1 = ((s32[16,9,2,128]{3,2,1,0:T(2,128)}), s32[16,9,2,128]{3,2,1,0:T(2,128)S(1)}, u32[]{:S(2)}, u32[]{:S(2)}) async-start(s32[16,9,2,128]{3,2,1,0:T(2,128)} %prefix_attention.1), calls=%async_computation.1 | async-start | bytes 294912 | tf_op jit(solution)/shard_map/all_to_all | solution.py:458
  26.6 2.9 %suffix_attention_1.1 = (f32[2,64,128]{2,1,0:T(8,128)S(1)}, f32[2,64,128]{2,1,0:T(8,128)S(1)}) custom-call(s32[2]{0:T(128)} %refs_0_.3, s32[2]{0:T(128)} %refs_1_.3, bf16[2,64,128]{2,1,0:T(8,128)(2,1)} %refs_2_.3, bf16[2,8192,128]{2,1,0:T(8,128)(2,1)} %bitcast.8, bf16[2,8192,128]{2,1,0:T(8,128)(2,1)} %bitcast.10, f32[64,128]{1,0:T(8,128)S(1)} %get-tuple-element.10._.refs_5_, ...), custom_call_target="tpu_custom_call" | custom-call | flops 268435456 | bytes 4194304 | tf_op jit(solution)/shard_map/suffix_attention_1/pallas_call | solution.py:204
  29.4 1.5 %all-to-all-done.1.got_ref = s32[16,9,2,128]{3,2,1,0:T(2,128)S(1)} async-done(((s32[16,9,2,128]{3,2,1,0:T(2,128)}), s32[16,9,2,128]{3,2,1,0:T(2,128)S(1)}, u32[]{:S(2)}, u32[]{:S(2)}) %all-to-all-start.1) | async-done | bytes 147488 | tf_op jit(solution)/shard_map/all_to_all | solution.py:458
  31.0 0.9 %join_partials.1 = (f32[2,64,128]{2,1,0:T(8,128)}, f32[2,64]{1,0:T(2,128)}) custom-call(s32[16,9,2,128]{3,2,1,0:T(2,128)S(1)} %all-to-all-done.1.got_ref, f32[2,64,128]{2,1,0:T(8,128)S(1)} %get-tuple-element.12.suf_ref, f32[2,64,128]{2,1,0:T(8,128)S(1)} %get-tuple-element.13.suf_log_ref), custom_call_target="tpu_custom_call" | custom-call | tf_op jit(solution)/shard_map/join_partials/pallas_call | solution.py:438
Async XLA Ops:
  0.6 16.1 %collective-permute-start = (bf16[2048,128]{1,0:T(8,128)(2,1)}, bf16[2048,128]{1,0:T(8,128)(2,1)S(1)}, u32[]{:S(2)}, u32[]{:S(2)}) collective-permute-start(bf16[2048,128]{1,0:T(8,128)(2,1)} %bitcast.11), channel_id=1, source_target_pairs={{0,1},{1,0},{2,3},{3,2},{4,5},{5,4},{6,7},{7,6},{8,9},{9,8},{10,11... | collective-permute-start | bytes 1572872 | tf_op jit(solution)/shard_map/ppermute | solution.py:481
  1.1 15.6 %collective-permute-start.1 = (bf16[2048,128]{1,0:T(8,128)(2,1)}, bf16[2048,128]{1,0:T(8,128)(2,1)S(1)}, u32[]{:S(2)}, u32[]{:S(2)}) collective-permute-start(bf16[2048,128]{1,0:T(8,128)(2,1)} %bitcast.13), channel_id=1, source_target_pairs={{0,1},{1,0},{2,3},{3,2},{4,5},{5,4},{6,7},{7,6},{8,9},{9,8},{10,11... | collective-permute-start | bytes 1572872 | tf_op jit(solution)/shard_map/ppermute | solution.py:482
  2.7 14.0 %all-to-all-start = ((bf16[16,2,16,128]{3,2,1,0:T(8,128)(2,1)}), bf16[16,2,16,128]{3,2,1,0:T(8,128)(2,1)S(1)}, u32[]{:S(2)}, u32[]{:S(2)}) async-start(bf16[16,2,16,128]{3,2,1,0:T(8,128)(2,1)} %layout_queries.1), calls=%async_computation | async-start | bytes 262144 | tf_op jit(solution)/shard_map/all_to_all | solution.py:458
  20.5 10.4 %all-to-all-start.1 = ((s32[16,9,2,128]{3,2,1,0:T(2,128)}), s32[16,9,2,128]{3,2,1,0:T(2,128)S(1)}, u32[]{:S(2)}, u32[]{:S(2)}) async-start(s32[16,9,2,128]{3,2,1,0:T(2,128)} %prefix_attention.1), calls=%async_computation.1 | async-start | bytes 294912 | tf_op jit(solution)/shard_map/all_to_all | solution.py:458

commit v13 on v11

--- a/solution.py
+++ b/solution.py
@@ -11,7 +11,7 @@
 ROW_TILE = 128
 STEP_ROWS = 512
 SUF_COPIES = 4
-AT_ONCE = 2
+AT_ONCE = 4
 LANES = 128
 PIECE = 256
 TILE_ROWS = 2
@@ -111,7 +111,7 @@
         )
     ]
     small, carries = small[:3], small[3:]
-    for copy in small + k_copies[:AT_ONCE] + carries:
+    for copy in small + k_copies[:AT_ONCE] + v_copies[:1] + carries:
         copy.start()
     for copy in small:
         copy.wait()
@@ -143,7 +143,8 @@
         def _(c=c):
             if c >= AT_ONCE:
                 k_copies[c].wait()
-            v_copies[c].start()
+            if c > 0:
+                v_copies[c].start()
             peak = peak_ref[...]
             for at in range(c * copy_rows, (c + 1) * copy_rows, 2 * PIECE):
                 part = lax.dot_general(

time: 32.1 us -> 32.1 us (level)
  transfers between devices with their start and end apart: 4 -> 4, of which waited for: 2 -> 2; matrix products, arithmetic and copies ran while one was open for 0% -> 0% of each run, Pallas kernels for 25% -> 26%
where the time goes in v13:
time: 32.1 us; the launch traced here: 31.7 us
  starting transfers between devices  15.4 us (48%)
  Pallas kernels  12.8 us (40%)
  waiting for transfers between devices  2.84 us (9%)
  between operations  0.66 us (2%)
    all_to_all x2, starting transfers between devices, exchange(): lax.all_to_all(pieces, ('seq', 'head', 'rep'), split_axis=0, concat_axis=...  14.8 us
    pallas_call x2, Pallas kernels, suffix_partials(): pl.pallas_call(functools.partial(suffix_kernel, place=place, carried=len(...  6.75 us
    pallas_call x1, Pallas kernels, prefix_partials(): pl.pallas_call(functools.partial(prefix_kernel, per_dest=per_dest, turn=t...  3.71 us
    all_to_all x2, waiting for transfers between devices, exchange(): lax.all_to_all(pieces, ('seq', 'head', 'rep'), split_axis=0, concat_axis=...  2.84 us
    pallas_call x1, Pallas kernels, layout_queries(): pl.pallas_call(layout_kernel, in_specs=[IN_HBM], out_specs=IN_HBM, out_sh...  1.47 us
    pallas_call x1, Pallas kernels, join_partials(): pl.pallas_call(functools.partial(join_kernel, kv_count=kv_count), in_spec...  0.87 us
  transfers between devices with their start and end apart: 4, of which 2 were waited for; matrix products, arithmetic and copies ran while one was open for 0% of the time, Pallas kernels for 26%

profile of v13, /device:TPU:0, one launch (start us, length us, event | category | flops | bytes accessed | tf_op | source)
XLA Modules:
  0.0 31.7 jit_solution(7099410345184178497)
XLA Ops:
  0.6 0.5 %collective-permute-start = (bf16[2048,128]{1,0:T(8,128)(2,1)}, bf16[2048,128]{1,0:T(8,128)(2,1)S(1)}, u32[]{:S(2)}, u32[]{:S(2)}) collective-permute-start(bf16[2048,128]{1,0:T(8,128)(2,1)} %bitcast.11), channel_id=1, source_target_pairs={{0,1},{1,0},{2,3},{3,2},{4,5},{5,4},{6,7},{7,6},{8,9},{9,8},{10,11... | collective-permute-start | bytes 1572872 | tf_op jit(solution)/shard_map/ppermute | solution.py:472
  1.1 0.1 collective-permute-start.1
  1.2 1.5 %layout_queries.1 = bf16[16,2,16,128]{3,2,1,0:T(8,128)(2,1)} custom-call(bf16[2,4,16,128]{3,2,1,0:T(8,128)(2,1)} %bitcast.15), custom_call_target="tpu_custom_call" | custom-call | tf_op jit(solution)/shard_map/layout_queries/pallas_call | solution.py:59
  2.7 8.8 %all-to-all-start = ((bf16[16,2,16,128]{3,2,1,0:T(8,128)(2,1)}), bf16[16,2,16,128]{3,2,1,0:T(8,128)(2,1)S(1)}, u32[]{:S(2)}, u32[]{:S(2)}) async-start(bf16[16,2,16,128]{3,2,1,0:T(8,128)(2,1)} %layout_queries.1), calls=%async_computation | async-start | bytes 262144 | tf_op jit(solution)/shard_map/all_to_all | solution.py:449
  11.5 3.6 %suffix_attention_0.1 = (f32[64,128]{1,0:T(8,128)S(1)}, f32[64,128]{1,0:T(8,128)S(1)}, bf16[2048,128]{1,0:T(8,128)(2,1)S(1)}, bf16[2048,128]{1,0:T(8,128)(2,1)S(1)}) custom-call(s32[2]{0:T(128)} %refs_0_.3, s32[2]{0:T(128)} %refs_1_.3, bf16[2,64,128]{2,1,0:T(8,128)(2,1)} %refs_2_.3, bf16[2,8192,128]{2,1,0:T(8,128)(2,1)} %bitcast.7, ...), custom_call_target="tpu_custom_call" | custom-call | flops 268435456 | bytes 4194304 | tf_op jit(solution)/shard_map/suffix_attention_0/pallas_call | solution.py:205
  15.1 1.6 %all-to-all-done = bf16[16,2,16,128]{3,2,1,0:T(8,128)(2,1)S(1)} async-done(((bf16[16,2,16,128]{3,2,1,0:T(8,128)(2,1)}), bf16[16,2,16,128]{3,2,1,0:T(8,128)(2,1)S(1)}, u32[]{:S(2)}, u32[]{:S(2)}) %all-to-all-start) | async-done | bytes 131104 | tf_op jit(solution)/shard_map/all_to_all | solution.py:449
  16.7 0.0 collective-permute-done.k1_ref
  16.7 0.0 collective-permute-done.1.v1_ref
  16.7 3.7 %prefix_attention.1 = s32[16,9,2,128]{3,2,1,0:T(2,128)} custom-call(bf16[512,128]{1,0:T(8,128)(2,1)S(1)} %bitcast.6, bf16[2048,128]{1,0:T(8,128)(2,1)S(1)} %get-tuple-element.8.k0_ref, bf16[2048,128]{1,0:T(8,128)(2,1)S(1)} %get-tuple-element.9.v0_ref, bf16[2048,128]{1,0:T(8,128)(2,1)S(1)} %collective-permute-done.k1_ref, ...), custom_call_target="tpu_custom_call" | custom-call | flops 1073741824 | bytes 2490368 | tf_op jit(solution)/shard_map/prefix_attention/pallas_call | solution.py:352
  20.4 6.0 %all-to-all-start.1 = ((s32[16,9,2,128]{3,2,1,0:T(2,128)}), s32[16,9,2,128]{3,2,1,0:T(2,128)S(1)}, u32[]{:S(2)}, u32[]{:S(2)}) async-start(s32[16,9,2,128]{3,2,1,0:T(2,128)} %prefix_attention.1), calls=%async_computation.1 | async-start | bytes 294912 | tf_op jit(solution)/shard_map/all_to_all | solution.py:449
  26.4 3.2 %suffix_attention_1.1 = (f32[2,64,128]{2,1,0:T(8,128)S(1)}, f32[2,64,128]{2,1,0:T(8,128)S(1)}) custom-call(s32[2]{0:T(128)} %refs_0_.3, s32[2]{0:T(128)} %refs_1_.3, bf16[2,64,128]{2,1,0:T(8,128)(2,1)} %refs_2_.3, bf16[2,8192,128]{2,1,0:T(8,128)(2,1)} %bitcast.8, bf16[2,8192,128]{2,1,0:T(8,128)(2,1)} %bitcast.10, f32[64,128]{1,0:T(8,128)S(1)} %get-tuple-element.10._.refs_5_, ...), custom_call_target="tpu_custom_call" | custom-call | flops 268435456 | bytes 4194304 | tf_op jit(solution)/shard_map/suffix_attention_1/pallas_call | solution.py:205
  29.6 1.2 %all-to-all-done.1.got_ref = s32[16,9,2,128]{3,2,1,0:T(2,128)S(1)} async-done(((s32[16,9,2,128]{3,2,1,0:T(2,128)}), s32[16,9,2,128]{3,2,1,0:T(2,128)S(1)}, u32[]{:S(2)}, u32[]{:S(2)}) %all-to-all-start.1) | async-done | bytes 147488 | tf_op jit(solution)/shard_map/all_to_all | solution.py:449
  30.8 0.9 %join_partials.1 = (f32[2,64,128]{2,1,0:T(8,128)}, f32[2,64]{1,0:T(2,128)}) custom-call(s32[16,9,2,128]{3,2,1,0:T(2,128)S(1)} %all-to-all-done.1.got_ref, f32[2,64,128]{2,1,0:T(8,128)S(1)} %get-tuple-element.12.suf_ref, f32[2,64,128]{2,1,0:T(8,128)S(1)} %get-tuple-element.13.suf_log_ref), custom_call_target="tpu_custom_call" | custom-call | tf_op jit(solution)/shard_map/join_partials/pallas_call | solution.py:429
Async XLA Ops:
  0.6 16.1 %collective-permute-start = (bf16[2048,128]{1,0:T(8,128)(2,1)}, bf16[2048,128]{1,0:T(8,128)(2,1)S(1)}, u32[]{:S(2)}, u32[]{:S(2)}) collective-permute-start(bf16[2048,128]{1,0:T(8,128)(2,1)} %bitcast.11), channel_id=1, source_target_pairs={{0,1},{1,0},{2,3},{3,2},{4,5},{5,4},{6,7},{7,6},{8,9},{9,8},{10,11... | collective-permute-start | bytes 1572872 | tf_op jit(solution)/shard_map/ppermute | solution.py:472
  1.1 15.6 %collective-permute-start.1 = (bf16[2048,128]{1,0:T(8,128)(2,1)}, bf16[2048,128]{1,0:T(8,128)(2,1)S(1)}, u32[]{:S(2)}, u32[]{:S(2)}) collective-permute-start(bf16[2048,128]{1,0:T(8,128)(2,1)} %bitcast.13), channel_id=1, source_target_pairs={{0,1},{1,0},{2,3},{3,2},{4,5},{5,4},{6,7},{7,6},{8,9},{9,8},{10,11... | collective-permute-start | bytes 1572872 | tf_op jit(solution)/shard_map/ppermute | solution.py:473
  2.7 14.0 %all-to-all-start = ((bf16[16,2,16,128]{3,2,1,0:T(8,128)(2,1)}), bf16[16,2,16,128]{3,2,1,0:T(8,128)(2,1)S(1)}, u32[]{:S(2)}, u32[]{:S(2)}) async-start(bf16[16,2,16,128]{3,2,1,0:T(8,128)(2,1)} %layout_queries.1), calls=%async_computation | async-start | bytes 262144 | tf_op jit(solution)/shard_map/all_to_all | solution.py:449
  20.4 10.4 %all-to-all-start.1 = ((s32[16,9,2,128]{3,2,1,0:T(2,128)}), s32[16,9,2,128]{3,2,1,0:T(2,128)S(1)}, u32[]{:S(2)}, u32[]{:S(2)}) async-start(s32[16,9,2,128]{3,2,1,0:T(2,128)} %prefix_attention.1), calls=%async_computation.1 | async-start | bytes 294912 | tf_op jit(solution)/shard_map/all_to_all | solution.py:449
